TPU v7x, 32 devices: a whole 2x2x4 slice. The times are simulated.
32 devices in a mesh: gy: 4 (over y, x), gx: 8 (over z, core).
Axes of the slice: x: 2, y: 2, z: 4, core: 2. Of those that a mesh axis runs over, the one named last changes fastest.
Arguments:
- estimate: float32 [128, 128, 128], P('gy', 'gx'), may hold values from 0.5 to 2
- recorded: float32 [4, 128, 128, 128], P(None, 'gy', 'gx'), may hold values from 0.2 to 5
- quarter_turns: int32 [4], replicated, may hold values from 0 to 3, each once
- offsets: int32 [4], replicated, may hold values from 0 to 127
- depth_taps: float32 [4, 41], replicated, may hold values from 0.002 to 0.1
- row_taps: float32 [4, 9], replicated, may hold values from 0.01 to 0.5
- column_taps: float32 [4, 9], replicated, may hold values from 0.01 to 0.5
Outputs:
- deconvolved: float32 [128, 128, 128], P('gy', 'gx')
Inputs may be any that keep to these rules, and one draw needn't show every extreme that they name: `quarter_turns`: every view has a different number of quarter turns.
All inputs are finite; a program needn't handle non-finite values.
Results may differ from a plain program's by a relative error of at most 0.0001.
Values sent between devices are 32-bit elements; how exact they have to be, the bound alone decides.
No kernel may reach another device: no remote copies, remote signals or barrier semaphores. Data moves between devices by JAX's collectives and lax.ppermute only.
A program may use at most 128 MiB of HBM per device.

v0:
```python
import functools

import jax
import jax.numpy as jnp
from jax import lax
from jax.experimental import pallas as pl
from jax.experimental.pallas import tpu as pltpu
from jax.sharding import PartitionSpec as P

VIEWS = 4
LANES = 128
VMEM = pl.BlockSpec(memory_space=pltpu.VMEM)
SMEM = pl.BlockSpec(memory_space=pltpu.SMEM)
PARAMS = pltpu.CompilerParams(vmem_limit_bytes=24 * 1024 * 1024)
F32 = jnp.float32
BF16 = jnp.bfloat16


def struct(*shape, dtype=F32):
    return jax.ShapeDtypeStruct(shape, dtype)


def view_of(turns_ref, turn):
    found = jnp.int32(0)
    for view in range(1, VIEWS):
        found = jnp.where(turns_ref[view] == turn, jnp.int32(view), found)
    return found


def split(value):
    high = value.astype(BF16)
    return high, (value - high.astype(F32)).astype(BF16)


def dot(left, right):
    return jnp.dot(left, right, preferred_element_type=F32)


def along(axis, width):
    return [(i, i + 1) for i in range(width - 1)], [(i + 1, i) for i in range(width - 1)]


def prepare(turns, offsets, recorded, kept, mirrored, sent):
    depth, rows, lanes = recorded.shape[1:]
    parts = sent.shape[0]
    kept[...] = recorded[view_of(turns, 0)]
    mirrored[...] = recorded[view_of(turns, 2)]
    for slot, turn in enumerate((1, 3)):
        view = view_of(turns, turn)
        volume = recorded[view].reshape(depth * rows, lanes)
        volume = pltpu.roll(volume, lax.rem(lanes - offsets[view], lanes), 1)
        across = volume.T
        for part in range(parts):
            to = parts - 1 - part if turn == 1 else part
            sent[to, slot] = across[part * rows : (part + 1) * rows]


def edges(own, before, after, left, right):
    depth, rows, _ = own.shape
    reach = before.shape[0]
    side = left.shape[0]
    for target, initial in ((left, 0), (right, rows - side)):
        for i in range(side):
            target[i, 0:depth] = own[:, initial + i]
            target[i, depth : depth + reach] = before[:, initial + i]
            target[i, depth + reach : depth + 2 * reach] = after[:, initial + i]


def row_taps_of(turn, view, row_taps, column_taps, width):
    source = column_taps if turn % 2 else row_taps
    flipped = turn in (1, 2)
    return [source[view, width - 1 - s if flipped else s] for s in range(width)]


def predict(turns, offsets, depth_taps, row_taps, column_taps, own, before, after, left, right,
            predicted, lane_back, depth_back, extended, blurred):
    depth, rows, lanes = own.shape
    reach = before.shape[0]
    side = left.shape[0]
    width = 2 * side + 1
    deep = depth + 2 * reach
    padded = extended.shape[1]
    views = [view_of(turns, turn) for turn in range(VIEWS)]

    column = lax.broadcasted_iota(jnp.int32, (depth, LANES), 1)
    row = lax.broadcasted_iota(jnp.int32, (depth, LANES), 0)
    layer = jnp.where(column < depth, column, jnp.where(column < depth + reach, column - depth - reach, column - reach))
    tap = jnp.where(column < deep, layer - row + reach, -1)
    stacked = []
    for view in views:
        matrix = jnp.zeros((depth, LANES), F32)
        for t in range(2 * reach + 1):
            matrix = jnp.where(tap == t, depth_taps[view, t], matrix)
        stacked.append(matrix)
    matrix = jnp.concatenate(stacked, axis=0)
    back_high, back_low = split(matrix.T[:padded])
    depth_back[0] = back_high
    depth_back[1] = back_low
    high, low = split(matrix)
    zero = jnp.zeros((VIEWS * depth, LANES - padded), BF16)
    del zero
    depth_high, depth_low = high[:, :padded], low[:, :padded]

    for i in range(side):
        extended[i, 0:deep] = left[i]
        extended[side + rows + i, 0:deep] = right[i]
    for i in range(rows):
        extended[side + i, 0:depth] = own[:, i]
        extended[side + i, depth : depth + reach] = before[:, i]
        extended[side + i, depth + reach : deep] = after[:, i]
    if padded > deep:
        for i in range(rows + 2 * side):
            extended[i, deep:padded] = jnp.zeros((padded - deep, lanes), F32)

    for i in range(rows + 2 * side):
        e_high, e_low = split(extended[i])
        blurred[i] = dot(depth_high, e_high) + dot(depth_high, e_low) + dot(depth_low, e_high)

    inward = lax.broadcasted_iota(jnp.int32, (lanes, lanes), 0)
    outward = lax.broadcasted_iota(jnp.int32, (lanes, lanes), 1)
    for turn, view in enumerate(views):
        place = outward
        if turn % 2 == 0:
            place = outward - offsets[view]
            place = jnp.where(place < 0, place + lanes, place)
        tap = (lanes - 1 - place - inward if turn >= 2 else inward - place) + side
        source = row_taps if turn % 2 else column_taps
        matrix = jnp.zeros((lanes, lanes), F32)
        for r in range(width):
            matrix = jnp.where(tap == r, source[view, r], matrix)
        high, low = split(matrix)
        back_high, back_low = split(matrix.T)
        lane_back[turn, 0] = back_high
        lane_back[turn, 1] = back_low
        both = jnp.concatenate([high, high], axis=0)
        factor = row_taps_of(turn, view, row_taps, column_taps, width)
        for i in range(rows):
            layers = pl.ds(turn * depth, depth)
            total = factor[0] * blurred[i, layers]
            for s in range(1, width):
                total = total + factor[s] * blurred[i + s, layers]
            t_high, t_low = split(total)
            predicted[turn, i] = dot(jnp.concatenate([t_high, t_low], axis=1), both) + dot(t_high, low)


def project(turns, row_taps, column_taps, predicted, lane_back, depth_back, kept, mirrored, arrived,
            middle, left, right, data, backed, spread):
    _, rows, depth, lanes = predicted.shape
    side = left.shape[0]
    deep = left.shape[1]
    width = 2 * side + 1
    views = [view_of(turns, turn) for turn in range(VIEWS)]
    parts = arrived.shape[0]
    group = LANES // rows
    granule = lax.broadcasted_iota(jnp.int32, (8, LANES), 1) // rows

    for slot in range(2):
        for part in range(0, parts, group):
            for eight in range(0, rows, 8):
                for chunk in range(depth * rows // LANES):
                    held = [
                        arrived[part + s, slot, eight : eight + 8, chunk * LANES : (chunk + 1) * LANES]
                        for s in range(group)
                    ]
                    step = 1
                    while step < group:
                        upper = (granule // step) % 2 == 1
                        swapped = list(held)
                        for s in range(group):
                            if s & step == 0:
                                one, two = held[s], held[s + step]
                                swapped[s] = jnp.where(upper, pltpu.roll(two, step * rows, 1), one)
                                swapped[s + step] = jnp.where(upper, two, pltpu.roll(one, LANES - step * rows, 1))
                        held = swapped
                        step *= 2
                    for s in range(group):
                        data[slot, eight : eight + 8, chunk * group + s, part * rows : part * rows + LANES] = held[s]

    for turn, view in enumerate(views):
        high, low = lane_back[turn, 0], lane_back[turn, 1]
        both = jnp.concatenate([high, high], axis=0)
        for i in range(rows):
            there = rows - 1 - i if turn in (1, 2) else i
            if turn == 0:
                recorded = kept[:, there]
            elif turn == 2:
                recorded = mirrored[:, there]
            else:
                recorded = data[turn // 2, there]
            r_high, r_low = split(recorded / predicted[turn, i])
            backed[turn, i] = dot(jnp.concatenate([r_high, r_low], axis=1), both) + dot(r_high, low)
        factor = row_taps_of(turn, view, row_taps, column_taps, width)
        for e in range(rows + 2 * side):
            total = None
            for i in range(max(0, e - 2 * side), min(rows, e + 1)):
                term = factor[e - i] * backed[turn, i]
                total = term if total is None else total + term
            spread[e, turn * depth : (turn + 1) * depth] = total

    high, low = depth_back[0], depth_back[1]
    both = jnp.concatenate([high, low], axis=1)
    for e in range(rows + 2 * side):
        s_high, s_low = split(spread[e])
        result = dot(both, jnp.concatenate([s_high, s_high], axis=0)) + dot(high, s_low)
        result = result[:deep]
        if e < side:
            left[e] = result
        elif e < side + rows:
            middle[e - side] = result
        else:
            right[e - side - rows] = result


def gather_sides(middle, left, right, own, up, down):
    rows = middle.shape[0]
    side = left.shape[0]
    depth = own.shape[1]
    reach = up.shape[0] // rows
    for i in range(rows):
        value = middle[i]
        if i < side:
            value = value + left[i]
        if i >= rows - side:
            value = value + right[i - rows + side]
        own[i] = value[:depth]
        up[i * reach : (i + 1) * reach] = value[depth : depth + reach]
        down[i * reach : (i + 1) * reach] = value[depth + reach : depth + 2 * reach]


def finish(estimate, own, up, down, out):
    rows, depth, _ = own.shape
    reach = up.shape[0] // rows
    for i in range(rows):
        value = own[i]
        lane = value.shape[1]
        first = up[i * reach : (i + 1) * reach]
        last = down[i * reach : (i + 1) * reach]
        rest = jnp.zeros((depth - reach, lane), F32)
        value = value + jnp.concatenate([first, rest], axis=0) + jnp.concatenate([rest, last], axis=0)
        out[:, i] = estimate[:, i] * value * (1.0 / VIEWS)


def call(body, out_shape, specs, scratch=(), cost=None):
    return pl.pallas_call(
        body,
        out_shape=out_shape,
        in_specs=specs,
        out_specs=jax.tree.map(lambda _: VMEM, out_shape),
        scratch_shapes=scratch,
        compiler_params=PARAMS,
        cost_estimate=cost,
    )


def shards(estimate, recorded, quarter_turns, offsets, depth_taps, row_taps, column_taps):
    depth, rows, lanes = estimate.shape
    reach = (depth_taps.shape[1] - 1) // 2
    side = (row_taps.shape[1] - 1) // 2
    deep = depth + 2 * reach
    padded = -(-deep // 16) * 16
    parts = lax.axis_size("gx")
    forth_y, back_y = along("gy", lax.axis_size("gy"))
    forth_x, back_x = along("gx", parts)

    before = lax.ppermute(estimate[depth - reach :], "gy", forth_y)
    after = lax.ppermute(estimate[:reach], "gy", back_y)
    kept, mirrored, sent = call(
        prepare,
        (struct(depth, rows, lanes), struct(depth, rows, lanes), struct(parts, 2, rows, depth * rows)),
        [SMEM, SMEM, VMEM],
    )(quarter_turns, offsets, recorded)
    mirrored = lax.ppermute(mirrored, "gx", [(i, parts - 1 - i) for i in range(parts)])
    arrived = lax.all_to_all(sent, "gx", 0, 0)

    left, right = call(
        edges, (struct(side, deep, lanes), struct(side, deep, lanes)), [VMEM] * 3
    )(estimate, before, after)
    left, right = lax.ppermute(right, "gx", forth_x), lax.ppermute(left, "gx", back_x)

    predicted, lane_back, depth_back = call(
        predict,
        (
            struct(VIEWS, rows, depth, lanes),
            struct(VIEWS, 2, lanes, lanes, dtype=BF16),
            struct(2, padded, VIEWS * depth, dtype=BF16),
        ),
        [SMEM] * 5 + [VMEM] * 5,
        [
            pltpu.VMEM((rows + 2 * side, padded, lanes), F32),
            pltpu.VMEM((rows + 2 * side, VIEWS * depth, lanes), F32),
        ],
        pl.CostEstimate(flops=4_000_000_000, bytes_accessed=4_000_000, transcendentals=0),
    )(quarter_turns, offsets, depth_taps, row_taps, column_taps, estimate, before, after, left, right)

    middle, left, right = call(
        project,
        (struct(rows, deep, lanes), struct(side, deep, lanes), struct(side, deep, lanes)),
        [SMEM] * 3 + [VMEM] * 6,
        [
            pltpu.VMEM((2, rows, depth, lanes), F32),
            pltpu.VMEM((VIEWS, rows, depth, lanes), F32),
            pltpu.VMEM((rows + 2 * side, VIEWS * depth, lanes), F32),
        ],
        pl.CostEstimate(flops=4_000_000_000, bytes_accessed=4_000_000, transcendentals=0),
    )(quarter_turns, row_taps, column_taps, predicted, lane_back, depth_back, kept, mirrored, arrived)

    left, right = lax.ppermute(right, "gx", forth_x), lax.ppermute(left, "gx", back_x)
    own, up, down = call(
        gather_sides,
        (struct(rows, depth, lanes), struct(rows * reach, lanes), struct(rows * reach, lanes)),
        [VMEM] * 3,
    )(middle, left, right)
    first = lax.ppermute(down, "gy", forth_y)
    last = lax.ppermute(up, "gy", back_y)
    return call(finish, struct(depth, rows, lanes), [VMEM] * 4)(estimate, own, first, last)


def solution(mesh):
    in_specs = (P("gy", "gx", None), P(None, "gy", "gx", None), P(), P(), P(), P(), P())
    out_specs = P("gy", "gx", None)
    return jax.shard_map(shards, mesh=mesh, in_specs=in_specs, out_specs=out_specs, check_vma=False)
```

profile of v0, /device:TPU:16, one launch (start us, length us, event | category | flops | bytes accessed | tf_op | source)
XLA Modules:
  0.0 66.8 jit_solution(18328726380343740317)
XLA Ops:
  0.0 0.0 copy-start.1
  0.0 1.2 %copy-done.1 = f32[4,32,16,128]{3,2,1,0:T(8,128)S(1)} copy-done((f32[4,32,16,128]{3,2,1,0:T(8,128)S(1)}, f32[4,32,16,128]{3,2,1,0:T(8,128)}, u32[]{:S(2)}) %copy-start.1) | copy-done | bytes 1048600
  1.2 0.0 copy-start.2
  1.2 0.7 copy-done.2
  1.9 0.0 copy-start.4
  1.9 0.7 copy-done.4
  2.5 1.7 %shard_map.75 = (f32[32,16,128]{2,1,0:T(8,128)S(1)}, f32[32,16,128]{2,1,0:T(8,128)S(1)}, f32[8,2,16,512]{3,2,1,0:T(8,128)}) custom-call(s32[4]{0:T(128)S(1)} %copy-done.4, s32[4]{0:T(128)S(1)} %copy-done.2, f32[4,32,16,128]{3,2,1,0:T(8,128)S(1)} %copy-done.1), custom_call_target="tpu_custom_call" | custom-call | tf_op jit(solution)/shard_map/pallas_call | solution.py:267
  4.3 0.0 copy-start
  4.3 5.3 %all-to-all-start = ((f32[8,2,16,512]{3,2,1,0:T(8,128)}), f32[8,2,16,512]{3,2,1,0:T(8,128)S(1)}, u32[]{:S(2)}, u32[]{:S(2)}) async-start(f32[8,2,16,512]{3,2,1,0:T(8,128)} %get-tuple-element.26), calls=%async_computation | async-start | bytes 1048576 | tf_op jit(solution)/shard_map/all_to_all | solution.py:273
  9.6 0.0 copy-done
  9.6 1.3 %collective-permute-start.1 = (f32[20,16,128]{2,1,0:T(8,128)S(1)}, f32[20,16,128]{2,1,0:T(8,128)S(1)}, u32[]{:S(2)}, u32[]{:S(2)}) collective-permute-start(f32[20,16,128]{2,1,0:T(8,128)S(1)} %get-tuple-element.33), channel_id=1, source_target_pairs={{8,0},{16,8},{24,16},{9,1},{17,9},{25,17},{10,2},{18,10},{26,18},{... | collective-permute-start | bytes 491528 | tf_op jit(solution)/shard_map/ppermute | solution.py:266
  10.9 4.6 %collective-permute-start = (f32[20,16,128]{2,1,0:T(8,128)S(1)}, f32[20,16,128]{2,1,0:T(8,128)S(1)}, u32[]{:S(2)}, u32[]{:S(2)}) collective-permute-start(f32[20,16,128]{2,1,0:T(8,128)S(1)} %get-tuple-element.34), channel_id=1, source_target_pairs={{0,8},{8,16},{16,24},{1,9},{9,17},{17,25},{2,10},{10,18},{18,26},{... | collective-permute-start | bytes 491528 | tf_op jit(solution)/shard_map/ppermute | solution.py:265
  15.5 2.3 %collective-permute-done.1.after = f32[20,16,128]{2,1,0:T(8,128)S(1)} collective-permute-done((f32[20,16,128]{2,1,0:T(8,128)S(1)}, f32[20,16,128]{2,1,0:T(8,128)S(1)}, u32[]{:S(2)}, u32[]{:S(2)}) %collective-permute-start.1) | collective-permute-done | bytes 163872 | tf_op jit(solution)/shard_map/ppermute | solution.py:266
  17.8 1.2 %collective-permute-done.before = f32[20,16,128]{2,1,0:T(8,128)S(1)} collective-permute-done((f32[20,16,128]{2,1,0:T(8,128)S(1)}, f32[20,16,128]{2,1,0:T(8,128)S(1)}, u32[]{:S(2)}, u32[]{:S(2)}) %collective-permute-start) | collective-permute-done | bytes 163872 | tf_op jit(solution)/shard_map/ppermute | solution.py:265
  19.0 0.0 copy-start.8
  19.0 0.2 shard_map.73
  19.1 0.0 copy-start.7
  19.1 0.0 copy-start.6
  19.1 1.9 %collective-permute-start.2 = (f32[4,72,128]{2,1,0:T(8,128)S(1)}, f32[4,72,128]{2,1,0:T(8,128)S(1)}, u32[]{:S(2)}, u32[]{:S(2)}) collective-permute-start(f32[4,72,128]{2,1,0:T(8,128)S(1)} %get-tuple-element.19), channel_id=1, source_target_pairs={{0,1},{1,2},{2,3},{3,4},{4,5},{5,6},{6,7},{8,9},{9,10},{10,11},{11... | collective-permute-start | bytes 442376 | tf_op jit(solution)/shard_map/ppermute | solution.py:278
  21.1 0.0 copy-start.3
  21.1 0.0 copy-start.5
  21.1 3.6 %collective-permute-start.3 = (f32[4,72,128]{2,1,0:T(8,128)S(1)}, f32[4,72,128]{2,1,0:T(8,128)S(1)}, u32[]{:S(2)}, u32[]{:S(2)}) collective-permute-start(f32[4,72,128]{2,1,0:T(8,128)S(1)} %get-tuple-element.20), channel_id=1, source_target_pairs={{1,0},{2,1},{3,2},{4,3},{5,4},{6,5},{7,6},{9,8},{10,9},{11,10},{12... | collective-permute-start | bytes 442376 | tf_op jit(solution)/shard_map/ppermute | solution.py:278
  24.7 0.1 collective-permute-start.4
  24.8 0.8 %collective-permute-done.2.left = f32[4,72,128]{2,1,0:T(8,128)S(1)} collective-permute-done((f32[4,72,128]{2,1,0:T(8,128)S(1)}, f32[4,72,128]{2,1,0:T(8,128)S(1)}, u32[]{:S(2)}, u32[]{:S(2)}) %collective-permute-start.2) | collective-permute-done | bytes 147488 | tf_op jit(solution)/shard_map/ppermute | solution.py:278
  25.6 8.1 %collective-permute-done.3.right = f32[4,72,128]{2,1,0:T(8,128)S(1)} collective-permute-done((f32[4,72,128]{2,1,0:T(8,128)S(1)}, f32[4,72,128]{2,1,0:T(8,128)S(1)}, u32[]{:S(2)}, u32[]{:S(2)}) %collective-permute-start.3) | collective-permute-done | bytes 147488 | tf_op jit(solution)/shard_map/ppermute | solution.py:278
  33.7 0.0 copy-done.8
  33.7 0.0 copy-done.7
  33.7 0.0 copy-done.6
  33.7 0.0 copy-done.3
  33.7 0.0 copy-done.5
  33.7 2.9 %shard_map.74 = (f32[4,16,32,128]{3,2,1,0:T(8,128)S(1)}, bf16[4,2,128,128]{3,2,1,0:T(8,128)(2,1)S(1)}, bf16[2,80,128]{2,1,0:T(8,128)(2,1)S(1)}) custom-call(s32[4]{0:T(128)S(1)} %copy-done.5, s32[4]{0:T(128)S(1)} %copy-done.3, f32[4,41]{1,0:T(4,128)S(1)} %copy-done.6, f32[4,9]{1,0:T(4,128)S(1)} %copy-done.7, f32[4,9]{1,0:T(4,128)S(1)} %copy-done.8, ...), custom_call_target="tpu_custom_call" | custom-call | flops 4000000000 | bytes 4000000 | tf_op jit(solution)/shard_map/pallas_call | solution.py:280
  36.6 2.4 %collective-permute-done.4.mirrored = f32[32,16,128]{2,1,0:T(8,128)S(1)} collective-permute-done((f32[32,16,128]{2,1,0:T(8,128)S(1)}, f32[32,16,128]{2,1,0:T(8,128)S(1)}, u32[]{:S(2)}, u32[]{:S(2)}) %collective-permute-start.4) | collective-permute-done | bytes 262176 | tf_op jit(solution)/shard_map/ppermute | solution.py:272
  39.0 0.0 all-to-all-done.arrived
  39.0 2.9 %shard_map.76 = (f32[16,72,128]{2,1,0:T(8,128)S(1)}, f32[4,72,128]{2,1,0:T(8,128)S(1)}, f32[4,72,128]{2,1,0:T(8,128)S(1)}) custom-call(s32[4]{0:T(128)S(1)} %copy-done.5, f32[4,9]{1,0:T(4,128)S(1)} %copy-done.7, f32[4,9]{1,0:T(4,128)S(1)} %copy-done.8, f32[4,16,32,128]{3,2,1,0:T(8,128)S(1)} %get-tuple-element.21.predicted, ...), custom_call_target="tpu_custom_call" | custom-call | flops 4000000000 | bytes 4000000 | tf_op jit(solution)/shard_map/pallas_call | solution.py:295
  41.9 2.0 %collective-permute-start.5 = (f32[4,72,128]{2,1,0:T(8,128)S(1)}, f32[4,72,128]{2,1,0:T(8,128)S(1)}, u32[]{:S(2)}, u32[]{:S(2)}) collective-permute-start(f32[4,72,128]{2,1,0:T(8,128)S(1)} %get-tuple-element.28), channel_id=1, source_target_pairs={{0,1},{1,2},{2,3},{3,4},{4,5},{5,6},{6,7},{8,9},{9,10},{10,11},{11... | collective-permute-start | bytes 442376 | tf_op jit(solution)/shard_map/ppermute | solution.py:307
  44.0 3.5 %collective-permute-start.6 = (f32[4,72,128]{2,1,0:T(8,128)S(1)}, f32[4,72,128]{2,1,0:T(8,128)S(1)}, u32[]{:S(2)}, u32[]{:S(2)}) collective-permute-start(f32[4,72,128]{2,1,0:T(8,128)S(1)} %get-tuple-element.29), channel_id=1, source_target_pairs={{1,0},{2,1},{3,2},{4,3},{5,4},{6,5},{7,6},{9,8},{10,9},{11,10},{12... | collective-permute-start | bytes 442376 | tf_op jit(solution)/shard_map/ppermute | solution.py:307
  47.5 0.9 %collective-permute-done.5.left = f32[4,72,128]{2,1,0:T(8,128)S(1)} collective-permute-done((f32[4,72,128]{2,1,0:T(8,128)S(1)}, f32[4,72,128]{2,1,0:T(8,128)S(1)}, u32[]{:S(2)}, u32[]{:S(2)}) %collective-permute-start.5) | collective-permute-done | bytes 147488 | tf_op jit(solution)/shard_map/ppermute | solution.py:307
  48.4 1.8 %collective-permute-done.6.right = f32[4,72,128]{2,1,0:T(8,128)S(1)} collective-permute-done((f32[4,72,128]{2,1,0:T(8,128)S(1)}, f32[4,72,128]{2,1,0:T(8,128)S(1)}, u32[]{:S(2)}, u32[]{:S(2)}) %collective-permute-start.6) | collective-permute-done | bytes 147488 | tf_op jit(solution)/shard_map/ppermute | solution.py:307
  50.2 0.1 shard_map.77
  50.2 4.4 %collective-permute-start.7 = (f32[320,128]{1,0:T(8,128)S(1)}, f32[320,128]{1,0:T(8,128)S(1)}, u32[]{:S(2)}, u32[]{:S(2)}) collective-permute-start(f32[320,128]{1,0:T(8,128)S(1)} %get-tuple-element.31), channel_id=1, source_target_pairs={{0,8},{8,16},{16,24},{1,9},{9,17},{17,25},{2,10},{10,18},{18,26},{... | collective-permute-start | bytes 491528 | tf_op jit(solution)/shard_map/ppermute | solution.py:313
  54.6 1.3 %collective-permute-start.8 = (f32[320,128]{1,0:T(8,128)S(1)}, f32[320,128]{1,0:T(8,128)S(1)}, u32[]{:S(2)}, u32[]{:S(2)}) collective-permute-start(f32[320,128]{1,0:T(8,128)S(1)} %get-tuple-element.32), channel_id=1, source_target_pairs={{8,0},{16,8},{24,16},{9,1},{17,9},{25,17},{10,2},{18,10},{26,18},{... | collective-permute-start | bytes 491528 | tf_op jit(solution)/shard_map/ppermute | solution.py:314
  55.9 2.6 %collective-permute-done.7.up = f32[320,128]{1,0:T(8,128)S(1)} collective-permute-done((f32[320,128]{1,0:T(8,128)S(1)}, f32[320,128]{1,0:T(8,128)S(1)}, u32[]{:S(2)}, u32[]{:S(2)}) %collective-permute-start.7) | collective-permute-done | bytes 163872 | tf_op jit(solution)/shard_map/ppermute | solution.py:313
  58.5 7.3 %collective-permute-done.8.down = f32[320,128]{1,0:T(8,128)S(1)} collective-permute-done((f32[320,128]{1,0:T(8,128)S(1)}, f32[320,128]{1,0:T(8,128)S(1)}, u32[]{:S(2)}, u32[]{:S(2)}) %collective-permute-start.8) | collective-permute-done | bytes 163872 | tf_op jit(solution)/shard_map/ppermute | solution.py:314
  65.8 1.0 %shard_map.78 = f32[32,16,128]{2,1,0:T(8,128)} custom-call(f32[32,16,128]{2,1,0:T(8,128)S(1)} %copy-done, f32[16,32,128]{2,1,0:T(8,128)S(1)} %get-tuple-element.30.own, f32[320,128]{1,0:T(8,128)S(1)} %collective-permute-done.7.up, f32[320,128]{1,0:T(8,128)S(1)} %collective-permute-done.8.down), custom_call_target="tpu_custom_call" | custom-call | tf_op jit(solution)/shard_map/pallas_call | solution.py:315
  (1 shorter events, 0.0 us)
Async XLA Ops:
  0.0 1.2 %copy-start.1 = (f32[4,32,16,128]{3,2,1,0:T(8,128)S(1)}, f32[4,32,16,128]{3,2,1,0:T(8,128)}, u32[]{:S(2)}) copy-start(f32[4,32,16,128]{3,2,1,0:T(8,128)} %recorded.1) | copy-start | bytes 3145732
  1.2 0.7 copy-start.2
  1.9 0.7 copy-start.4
  4.3 5.3 %copy-start = (f32[32,16,128]{2,1,0:T(8,128)S(1)}, f32[32,16,128]{2,1,0:T(8,128)}, u32[]{:S(2)}) copy-start(f32[32,16,128]{2,1,0:T(8,128)} %estimate.1) | copy-start | bytes 786436
  4.3 34.8 %all-to-all-start = ((f32[8,2,16,512]{3,2,1,0:T(8,128)}), f32[8,2,16,512]{3,2,1,0:T(8,128)S(1)}, u32[]{:S(2)}, u32[]{:S(2)}) async-start(f32[8,2,16,512]{3,2,1,0:T(8,128)} %get-tuple-element.26), calls=%async_computation | async-start | bytes 1048576 | tf_op jit(solution)/shard_map/all_to_all | solution.py:273
  9.6 8.1 %collective-permute-start.1 = (f32[20,16,128]{2,1,0:T(8,128)S(1)}, f32[20,16,128]{2,1,0:T(8,128)S(1)}, u32[]{:S(2)}, u32[]{:S(2)}) collective-permute-start(f32[20,16,128]{2,1,0:T(8,128)S(1)} %get-tuple-element.33), channel_id=1, source_target_pairs={{8,0},{16,8},{24,16},{9,1},{17,9},{25,17},{10,2},{18,10},{26,18},{... | collective-permute-start | bytes 491528 | tf_op jit(solution)/shard_map/ppermute | solution.py:266
  10.9 8.0 %collective-permute-start = (f32[20,16,128]{2,1,0:T(8,128)S(1)}, f32[20,16,128]{2,1,0:T(8,128)S(1)}, u32[]{:S(2)}, u32[]{:S(2)}) collective-permute-start(f32[20,16,128]{2,1,0:T(8,128)S(1)} %get-tuple-element.34), channel_id=1, source_target_pairs={{0,8},{8,16},{16,24},{1,9},{9,17},{17,25},{2,10},{10,18},{18,26},{... | collective-permute-start | bytes 491528 | tf_op jit(solution)/shard_map/ppermute | solution.py:265
  19.0 14.7 %copy-start.8 = (f32[4,9]{1,0:T(4,128)S(1)}, f32[4,9]{1,0:T(4,128)}, u32[]{:S(2)}) copy-start(f32[4,9]{1,0:T(4,128)} %column_taps.3) | copy-start | bytes 436
  19.1 14.5 %copy-start.7 = (f32[4,9]{1,0:T(4,128)S(1)}, f32[4,9]{1,0:T(4,128)}, u32[]{:S(2)}) copy-start(f32[4,9]{1,0:T(4,128)} %row_taps.3) | copy-start | bytes 436
  19.1 14.5 %copy-start.6 = (f32[4,41]{1,0:T(4,128)S(1)}, f32[4,41]{1,0:T(4,128)}, u32[]{:S(2)}) copy-start(f32[4,41]{1,0:T(4,128)} %depth_taps.1) | copy-start | bytes 1972
  19.1 6.5 %collective-permute-start.2 = (f32[4,72,128]{2,1,0:T(8,128)S(1)}, f32[4,72,128]{2,1,0:T(8,128)S(1)}, u32[]{:S(2)}, u32[]{:S(2)}) collective-permute-start(f32[4,72,128]{2,1,0:T(8,128)S(1)} %get-tuple-element.19), channel_id=1, source_target_pairs={{0,1},{1,2},{2,3},{3,4},{4,5},{5,6},{6,7},{8,9},{9,10},{10,11},{11... | collective-permute-start | bytes 442376 | tf_op jit(solution)/shard_map/ppermute | solution.py:278
  21.1 12.6 %copy-start.3 = (s32[4]{0:T(128)S(1)}, s32[4]{0:T(128)}, u32[]{:S(2)}) copy-start(s32[4]{0:T(128)} %offsets.3) | copy-start | bytes 52
  21.1 12.6 %copy-start.5 = (s32[4]{0:T(128)S(1)}, s32[4]{0:T(128)}, u32[]{:S(2)}) copy-start(s32[4]{0:T(128)} %turns.5) | copy-start | bytes 52
  21.1 12.6 %collective-permute-start.3 = (f32[4,72,128]{2,1,0:T(8,128)S(1)}, f32[4,72,128]{2,1,0:T(8,128)S(1)}, u32[]{:S(2)}, u32[]{:S(2)}) collective-permute-start(f32[4,72,128]{2,1,0:T(8,128)S(1)} %get-tuple-element.20), channel_id=1, source_target_pairs={{1,0},{2,1},{3,2},{4,3},{5,4},{6,5},{7,6},{9,8},{10,9},{11,10},{12... | collective-permute-start | bytes 442376 | tf_op jit(solution)/shard_map/ppermute | solution.py:278
  24.7 14.3 %collective-permute-start.4 = (f32[32,16,128]{2,1,0:T(8,128)S(1)}, f32[32,16,128]{2,1,0:T(8,128)S(1)}, u32[]{:S(2)}, u32[]{:S(2)}) collective-permute-start(f32[32,16,128]{2,1,0:T(8,128)S(1)} %get-tuple-element.25), channel_id=1, source_target_pairs={{0,7},{1,6},{2,5},{3,4},{4,3},{5,2},{6,1},{7,0},{8,15},{9,14},{10,... | collective-permute-start | bytes 786440 | tf_op jit(solution)/shard_map/ppermute | solution.py:272
  41.9 6.5 %collective-permute-start.5 = (f32[4,72,128]{2,1,0:T(8,128)S(1)}, f32[4,72,128]{2,1,0:T(8,128)S(1)}, u32[]{:S(2)}, u32[]{:S(2)}) collective-permute-start(f32[4,72,128]{2,1,0:T(8,128)S(1)} %get-tuple-element.28), channel_id=1, source_target_pairs={{0,1},{1,2},{2,3},{3,4},{4,5},{5,6},{6,7},{8,9},{9,10},{10,11},{11... | collective-permute-start | bytes 442376 | tf_op jit(solution)/shard_map/ppermute | solution.py:307
  44.0 6.2 %collective-permute-start.6 = (f32[4,72,128]{2,1,0:T(8,128)S(1)}, f32[4,72,128]{2,1,0:T(8,128)S(1)}, u32[]{:S(2)}, u32[]{:S(2)}) collective-permute-start(f32[4,72,128]{2,1,0:T(8,128)S(1)} %get-tuple-element.29), channel_id=1, source_target_pairs={{1,0},{2,1},{3,2},{4,3},{5,4},{6,5},{7,6},{9,8},{10,9},{11,10},{12... | collective-permute-start | bytes 442376 | tf_op jit(solution)/shard_map/ppermute | solution.py:307
  50.2 8.3 %collective-permute-start.7 = (f32[320,128]{1,0:T(8,128)S(1)}, f32[320,128]{1,0:T(8,128)S(1)}, u32[]{:S(2)}, u32[]{:S(2)}) collective-permute-start(f32[320,128]{1,0:T(8,128)S(1)} %get-tuple-element.31), channel_id=1, source_target_pairs={{0,8},{8,16},{16,24},{1,9},{9,17},{17,25},{2,10},{10,18},{18,26},{... | collective-permute-start | bytes 491528 | tf_op jit(solution)/shard_map/ppermute | solution.py:313
  54.6 11.1 %collective-permute-start.8 = (f32[320,128]{1,0:T(8,128)S(1)}, f32[320,128]{1,0:T(8,128)S(1)}, u32[]{:S(2)}, u32[]{:S(2)}) collective-permute-start(f32[320,128]{1,0:T(8,128)S(1)} %get-tuple-element.32), channel_id=1, source_target_pairs={{8,0},{16,8},{24,16},{9,1},{17,9},{25,17},{10,2},{18,10},{26,18},{... | collective-permute-start | bytes 491528 | tf_op jit(solution)/shard_map/ppermute | solution.py:314
where the time goes:
time: 67.2 us; the launch traced here: 66.8 us
  starting transfers between devices  28.1 us (42%)
  waiting for transfers between devices  27.2 us (40%)
  Pallas kernels  8.8 us (13%)
  local copies, waits for them, and re-layouts  2.59 us (4%)
    ppermute x2, waiting for transfers between devices, shards(): lax.ppermute(left, 'gx', back_x)  9.83 us
    ppermute x1, waiting for transfers between devices, shards(): last = lax.ppermute(up, 'gy', back_y)  7.26 us
    ppermute x2, starting transfers between devices, shards(): lax.ppermute(left, 'gx', back_x)  7.18 us
    all_to_all x1, starting transfers between devices, shards(): arrived = lax.all_to_all(sent, 'gx', 0, 0)  5.34 us
    ppermute x1, starting transfers between devices, shards(): before = lax.ppermute(estimate[depth - reach:], 'gy', forth_y)  4.56 us
    ppermute x1, starting transfers between devices, shards(): first = lax.ppermute(down, 'gy', forth_y)  4.4 us
    ppermute x2, starting transfers between devices, shards(): lax.ppermute(right, 'gx', forth_x)  3.94 us
    pallas_call x1, Pallas kernels, shards(): call(predict, (struct(VIEWS, rows, depth, lanes), struct(VIEWS, 2, lanes,...  2.94 us
  transfers between devices with their start and end apart: 10, of which 9 were waited for; matrix products, arithmetic and copies ran while one was open for 0% of the time, Pallas kernels for 5%

commit v1 on v0

--- a/solution.py
+++ b/solution.py
@@ -36,34 +36,60 @@
     return jnp.dot(left, right, preferred_element_type=F32)
 
 
-def along(axis, width):
-    return [(i, i + 1) for i in range(width - 1)], [(i + 1, i) for i in range(width - 1)]
-
-
-def prepare(turns, offsets, recorded, kept, mirrored, sent):
+def pairs(width):
+    def swaps(initial):
+        return [p for i in range(initial, width - 1, 2) for p in ((i, i + 1), (i + 1, i))]
+
+    return swaps(0), swaps(1)
+
+
+def is_odd(axis):
+    return lax.rem(lax.axis_index(axis), 2) == 1
+
+
+def prepare(turns, offsets, recorded, kept, mirrored, *rest):
+    sent, across = rest[:-1], rest[-1]
     depth, rows, lanes = recorded.shape[1:]
-    parts = sent.shape[0]
+    parts = len(sent)
+    me = lax.axis_index("gx")
     kept[...] = recorded[view_of(turns, 0)]
     mirrored[...] = recorded[view_of(turns, 2)]
     for slot, turn in enumerate((1, 3)):
         view = view_of(turns, turn)
         volume = recorded[view].reshape(depth * rows, lanes)
         volume = pltpu.roll(volume, lax.rem(lanes - offsets[view], lanes), 1)
-        across = volume.T
-        for part in range(parts):
-            to = parts - 1 - part if turn == 1 else part
-            sent[to, slot] = across[part * rows : (part + 1) * rows]
-
-
-def edges(own, before, after, left, right):
+        across[...] = volume.T
+        for k in range(parts):
+            to = lax.bitwise_xor(me, k)
+            part = parts - 1 - to if turn == 1 else to
+            sent[k][slot] = across[pl.ds(pl.multiple_of(part * rows, rows), rows)]
+
+
+def edges(own, even_pair, odd_pair):
+    rows = own.shape[1]
+    side = even_pair.shape[0]
+    odd = is_odd("gx")
+    for i in range(side):
+        first, last = own[:, i], own[:, rows - side + i]
+        even_pair[i] = jnp.where(odd, first, last)
+        odd_pair[i] = jnp.where(odd, last, first)
+
+
+def layers_out(own, from_even, from_odd, even_pair, odd_pair):
     depth, rows, _ = own.shape
-    reach = before.shape[0]
-    side = left.shape[0]
-    for target, initial in ((left, 0), (right, rows - side)):
-        for i in range(side):
-            target[i, 0:depth] = own[:, initial + i]
-            target[i, depth : depth + reach] = before[:, initial + i]
-            target[i, depth + reach : depth + 2 * reach] = after[:, initial + i]
+    side = from_even.shape[0]
+    reach = even_pair.shape[0] // (rows + 2 * side)
+    odd_x, odd_y = is_odd("gx"), is_odd("gy")
+    for e in range(rows + 2 * side):
+        if e < side:
+            value = jnp.where(odd_x, from_even[e], from_odd[e])
+        elif e < side + rows:
+            value = own[:, e - side]
+        else:
+            value = jnp.where(odd_x, from_odd[e - side - rows], from_even[e - side - rows])
+        first, last = value[:reach], value[depth - reach :]
+        even_pair[e * reach : (e + 1) * reach] = jnp.where(odd_y, first, last)
+        odd_pair[e * reach : (e + 1) * reach] = jnp.where(odd_y, last, first)
 
 
 def row_taps_of(turn, view, row_taps, column_taps, width):
@@ -72,11 +98,11 @@
     return [source[view, width - 1 - s if flipped else s] for s in range(width)]
 
 
-def predict(turns, offsets, depth_taps, row_taps, column_taps, own, before, after, left, right,
+def predict(turns, offsets, depth_taps, row_taps, column_taps, own, even_x, odd_x, even_y, odd_y,
             predicted, lane_back, depth_back, extended, blurred):
     depth, rows, lanes = own.shape
-    reach = before.shape[0]
-    side = left.shape[0]
+    side = even_x.shape[0]
+    reach = even_y.shape[0] // (rows + 2 * side)
     width = 2 * side + 1
     deep = depth + 2 * reach
     padded = extended.shape[1]
@@ -97,20 +123,21 @@
     depth_back[0] = back_high
     depth_back[1] = back_low
     high, low = split(matrix)
-    zero = jnp.zeros((VIEWS * depth, LANES - padded), BF16)
-    del zero
     depth_high, depth_low = high[:, :padded], low[:, :padded]
 
-    for i in range(side):
-        extended[i, 0:deep] = left[i]
-        extended[side + rows + i, 0:deep] = right[i]
-    for i in range(rows):
-        extended[side + i, 0:depth] = own[:, i]
-        extended[side + i, depth : depth + reach] = before[:, i]
-        extended[side + i, depth + reach : deep] = after[:, i]
-    if padded > deep:
-        for i in range(rows + 2 * side):
-            extended[i, deep:padded] = jnp.zeros((padded - deep, lanes), F32)
+    flip_x, flip_y = is_odd("gx"), is_odd("gy")
+    for e in range(rows + 2 * side):
+        if e < side:
+            extended[e, 0:depth] = jnp.where(flip_x, even_x[e], odd_x[e])
+        elif e < side + rows:
+            extended[e, 0:depth] = own[:, e - side]
+        else:
+            extended[e, 0:depth] = jnp.where(flip_x, odd_x[e - side - rows], even_x[e - side - rows])
+        even, odd = even_y[e * reach : (e + 1) * reach], odd_y[e * reach : (e + 1) * reach]
+        extended[e, depth : depth + reach] = jnp.where(flip_y, even, odd)
+        extended[e, depth + reach : deep] = jnp.where(flip_y, odd, even)
+        if padded > deep:
+            extended[e, deep:padded] = jnp.zeros((padded - deep, lanes), F32)
 
     for i in range(rows + 2 * side):
         e_high, e_low = split(extended[i])
@@ -143,16 +170,21 @@
             predicted[turn, i] = dot(jnp.concatenate([t_high, t_low], axis=1), both) + dot(t_high, low)
 
 
-def project(turns, row_taps, column_taps, predicted, lane_back, depth_back, kept, mirrored, arrived,
-            middle, left, right, data, backed, spread):
+def project(turns, row_taps, column_taps, predicted, lane_back, depth_back, kept, mirrored, *rest):
+    received = rest[:-7]
+    middle, even_pair, odd_pair, arrived, data, backed, spread = rest[-7:]
     _, rows, depth, lanes = predicted.shape
-    side = left.shape[0]
-    deep = left.shape[1]
+    side = even_pair.shape[0]
+    deep = even_pair.shape[1]
     width = 2 * side + 1
     views = [view_of(turns, turn) for turn in range(VIEWS)]
     parts = arrived.shape[0]
     group = LANES // rows
     granule = lax.broadcasted_iota(jnp.int32, (8, LANES), 1) // rows
+
+    me = lax.axis_index("gx")
+    for k in range(parts):
+        arrived[lax.bitwise_xor(me, k)] = received[k][...]
 
     for slot in range(2):
         for part in range(0, parts, group):
@@ -199,44 +231,50 @@
 
     high, low = depth_back[0], depth_back[1]
     both = jnp.concatenate([high, low], axis=1)
+    results = []
     for e in range(rows + 2 * side):
         s_high, s_low = split(spread[e])
         result = dot(both, jnp.concatenate([s_high, s_high], axis=0)) + dot(high, s_low)
         result = result[:deep]
-        if e < side:
-            left[e] = result
-        elif e < side + rows:
+        if side <= e < side + rows:
             middle[e - side] = result
         else:
-            right[e - side - rows] = result
-
-
-def gather_sides(middle, left, right, own, up, down):
+            results.append(result)
+    odd = is_odd("gx")
+    for i in range(side):
+        first, last = results[i], results[side + i]
+        even_pair[i] = jnp.where(odd, first, last)
+        odd_pair[i] = jnp.where(odd, last, first)
+
+
+def gather_sides(middle, even_x, odd_x, own, even_pair, odd_pair):
     rows = middle.shape[0]
-    side = left.shape[0]
+    side = even_x.shape[0]
     depth = own.shape[1]
-    reach = up.shape[0] // rows
+    reach = even_pair.shape[0] // rows
+    flip_x, flip_y = is_odd("gx"), is_odd("gy")
     for i in range(rows):
         value = middle[i]
         if i < side:
-            value = value + left[i]
+            value = value + jnp.where(flip_x, even_x[i], odd_x[i])
         if i >= rows - side:
-            value = value + right[i - rows + side]
+            j = i - rows + side
+            value = value + jnp.where(flip_x, odd_x[j], even_x[j])
         own[i] = value[:depth]
-        up[i * reach : (i + 1) * reach] = value[depth : depth + reach]
-        down[i * reach : (i + 1) * reach] = value[depth + reach : depth + 2 * reach]
-
-
-def finish(estimate, own, up, down, out):
-    rows, depth, _ = own.shape
-    reach = up.shape[0] // rows
+        before, after = value[depth : depth + reach], value[depth + reach : depth + 2 * reach]
+        even_pair[i * reach : (i + 1) * reach] = jnp.where(flip_y, before, after)
+        odd_pair[i * reach : (i + 1) * reach] = jnp.where(flip_y, after, before)
+
+
+def finish(estimate, own, even_y, odd_y, out):
+    rows, depth, lanes = own.shape
+    reach = even_y.shape[0] // rows
+    flip_y = is_odd("gy")
+    rest = jnp.zeros((depth - reach, lanes), F32)
     for i in range(rows):
-        value = own[i]
-        lane = value.shape[1]
-        first = up[i * reach : (i + 1) * reach]
-        last = down[i * reach : (i + 1) * reach]
-        rest = jnp.zeros((depth - reach, lane), F32)
-        value = value + jnp.concatenate([first, rest], axis=0) + jnp.concatenate([rest, last], axis=0)
+        even, odd = even_y[i * reach : (i + 1) * reach], odd_y[i * reach : (i + 1) * reach]
+        first, last = jnp.where(flip_y, even, odd), jnp.where(flip_y, odd, even)
+        value = own[i] + jnp.concatenate([first, rest], axis=0) + jnp.concatenate([rest, last], axis=0)
         out[:, i] = estimate[:, i] * value * (1.0 / VIEWS)
 
 
@@ -259,23 +297,23 @@
     deep = depth + 2 * reach
     padded = -(-deep // 16) * 16
     parts = lax.axis_size("gx")
-    forth_y, back_y = along("gy", lax.axis_size("gy"))
-    forth_x, back_x = along("gx", parts)
-
-    before = lax.ppermute(estimate[depth - reach :], "gy", forth_y)
-    after = lax.ppermute(estimate[:reach], "gy", back_y)
-    kept, mirrored, sent = call(
+    even_y, odd_y = pairs(lax.axis_size("gy"))
+    even_x, odd_x = pairs(parts)
+
+    first, second = call(edges, (struct(side, depth, lanes),) * 2, [VMEM])(estimate)
+    first, second = lax.ppermute(first, "gx", even_x), lax.ppermute(second, "gx", odd_x)
+    kept, mirrored, *sent = call(
         prepare,
-        (struct(depth, rows, lanes), struct(depth, rows, lanes), struct(parts, 2, rows, depth * rows)),
+        (struct(depth, rows, lanes),) * 2 + (struct(2, rows, depth * rows),) * parts,
         [SMEM, SMEM, VMEM],
+        [pltpu.VMEM((lanes, depth * rows), F32)],
     )(quarter_turns, offsets, recorded)
     mirrored = lax.ppermute(mirrored, "gx", [(i, parts - 1 - i) for i in range(parts)])
-    arrived = lax.all_to_all(sent, "gx", 0, 0)
-
-    left, right = call(
-        edges, (struct(side, deep, lanes), struct(side, deep, lanes)), [VMEM] * 3
-    )(estimate, before, after)
-    left, right = lax.ppermute(right, "gx", forth_x), lax.ppermute(left, "gx", back_x)
+    third, fourth = call(layers_out, (struct((rows + 2 * side) * reach, lanes),) * 2, [VMEM] * 3)(estimate, first, second)
+    third, fourth = lax.ppermute(third, "gy", even_y), lax.ppermute(fourth, "gy", odd_y)
+    arrived = [sent[0]] + [
+        lax.ppermute(sent[k], "gx", [(i, i ^ k) for i in range(parts)]) for k in range(1, parts)
+    ]
 
     predicted, lane_back, depth_back = call(
         predict,
@@ -290,29 +328,29 @@
             pltpu.VMEM((rows + 2 * side, VIEWS * depth, lanes), F32),
         ],
         pl.CostEstimate(flops=4_000_000_000, bytes_accessed=4_000_000, transcendentals=0),
-    )(quarter_turns, offsets, depth_taps, row_taps, column_taps, estimate, before, after, left, right)
-
-    middle, left, right = call(
+    )(quarter_turns, offsets, depth_taps, row_taps, column_taps, estimate, first, second, third, fourth)
+
+    middle, first, second = call(
         project,
         (struct(rows, deep, lanes), struct(side, deep, lanes), struct(side, deep, lanes)),
-        [SMEM] * 3 + [VMEM] * 6,
+        [SMEM] * 3 + [VMEM] * (5 + parts),
         [
+            pltpu.VMEM((parts, 2, rows, depth * rows), F32),
             pltpu.VMEM((2, rows, depth, lanes), F32),
             pltpu.VMEM((VIEWS, rows, depth, lanes), F32),
             pltpu.VMEM((rows + 2 * side, VIEWS * depth, lanes), F32),
         ],
         pl.CostEstimate(flops=4_000_000_000, bytes_accessed=4_000_000, transcendentals=0),
-    )(quarter_turns, row_taps, column_taps, predicted, lane_back, depth_back, kept, mirrored, arrived)
-
-    left, right = lax.ppermute(right, "gx", forth_x), lax.ppermute(left, "gx", back_x)
-    own, up, down = call(
+    )(quarter_turns, row_taps, column_taps, predicted, lane_back, depth_back, kept, mirrored, *arrived)
+
+    first, second = lax.ppermute(first, "gx", even_x), lax.ppermute(second, "gx", odd_x)
+    own, third, fourth = call(
         gather_sides,
         (struct(rows, depth, lanes), struct(rows * reach, lanes), struct(rows * reach, lanes)),
         [VMEM] * 3,
-    )(middle, left, right)
-    first = lax.ppermute(down, "gy", forth_y)
-    last = lax.ppermute(up, "gy", back_y)
-    return call(finish, struct(depth, rows, lanes), [VMEM] * 4)(estimate, own, first, last)
+    )(middle, first, second)
+    third, fourth = lax.ppermute(third, "gy", even_y), lax.ppermute(fourth, "gy", odd_y)
+    return call(finish, struct(depth, rows, lanes), [VMEM] * 4)(estimate, own, third, fourth)
 
 
 def solution(mesh):

time: 67.2 us -> 63.2 us (0.940)
  the two profiles are of different devices: /device:TPU:16 before, /device:TPU:12 now
where the time goes in v1:
time: 63.2 us; the launch traced here: 62.8 us
  waiting for transfers between devices  30.4 us (48%)
  starting transfers between devices  21.8 us (34%)
  Pallas kernels  8.17 us (13%)
  local copies, waits for them, and re-layouts  2.2 us (3%)
    ppermute x7, waiting for transfers between devices, shards(): lax.ppermute(sent[k], 'gx', [(i, i ^ k) for i in range(parts)])  10.8 us
    ppermute x7, starting transfers between devices, shards(): lax.ppermute(sent[k], 'gx', [(i, i ^ k) for i in range(parts)])  8.61 us
    ppermute x2, waiting for transfers between devices, shards(): lax.ppermute(second, 'gx', odd_x)  7.64 us
    ppermute x2, starting transfers between devices, shards(): lax.ppermute(fourth, 'gy', odd_y)  6.88 us
    ppermute x1, waiting for transfers between devices, shards(): lax.ppermute(mirrored, 'gx', [(i, parts - 1 - i) for i in range(parts)])  5.62 us
    ppermute x2, starting transfers between devices, shards(): lax.ppermute(second, 'gx', odd_x)  4.36 us
    ppermute x2, waiting for transfers between devices, shards(): lax.ppermute(fourth, 'gy', odd_y)  4.24 us
    pallas_call x1, Pallas kernels, shards(): call(project, (struct(rows, deep, lanes), struct(side, deep, lanes), stru...  2.91 us
  transfers between devices with their start and end apart: 16, of which 9 were waited for; matrix products, arithmetic and copies ran while one was open for 0% of the time, Pallas kernels for 6%

profile of v1, /device:TPU:12, one launch (start us, length us, event | category | flops | bytes accessed | tf_op | source)
XLA Modules:
  0.0 62.8 jit_solution(2593920786075125853)
XLA Ops:
  0.0 0.0 copy-start
  0.0 0.9 %copy-done = f32[32,16,128]{2,1,0:T(8,128)S(1)} copy-done((f32[32,16,128]{2,1,0:T(8,128)S(1)}, f32[32,16,128]{2,1,0:T(8,128)}, u32[]{:S(2)}) %copy-start) | copy-done | bytes 262168
  1.0 0.1 shard_map.73
  1.1 0.1 collective-permute-start
  1.1 2.4 %collective-permute-start.1 = (f32[4,32,128]{2,1,0:T(8,128)S(1)}, f32[4,32,128]{2,1,0:T(8,128)S(1)}, u32[]{:S(2)}, u32[]{:S(2)}) collective-permute-start(f32[4,32,128]{2,1,0:T(8,128)S(1)} %get-tuple-element.29), channel_id=1, source_target_pairs={{1,2},{2,1},{3,4},{4,3},{5,6},{6,5},{9,10},{10,9},{11,12},{12,11},... | collective-permute-start | bytes 196616 | tf_op jit(solution)/shard_map/ppermute | solution.py:304
  3.6 0.0 collective-permute-done.from_even.even_x
  3.6 3.1 %collective-permute-done.1.from_odd.odd_x = f32[4,32,128]{2,1,0:T(8,128)S(1)} collective-permute-done((f32[4,32,128]{2,1,0:T(8,128)S(1)}, f32[4,32,128]{2,1,0:T(8,128)S(1)}, u32[]{:S(2)}, u32[]{:S(2)}) %collective-permute-start.1) | collective-permute-done | bytes 65568 | tf_op jit(solution)/shard_map/ppermute | solution.py:304
  6.7 0.3 shard_map.74
  7.0 0.0 copy-start.3
  7.0 0.0 copy-start.4
  7.0 1.6 %collective-permute-start.2 = (f32[480,128]{1,0:T(8,128)S(1)}, f32[480,128]{1,0:T(8,128)S(1)}, u32[]{:S(2)}, u32[]{:S(2)}) collective-permute-start(f32[480,128]{1,0:T(8,128)S(1)} %get-tuple-element.30), channel_id=1, source_target_pairs={{0,8},{8,0},{16,24},{24,16},{1,9},{9,1},{17,25},{25,17},{2,10},{10... | collective-permute-start | bytes 737288 | tf_op jit(solution)/shard_map/ppermute | solution.py:313
  8.6 0.0 copy-start.1
  8.6 2.5 %collective-permute-start.3 = (f32[480,128]{1,0:T(8,128)S(1)}, f32[480,128]{1,0:T(8,128)S(1)}, u32[]{:S(2)}, u32[]{:S(2)}) collective-permute-start(f32[480,128]{1,0:T(8,128)S(1)} %get-tuple-element.31), channel_id=1, source_target_pairs={{8,16},{16,8},{9,17},{17,9},{10,18},{18,10},{11,19},{19,11},{12,20... | collective-permute-start | bytes 737288 | tf_op jit(solution)/shard_map/ppermute | solution.py:313
  11.1 0.0 copy-done.3
  11.1 0.0 copy-done.4
  11.1 0.0 copy-start.2
  11.1 1.2 %copy-done.2 = f32[4,32,16,128]{3,2,1,0:T(8,128)S(1)} copy-done((f32[4,32,16,128]{3,2,1,0:T(8,128)S(1)}, f32[4,32,16,128]{3,2,1,0:T(8,128)}, u32[]{:S(2)}) %copy-start.2) | copy-done | bytes 1048600
  12.3 0.0 copy-start.7
  12.3 0.9 %shard_map.76 = (f32[32,16,128]{2,1,0:T(8,128)S(1)}, f32[32,16,128]{2,1,0:T(8,128)S(1)}, f32[2,16,512]{2,1,0:T(8,128)S(1)}, f32[2,16,512]{2,1,0:T(8,128)S(1)}, f...) custom-call(s32[4]{0:T(128)S(1)} %copy-done.4, ...), custom_call_target="tpu_custom_call" | custom-call | tf_op jit(solution)/shard_map/pallas_call | solution.py:305
  13.3 0.1 collective-permute-start.5
  13.4 0.5 collective-permute-start.6
  13.8 1.4 %collective-permute-start.7 = (f32[2,16,512]{2,1,0:T(8,128)S(1)}, f32[2,16,512]{2,1,0:T(8,128)S(1)}, u32[]{:S(2)}, u32[]{:S(2)}) collective-permute-start(f32[2,16,512]{2,1,0:T(8,128)S(1)} %get-tuple-element.40), channel_id=1, source_target_pairs={{0,3},{1,2},{2,1},{3,0},{4,7},{5,6},{6,5},{7,4},{8,11},{9,10},{10,... | collective-permute-start | bytes 196616 | tf_op jit(solution)/shard_map/ppermute | solution.py:315
  15.2 0.0 collective-permute-done.5.rest_1_
  15.2 2.6 %collective-permute-start.8 = (f32[2,16,512]{2,1,0:T(8,128)S(1)}, f32[2,16,512]{2,1,0:T(8,128)S(1)}, u32[]{:S(2)}, u32[]{:S(2)}) collective-permute-start(f32[2,16,512]{2,1,0:T(8,128)S(1)} %get-tuple-element.41), channel_id=1, source_target_pairs={{0,4},{1,5},{2,6},{3,7},{4,0},{5,1},{6,2},{7,3},{8,12},{9,13},{10,... | collective-permute-start | bytes 196616 | tf_op jit(solution)/shard_map/ppermute | solution.py:315
  17.8 0.5 collective-permute-done.6.rest_2_
  18.3 1.4 %collective-permute-start.9 = (f32[2,16,512]{2,1,0:T(8,128)S(1)}, f32[2,16,512]{2,1,0:T(8,128)S(1)}, u32[]{:S(2)}, u32[]{:S(2)}) collective-permute-start(f32[2,16,512]{2,1,0:T(8,128)S(1)} %get-tuple-element.42), channel_id=1, source_target_pairs={{0,5},{1,4},{2,7},{3,6},{4,1},{5,0},{6,3},{7,2},{8,13},{9,12},{10,... | collective-permute-start | bytes 196616 | tf_op jit(solution)/shard_map/ppermute | solution.py:315
  19.7 0.0 collective-permute-done.7.rest_3_
  19.7 0.0 copy-start.6
  19.7 0.0 copy-start.5
  19.7 0.9 %collective-permute-start.10 = (f32[2,16,512]{2,1,0:T(8,128)S(1)}, f32[2,16,512]{2,1,0:T(8,128)S(1)}, u32[]{:S(2)}, u32[]{:S(2)}) collective-permute-start(f32[2,16,512]{2,1,0:T(8,128)S(1)} %get-tuple-element.43), channel_id=1, source_target_pairs={{0,6},{1,7},{2,4},{3,5},{4,2},{5,3},{6,0},{7,1},{8,14},{9,15},{10,... | collective-permute-start | bytes 196616 | tf_op jit(solution)/shard_map/ppermute | solution.py:315
  20.6 0.0 collective-permute-done.2.even_y
  20.6 1.8 %collective-permute-start.11 = (f32[2,16,512]{2,1,0:T(8,128)S(1)}, f32[2,16,512]{2,1,0:T(8,128)S(1)}, u32[]{:S(2)}, u32[]{:S(2)}) collective-permute-start(f32[2,16,512]{2,1,0:T(8,128)S(1)} %get-tuple-element.44), channel_id=1, source_target_pairs={{0,7},{1,6},{2,5},{3,4},{4,3},{5,2},{6,1},{7,0},{8,15},{9,14},{10,... | collective-permute-start | bytes 196616 | tf_op jit(solution)/shard_map/ppermute | solution.py:315
  22.4 0.0 collective-permute-done.3.odd_y
  22.4 0.1 collective-permute-start.4
  22.5 0.0 copy-done.1
  22.5 0.0 copy-done.7
  22.5 0.0 copy-done.6
  22.5 0.0 copy-done.5
  22.5 2.8 %shard_map.75 = (f32[4,16,32,128]{3,2,1,0:T(8,128)S(1)}, bf16[4,2,128,128]{3,2,1,0:T(8,128)(2,1)S(1)}, bf16[2,80,128]{2,1,0:T(8,128)(2,1)S(1)}) custom-call(s32[4]{0:T(128)S(1)} %copy-done.4, s32[4]{0:T(128)S(1)} %copy-done.3, f32[4,41]{1,0:T(4,128)S(1)} %copy-done.5, f32[4,9]{1,0:T(4,128)S(1)} %copy-done.6, f32[4,9]{1,0:T(4,128)S(1)} %copy-done.7, ...), custom_call_target="tpu_custom_call" | custom-call | flops 4000000000 | bytes 4000000 | tf_op jit(solution)/shard_map/pallas_call | solution.py:318
  25.4 0.0 collective-permute-done.8.rest_4_
  25.4 1.3 %collective-permute-done.9.rest_5_ = f32[2,16,512]{2,1,0:T(8,128)S(1)} collective-permute-done((f32[2,16,512]{2,1,0:T(8,128)S(1)}, f32[2,16,512]{2,1,0:T(8,128)S(1)}, u32[]{:S(2)}, u32[]{:S(2)}) %collective-permute-start.9) | collective-permute-done | bytes 65568 | tf_op jit(solution)/shard_map/ppermute | solution.py:315
  26.6 7.9 %collective-permute-done.10.rest_6_ = f32[2,16,512]{2,1,0:T(8,128)S(1)} collective-permute-done((f32[2,16,512]{2,1,0:T(8,128)S(1)}, f32[2,16,512]{2,1,0:T(8,128)S(1)}, u32[]{:S(2)}, u32[]{:S(2)}) %collective-permute-start.10) | collective-permute-done | bytes 65568 | tf_op jit(solution)/shard_map/ppermute | solution.py:315
  34.6 1.1 %collective-permute-done.11.rest_7_ = f32[2,16,512]{2,1,0:T(8,128)S(1)} collective-permute-done((f32[2,16,512]{2,1,0:T(8,128)S(1)}, f32[2,16,512]{2,1,0:T(8,128)S(1)}, u32[]{:S(2)}, u32[]{:S(2)}) %collective-permute-start.11) | collective-permute-done | bytes 65568 | tf_op jit(solution)/shard_map/ppermute | solution.py:315
  35.7 5.6 %collective-permute-done.4.mirrored = f32[32,16,128]{2,1,0:T(8,128)S(1)} collective-permute-done((f32[32,16,128]{2,1,0:T(8,128)S(1)}, f32[32,16,128]{2,1,0:T(8,128)S(1)}, u32[]{:S(2)}, u32[]{:S(2)}) %collective-permute-start.4) | collective-permute-done | bytes 262176 | tf_op jit(solution)/shard_map/ppermute | solution.py:311
  41.3 2.9 %shard_map.77 = (f32[16,72,128]{2,1,0:T(8,128)S(1)}, f32[4,72,128]{2,1,0:T(8,128)S(1)}, f32[4,72,128]{2,1,0:T(8,128)S(1)}) custom-call(s32[4]{0:T(128)S(1)} %copy-done.4, f32[4,9]{1,0:T(4,128)S(1)} %copy-done.6, f32[4,9]{1,0:T(4,128)S(1)} %copy-done.7, f32[4,16,32,128]{3,2,1,0:T(8,128)S(1)} %get-tuple-element.32.predicted, ...), custom_call_target="tpu_custom_call" | custom-call | flops 4000000000 | bytes 4000000 | tf_op jit(solution)/shard_map/pallas_call | solution.py:333
  44.2 0.2 collective-permute-start.12
  44.4 1.9 %collective-permute-start.13 = (f32[4,72,128]{2,1,0:T(8,128)S(1)}, f32[4,72,128]{2,1,0:T(8,128)S(1)}, u32[]{:S(2)}, u32[]{:S(2)}) collective-permute-start(f32[4,72,128]{2,1,0:T(8,128)S(1)} %get-tuple-element.47), channel_id=1, source_target_pairs={{1,2},{2,1},{3,4},{4,3},{5,6},{6,5},{9,10},{10,9},{11,12},{12,11},... | collective-permute-start | bytes 442376 | tf_op jit(solution)/shard_map/ppermute | solution.py:346
  46.3 0.0 collective-permute-done.12.even_x
  46.3 4.5 %collective-permute-done.13.odd_x = f32[4,72,128]{2,1,0:T(8,128)S(1)} collective-permute-done((f32[4,72,128]{2,1,0:T(8,128)S(1)}, f32[4,72,128]{2,1,0:T(8,128)S(1)}, u32[]{:S(2)}, u32[]{:S(2)}) %collective-permute-start.13) | collective-permute-done | bytes 147488 | tf_op jit(solution)/shard_map/ppermute | solution.py:346
  50.9 0.1 shard_map.78
  50.9 0.1 collective-permute-start.14
  51.0 4.4 %collective-permute-start.15 = (f32[320,128]{1,0:T(8,128)S(1)}, f32[320,128]{1,0:T(8,128)S(1)}, u32[]{:S(2)}, u32[]{:S(2)}) collective-permute-start(f32[320,128]{1,0:T(8,128)S(1)} %get-tuple-element.50), channel_id=1, source_target_pairs={{8,16},{16,8},{9,17},{17,9},{10,18},{18,10},{11,19},{19,11},{12,20... | collective-permute-start | bytes 491528 | tf_op jit(solution)/shard_map/ppermute | solution.py:352
  55.4 2.1 %collective-permute-done.14.even_y = f32[320,128]{1,0:T(8,128)S(1)} collective-permute-done((f32[320,128]{1,0:T(8,128)S(1)}, f32[320,128]{1,0:T(8,128)S(1)}, u32[]{:S(2)}, u32[]{:S(2)}) %collective-permute-start.14) | collective-permute-done | bytes 163872 | tf_op jit(solution)/shard_map/ppermute | solution.py:352
  57.5 4.2 %collective-permute-done.15.odd_y = f32[320,128]{1,0:T(8,128)S(1)} collective-permute-done((f32[320,128]{1,0:T(8,128)S(1)}, f32[320,128]{1,0:T(8,128)S(1)}, u32[]{:S(2)}, u32[]{:S(2)}) %collective-permute-start.15) | collective-permute-done | bytes 163872 | tf_op jit(solution)/shard_map/ppermute | solution.py:352
  61.8 1.0 %shard_map.79 = f32[32,16,128]{2,1,0:T(8,128)} custom-call(f32[32,16,128]{2,1,0:T(8,128)S(1)} %copy-done.1, f32[16,32,128]{2,1,0:T(8,128)S(1)} %get-tuple-element.48.own, f32[320,128]{1,0:T(8,128)S(1)} %collective-permute-done.14.even_y, f32[320,128]{1,0:T(8,128)S(1)} %collective-permute-done.15.odd_y), custom_call_target="tpu_custom_call" | custom-call | tf_op jit(solution)/shard_map/pallas_call | solution.py:353
Async XLA Ops:
  0.0 0.9 %copy-start = (f32[32,16,128]{2,1,0:T(8,128)S(1)}, f32[32,16,128]{2,1,0:T(8,128)}, u32[]{:S(2)}) copy-start(f32[32,16,128]{2,1,0:T(8,128)} %estimate.1) | copy-start | bytes 786436
  1.1 2.5 %collective-permute-start = (f32[4,32,128]{2,1,0:T(8,128)S(1)}, f32[4,32,128]{2,1,0:T(8,128)S(1)}, u32[]{:S(2)}, u32[]{:S(2)}) collective-permute-start(f32[4,32,128]{2,1,0:T(8,128)S(1)} %get-tuple-element.28), channel_id=1, source_target_pairs={{0,1},{1,0},{2,3},{3,2},{4,5},{5,4},{6,7},{7,6},{8,9},{9,8},{10,11... | collective-permute-start | bytes 196616 | tf_op jit(solution)/shard_map/ppermute | solution.py:304
  1.1 5.6 %collective-permute-start.1 = (f32[4,32,128]{2,1,0:T(8,128)S(1)}, f32[4,32,128]{2,1,0:T(8,128)S(1)}, u32[]{:S(2)}, u32[]{:S(2)}) collective-permute-start(f32[4,32,128]{2,1,0:T(8,128)S(1)} %get-tuple-element.29), channel_id=1, source_target_pairs={{1,2},{2,1},{3,4},{4,3},{5,6},{6,5},{9,10},{10,9},{11,12},{12,11},... | collective-permute-start | bytes 196616 | tf_op jit(solution)/shard_map/ppermute | solution.py:304
  7.0 4.1 %copy-start.3 = (s32[4]{0:T(128)S(1)}, s32[4]{0:T(128)}, u32[]{:S(2)}) copy-start(s32[4]{0:T(128)} %offsets.3) | copy-start | bytes 52
  7.0 4.1 %copy-start.4 = (s32[4]{0:T(128)S(1)}, s32[4]{0:T(128)}, u32[]{:S(2)}) copy-start(s32[4]{0:T(128)} %turns.5) | copy-start | bytes 52
  7.0 13.6 %collective-permute-start.2 = (f32[480,128]{1,0:T(8,128)S(1)}, f32[480,128]{1,0:T(8,128)S(1)}, u32[]{:S(2)}, u32[]{:S(2)}) collective-permute-start(f32[480,128]{1,0:T(8,128)S(1)} %get-tuple-element.30), channel_id=1, source_target_pairs={{0,8},{8,0},{16,24},{24,16},{1,9},{9,1},{17,25},{25,17},{2,10},{10... | collective-permute-start | bytes 737288 | tf_op jit(solution)/shard_map/ppermute | solution.py:313
  8.6 13.9 %copy-start.1 = (f32[32,16,128]{2,1,0:T(8,128)S(1)}, f32[32,16,128]{2,1,0:T(8,128)}, u32[]{:S(2)}) copy-start(f32[32,16,128]{2,1,0:T(8,128)} %estimate.1) | copy-start | bytes 786436
  8.6 13.8 %collective-permute-start.3 = (f32[480,128]{1,0:T(8,128)S(1)}, f32[480,128]{1,0:T(8,128)S(1)}, u32[]{:S(2)}, u32[]{:S(2)}) collective-permute-start(f32[480,128]{1,0:T(8,128)S(1)} %get-tuple-element.31), channel_id=1, source_target_pairs={{8,16},{16,8},{9,17},{17,9},{10,18},{18,10},{11,19},{19,11},{12,20... | collective-permute-start | bytes 737288 | tf_op jit(solution)/shard_map/ppermute | solution.py:313
  11.1 1.2 %copy-start.2 = (f32[4,32,16,128]{3,2,1,0:T(8,128)S(1)}, f32[4,32,16,128]{3,2,1,0:T(8,128)}, u32[]{:S(2)}) copy-start(f32[4,32,16,128]{3,2,1,0:T(8,128)} %recorded.1) | copy-start | bytes 3145732
  12.3 10.2 %copy-start.7 = (f32[4,9]{1,0:T(4,128)S(1)}, f32[4,9]{1,0:T(4,128)}, u32[]{:S(2)}) copy-start(f32[4,9]{1,0:T(4,128)} %column_taps.3) | copy-start | bytes 436
  13.3 1.9 %collective-permute-start.5 = (f32[2,16,512]{2,1,0:T(8,128)S(1)}, f32[2,16,512]{2,1,0:T(8,128)S(1)}, u32[]{:S(2)}, u32[]{:S(2)}) collective-permute-start(f32[2,16,512]{2,1,0:T(8,128)S(1)} %get-tuple-element.38), channel_id=1, source_target_pairs={{0,1},{1,0},{2,3},{3,2},{4,5},{5,4},{6,7},{7,6},{8,9},{9,8},{10,11... | collective-permute-start | bytes 196616 | tf_op jit(solution)/shard_map/ppermute | solution.py:315
  13.4 5.0 %collective-permute-start.6 = (f32[2,16,512]{2,1,0:T(8,128)S(1)}, f32[2,16,512]{2,1,0:T(8,128)S(1)}, u32[]{:S(2)}, u32[]{:S(2)}) collective-permute-start(f32[2,16,512]{2,1,0:T(8,128)S(1)} %get-tuple-element.39), channel_id=1, source_target_pairs={{0,2},{1,3},{2,0},{3,1},{4,6},{5,7},{6,4},{7,5},{8,10},{9,11},{10,... | collective-permute-start | bytes 196616 | tf_op jit(solution)/shard_map/ppermute | solution.py:315
  13.8 5.9 %collective-permute-start.7 = (f32[2,16,512]{2,1,0:T(8,128)S(1)}, f32[2,16,512]{2,1,0:T(8,128)S(1)}, u32[]{:S(2)}, u32[]{:S(2)}) collective-permute-start(f32[2,16,512]{2,1,0:T(8,128)S(1)} %get-tuple-element.40), channel_id=1, source_target_pairs={{0,3},{1,2},{2,1},{3,0},{4,7},{5,6},{6,5},{7,4},{8,11},{9,10},{10,... | collective-permute-start | bytes 196616 | tf_op jit(solution)/shard_map/ppermute | solution.py:315
  15.2 10.1 %collective-permute-start.8 = (f32[2,16,512]{2,1,0:T(8,128)S(1)}, f32[2,16,512]{2,1,0:T(8,128)S(1)}, u32[]{:S(2)}, u32[]{:S(2)}) collective-permute-start(f32[2,16,512]{2,1,0:T(8,128)S(1)} %get-tuple-element.41), channel_id=1, source_target_pairs={{0,4},{1,5},{2,6},{3,7},{4,0},{5,1},{6,2},{7,3},{8,12},{9,13},{10,... | collective-permute-start | bytes 196616 | tf_op jit(solution)/shard_map/ppermute | solution.py:315
  18.3 8.3 %collective-permute-start.9 = (f32[2,16,512]{2,1,0:T(8,128)S(1)}, f32[2,16,512]{2,1,0:T(8,128)S(1)}, u32[]{:S(2)}, u32[]{:S(2)}) collective-permute-start(f32[2,16,512]{2,1,0:T(8,128)S(1)} %get-tuple-element.42), channel_id=1, source_target_pairs={{0,5},{1,4},{2,7},{3,6},{4,1},{5,0},{6,3},{7,2},{8,13},{9,12},{10,... | collective-permute-start | bytes 196616 | tf_op jit(solution)/shard_map/ppermute | solution.py:315
  19.7 2.8 %copy-start.6 = (f32[4,9]{1,0:T(4,128)S(1)}, f32[4,9]{1,0:T(4,128)}, u32[]{:S(2)}) copy-start(f32[4,9]{1,0:T(4,128)} %row_taps.3) | copy-start | bytes 436
  19.7 2.8 %copy-start.5 = (f32[4,41]{1,0:T(4,128)S(1)}, f32[4,41]{1,0:T(4,128)}, u32[]{:S(2)}) copy-start(f32[4,41]{1,0:T(4,128)} %depth_taps.1) | copy-start | bytes 1972
  19.7 14.8 %collective-permute-start.10 = (f32[2,16,512]{2,1,0:T(8,128)S(1)}, f32[2,16,512]{2,1,0:T(8,128)S(1)}, u32[]{:S(2)}, u32[]{:S(2)}) collective-permute-start(f32[2,16,512]{2,1,0:T(8,128)S(1)} %get-tuple-element.43), channel_id=1, source_target_pairs={{0,6},{1,7},{2,4},{3,5},{4,2},{5,3},{6,0},{7,1},{8,14},{9,15},{10,... | collective-permute-start | bytes 196616 | tf_op jit(solution)/shard_map/ppermute | solution.py:315
  20.6 15.1 %collective-permute-start.11 = (f32[2,16,512]{2,1,0:T(8,128)S(1)}, f32[2,16,512]{2,1,0:T(8,128)S(1)}, u32[]{:S(2)}, u32[]{:S(2)}) collective-permute-start(f32[2,16,512]{2,1,0:T(8,128)S(1)} %get-tuple-element.44), channel_id=1, source_target_pairs={{0,7},{1,6},{2,5},{3,4},{4,3},{5,2},{6,1},{7,0},{8,15},{9,14},{10,... | collective-permute-start | bytes 196616 | tf_op jit(solution)/shard_map/ppermute | solution.py:315
  22.4 18.9 %collective-permute-start.4 = (f32[32,16,128]{2,1,0:T(8,128)S(1)}, f32[32,16,128]{2,1,0:T(8,128)S(1)}, u32[]{:S(2)}, u32[]{:S(2)}) collective-permute-start(f32[32,16,128]{2,1,0:T(8,128)S(1)} %get-tuple-element.36), channel_id=1, source_target_pairs={{0,7},{1,6},{2,5},{3,4},{4,3},{5,2},{6,1},{7,0},{8,15},{9,14},{10,... | collective-permute-start | bytes 786440 | tf_op jit(solution)/shard_map/ppermute | solution.py:311
  44.2 2.1 %collective-permute-start.12 = (f32[4,72,128]{2,1,0:T(8,128)S(1)}, f32[4,72,128]{2,1,0:T(8,128)S(1)}, u32[]{:S(2)}, u32[]{:S(2)}) collective-permute-start(f32[4,72,128]{2,1,0:T(8,128)S(1)} %get-tuple-element.46), channel_id=1, source_target_pairs={{0,1},{1,0},{2,3},{3,2},{4,5},{5,4},{6,7},{7,6},{8,9},{9,8},{10,11... | collective-permute-start | bytes 442376 | tf_op jit(solution)/shard_map/ppermute | solution.py:346
  44.4 6.5 %collective-permute-start.13 = (f32[4,72,128]{2,1,0:T(8,128)S(1)}, f32[4,72,128]{2,1,0:T(8,128)S(1)}, u32[]{:S(2)}, u32[]{:S(2)}) collective-permute-start(f32[4,72,128]{2,1,0:T(8,128)S(1)} %get-tuple-element.47), channel_id=1, source_target_pairs={{1,2},{2,1},{3,4},{4,3},{5,6},{6,5},{9,10},{10,9},{11,12},{12,11},... | collective-permute-start | bytes 442376 | tf_op jit(solution)/shard_map/ppermute | solution.py:346
  50.9 6.6 %collective-permute-start.14 = (f32[320,128]{1,0:T(8,128)S(1)}, f32[320,128]{1,0:T(8,128)S(1)}, u32[]{:S(2)}, u32[]{:S(2)}) collective-permute-start(f32[320,128]{1,0:T(8,128)S(1)} %get-tuple-element.49), channel_id=1, source_target_pairs={{0,8},{8,0},{16,24},{24,16},{1,9},{9,1},{17,25},{25,17},{2,10},{10... | collective-permute-start | bytes 491528 | tf_op jit(solution)/shard_map/ppermute | solution.py:352
  51.0 10.7 %collective-permute-start.15 = (f32[320,128]{1,0:T(8,128)S(1)}, f32[320,128]{1,0:T(8,128)S(1)}, u32[]{:S(2)}, u32[]{:S(2)}) collective-permute-start(f32[320,128]{1,0:T(8,128)S(1)} %get-tuple-element.50), channel_id=1, source_target_pairs={{8,16},{16,8},{9,17},{17,9},{10,18},{18,10},{11,19},{19,11},{12,20... | collective-permute-start | bytes 491528 | tf_op jit(solution)/shard_map/ppermute | solution.py:352

commit v2 on v1

--- a/solution.py
+++ b/solution.py
@@ -47,22 +47,53 @@
     return lax.rem(lax.axis_index(axis), 2) == 1
 
 
-def prepare(turns, offsets, recorded, kept, mirrored, *rest):
-    sent, across = rest[:-1], rest[-1]
+def pick(turns, recorded, outer):
+    rows = recorded.shape[2]
+    half = outer.shape[1] // 2
+    outer[:, :half] = recorded[0, :, :half]
+    outer[:, half:] = recorded[0, :, rows - half :]
+
+
+def prepare(turns, offsets, recorded, kept, mine, theirs, across):
     depth, rows, lanes = recorded.shape[1:]
-    parts = len(sent)
+    chips, _, _, eight, wide = mine.shape
+    side = eight // 2
     me = lax.axis_index("gx")
     kept[...] = recorded[view_of(turns, 0)]
-    mirrored[...] = recorded[view_of(turns, 2)]
     for slot, turn in enumerate((1, 3)):
         view = view_of(turns, turn)
         volume = recorded[view].reshape(depth * rows, lanes)
         volume = pltpu.roll(volume, lax.rem(lanes - offsets[view], lanes), 1)
         across[...] = volume.T
-        for k in range(parts):
+        for k in range(2 * chips):
             to = lax.bitwise_xor(me, k)
-            part = parts - 1 - to if turn == 1 else to
-            sent[k][slot] = across[pl.ds(pl.multiple_of(part * rows, rows), rows)]
+            part = 2 * chips - 1 - to if turn == 1 else to
+            block = across[pl.ds(pl.multiple_of(part * rows, rows), rows)]
+            outer = jnp.concatenate([block[:side], block[rows - side :]], axis=0)
+            for chunk, value in enumerate((outer, block[side : rows - side])):
+                if k % 2 == 0:
+                    mine[k // 2, chunk, slot] = value
+                else:
+                    theirs[pl.ds((((k // 2) * 2 + chunk) * 2 + slot) * eight, eight)] = value
+    view = view_of(turns, 2)
+    fold = wide // lanes
+    run = depth // fold
+    for q in range(fold):
+        inner = recorded[view, q * run : (q + 1) * run, side : rows - side]
+        theirs[chips * 4 * eight :, q * lanes : (q + 1) * lanes] = inner.reshape(run * eight, lanes)
+
+
+def merge(mine, swapped, *outs):
+    chips, _, _, eight, _ = mine.shape
+    for chunk in range(2):
+        for k in range(1, chips):
+            out = outs[chunk * (chips - 1) + k - 1]
+            for slot in range(2):
+                out[slot * eight : (slot + 1) * eight] = mine[k, chunk, slot]
+            start = (k * 2 + chunk) * 2 * eight
+            out[2 * eight : 4 * eight] = swapped[start : start + 2 * eight]
+            if chunk == 1 and k == chips - 1:
+                out[4 * eight :] = swapped[chips * 4 * eight :]
 
 
 def edges(own, even_pair, odd_pair):
@@ -170,81 +201,131 @@
             predicted[turn, i] = dot(jnp.concatenate([t_high, t_low], axis=1), both) + dot(t_high, low)
 
 
-def project(turns, row_taps, column_taps, predicted, lane_back, depth_back, kept, mirrored, *rest):
-    received = rest[:-7]
-    middle, even_pair, odd_pair, arrived, data, backed, spread = rest[-7:]
-    _, rows, depth, lanes = predicted.shape
-    side = even_pair.shape[0]
-    deep = even_pair.shape[1]
-    width = 2 * side + 1
-    views = [view_of(turns, turn) for turn in range(VIEWS)]
-    parts = arrived.shape[0]
+def turned(chunk, mine, swapped, received, arrived, data):
+    parts, _, eight, wide = arrived.shape
+    depth = data.shape[2]
+    rows = wide // depth
     group = LANES // rows
-    granule = lax.broadcasted_iota(jnp.int32, (8, LANES), 1) // rows
-
     me = lax.axis_index("gx")
-    for k in range(parts):
-        arrived[lax.bitwise_xor(me, k)] = received[k][...]
-
+    for k in range(parts // 2):
+        for core in range(2):
+            source = lax.bitwise_xor(me, 2 * k + core)
+            for slot in range(2):
+                if k > 0:
+                    start = (core * 2 + slot) * eight
+                    value = received[k - 1][start : start + eight]
+                elif core == 0:
+                    value = mine[0, chunk, slot]
+                else:
+                    start = (chunk * 2 + slot) * eight
+                    value = swapped[start : start + eight]
+                arrived[source, slot] = value
+    granule = lax.broadcasted_iota(jnp.int32, (eight, LANES), 1) // rows
     for slot in range(2):
         for part in range(0, parts, group):
-            for eight in range(0, rows, 8):
-                for chunk in range(depth * rows // LANES):
-                    held = [
-                        arrived[part + s, slot, eight : eight + 8, chunk * LANES : (chunk + 1) * LANES]
-                        for s in range(group)
-                    ]
-                    step = 1
-                    while step < group:
-                        upper = (granule // step) % 2 == 1
-                        swapped = list(held)
-                        for s in range(group):
-                            if s & step == 0:
-                                one, two = held[s], held[s + step]
-                                swapped[s] = jnp.where(upper, pltpu.roll(two, step * rows, 1), one)
-                                swapped[s + step] = jnp.where(upper, two, pltpu.roll(one, LANES - step * rows, 1))
-                        held = swapped
-                        step *= 2
+            for piece in range(wide // LANES):
+                held = [arrived[part + s, slot, :, piece * LANES : (piece + 1) * LANES] for s in range(group)]
+                step = 1
+                while step < group:
+                    upper = (granule // step) % 2 == 1
+                    swapped_now = list(held)
                     for s in range(group):
-                        data[slot, eight : eight + 8, chunk * group + s, part * rows : part * rows + LANES] = held[s]
-
-    for turn, view in enumerate(views):
+                        if s & step == 0:
+                            one, two = held[s], held[s + step]
+                            swapped_now[s] = jnp.where(upper, pltpu.roll(two, step * rows, 1), one)
+                            swapped_now[s + step] = jnp.where(upper, two, pltpu.roll(one, LANES - step * rows, 1))
+                    held = swapped_now
+                    step *= 2
+                for s in range(group):
+                    data[slot, :, piece * group + s, part * rows : part * rows + LANES] = held[s]
+
+
+def ratios(row_list, half_turned, predicted, lane_back, kept, data, backed):
+    count = len(row_list)
+    for turn in range(VIEWS):
         high, low = lane_back[turn, 0], lane_back[turn, 1]
         both = jnp.concatenate([high, high], axis=0)
-        for i in range(rows):
-            there = rows - 1 - i if turn in (1, 2) else i
+        for j, i in enumerate(row_list):
+            there = count - 1 - j if turn in (1, 2) else j
             if turn == 0:
-                recorded = kept[:, there]
+                recorded = kept[:, i]
             elif turn == 2:
-                recorded = mirrored[:, there]
+                recorded = half_turned(there)
             else:
                 recorded = data[turn // 2, there]
             r_high, r_low = split(recorded / predicted[turn, i])
-            backed[turn, i] = dot(jnp.concatenate([r_high, r_low], axis=1), both) + dot(r_high, low)
-        factor = row_taps_of(turn, view, row_taps, column_taps, width)
-        for e in range(rows + 2 * side):
-            total = None
-            for i in range(max(0, e - 2 * side), min(rows, e + 1)):
-                term = factor[e - i] * backed[turn, i]
-                total = term if total is None else total + term
-            spread[e, turn * depth : (turn + 1) * depth] = total
-
+            backed[turn, j] = dot(jnp.concatenate([r_high, r_low], axis=1), both) + dot(r_high, low)
+
+
+def spread_row(e, turn, factor, row_list, side, backed):
+    total = None
+    for j, i in enumerate(row_list):
+        if 0 <= e - i <= 2 * side:
+            term = factor[e - i] * backed[turn, j]
+            total = term if total is None else total + term
+    return total
+
+
+def depth_blur(high, both, value):
+    s_high, s_low = split(value)
+    return dot(both, jnp.concatenate([s_high, s_high], axis=0)) + dot(high, s_low)
+
+
+def project_outer(turns, row_taps, column_taps, predicted, lane_back, depth_back, kept, mirrored, mine, swapped, *rest):
+    received, (even_pair, odd_pair, partial, arrived, data, backed) = rest[:-6], rest[-6:]
+    _, rows, depth, lanes = predicted.shape
+    side, deep, _ = even_pair.shape
+    row_list = [*range(side), *range(rows - side, rows)]
+    turned(0, mine, swapped, received, arrived, data)
+    ratios(row_list, lambda j: mirrored[:, j], predicted, lane_back, kept, data, backed)
+    factors = [
+        row_taps_of(turn, view_of(turns, turn), row_taps, column_taps, 2 * side + 1) for turn in range(VIEWS)
+    ]
     high, low = depth_back[0], depth_back[1]
     both = jnp.concatenate([high, low], axis=1)
     results = []
-    for e in range(rows + 2 * side):
-        s_high, s_low = split(spread[e])
-        result = dot(both, jnp.concatenate([s_high, s_high], axis=0)) + dot(high, s_low)
-        result = result[:deep]
-        if side <= e < side + rows:
-            middle[e - side] = result
-        else:
-            results.append(result)
+    for e in [*range(side), *range(rows + side, rows + 2 * side)]:
+        value = jnp.concatenate(
+            [spread_row(e, turn, factors[turn], row_list, side, backed) for turn in range(VIEWS)], axis=0
+        )
+        results.append(depth_blur(high, both, value)[:deep])
     odd = is_odd("gx")
     for i in range(side):
         first, last = results[i], results[side + i]
         even_pair[i] = jnp.where(odd, first, last)
         odd_pair[i] = jnp.where(odd, last, first)
+    for e in range(side, rows + side):
+        for turn in range(VIEWS):
+            total = spread_row(e, turn, factors[turn], row_list, side, backed)
+            partial[e - side, turn * depth : (turn + 1) * depth] = total
+
+
+def project_inner(turns, row_taps, column_taps, predicted, lane_back, depth_back, kept, partial, mine, swapped, *rest):
+    received, (middle, arrived, data, backed, inner) = rest[:-5], rest[-5:]
+    _, rows, depth, lanes = predicted.shape
+    deep = middle.shape[1]
+    _, _, eight, wide = arrived.shape
+    side = (rows - eight) // 2
+    row_list = [*range(side, rows - side)]
+    fold = wide // lanes
+    run = depth // fold
+
+    for q in range(fold):
+        block = received[-1][4 * eight :, q * lanes : (q + 1) * lanes]
+        inner[q * run : (q + 1) * run] = block.reshape(run, eight, lanes)
+
+    turned(1, mine, swapped, received, arrived, data)
+    ratios(row_list, lambda j: inner[:, j], predicted, lane_back, kept, data, backed)
+    factors = [
+        row_taps_of(turn, view_of(turns, turn), row_taps, column_taps, 2 * side + 1) for turn in range(VIEWS)
+    ]
+    high, low = depth_back[0], depth_back[1]
+    both = jnp.concatenate([high, low], axis=1)
+    for e in range(side, rows + side):
+        value = partial[e - side] + jnp.concatenate(
+            [spread_row(e, turn, factors[turn], row_list, side, backed) for turn in range(VIEWS)], axis=0
+        )
+        middle[e - side] = depth_blur(high, both, value)[:deep]
 
 
 def gather_sides(middle, even_x, odd_x, own, even_pair, odd_pair):
@@ -302,18 +383,43 @@
 
     first, second = call(edges, (struct(side, depth, lanes),) * 2, [VMEM])(estimate)
     first, second = lax.ppermute(first, "gx", even_x), lax.ppermute(second, "gx", odd_x)
-    kept, mirrored, *sent = call(
+    mirror = [(i, parts - 1 - i) for i in range(parts)]
+    outer = pl.pallas_call(
+        pick,
+        out_shape=struct(depth, 2 * side, lanes),
+        grid_spec=pltpu.PrefetchScalarGridSpec(
+            num_scalar_prefetch=1,
+            grid=(1,),
+            in_specs=[pl.BlockSpec((1, depth, rows, lanes), lambda i, turns: (view_of(turns, 2), 0, 0, 0))],
+            out_specs=pl.BlockSpec((depth, 2 * side, lanes), lambda i, turns: (0, 0, 0)),
+        ),
+        compiler_params=PARAMS,
+    )(quarter_turns, recorded)
+    outer = lax.ppermute(outer, "gx", mirror)
+    eight, wide, chips = rows // 2, depth * rows, parts // 2
+    extra = depth * eight * lanes // wide
+    kept, mine, theirs = call(
         prepare,
-        (struct(depth, rows, lanes),) * 2 + (struct(2, rows, depth * rows),) * parts,
+        (struct(depth, rows, lanes), struct(chips, 2, 2, eight, wide), struct(chips * 4 * eight + extra, wide)),
         [SMEM, SMEM, VMEM],
         [pltpu.VMEM((lanes, depth * rows), F32)],
     )(quarter_turns, offsets, recorded)
-    mirrored = lax.ppermute(mirrored, "gx", [(i, parts - 1 - i) for i in range(parts)])
+    swapped = lax.ppermute(theirs, "gx", [(i, i ^ 1) for i in range(parts)])
+    messages = call(
+        merge,
+        (struct(4 * eight, wide),) * (2 * chips - 3) + (struct(4 * eight + extra, wide),),
+        [VMEM] * 2,
+    )(mine, swapped)
     third, fourth = call(layers_out, (struct((rows + 2 * side) * reach, lanes),) * 2, [VMEM] * 3)(estimate, first, second)
     third, fourth = lax.ppermute(third, "gy", even_y), lax.ppermute(fourth, "gy", odd_y)
-    arrived = [sent[0]] + [
-        lax.ppermute(sent[k], "gx", [(i, i ^ k) for i in range(parts)]) for k in range(1, parts)
-    ]
+    order = [*range(chips - 1, 0, -1)]
+    moved = {
+        (chunk, k): lax.ppermute(
+            messages[chunk * (chips - 1) + k - 1], "gx", [(i, i ^ (2 * k)) for i in range(parts)]
+        )
+        for chunk in range(2)
+        for k in order
+    }
 
     predicted, lane_back, depth_back = call(
         predict,
@@ -330,20 +436,28 @@
         pl.CostEstimate(flops=4_000_000_000, bytes_accessed=4_000_000, transcendentals=0),
     )(quarter_turns, offsets, depth_taps, row_taps, column_taps, estimate, first, second, third, fourth)
 
-    middle, first, second = call(
-        project,
-        (struct(rows, deep, lanes), struct(side, deep, lanes), struct(side, deep, lanes)),
-        [SMEM] * 3 + [VMEM] * (5 + parts),
-        [
-            pltpu.VMEM((parts, 2, rows, depth * rows), F32),
-            pltpu.VMEM((2, rows, depth, lanes), F32),
-            pltpu.VMEM((VIEWS, rows, depth, lanes), F32),
-            pltpu.VMEM((rows + 2 * side, VIEWS * depth, lanes), F32),
-        ],
-        pl.CostEstimate(flops=4_000_000_000, bytes_accessed=4_000_000, transcendentals=0),
-    )(quarter_turns, row_taps, column_taps, predicted, lane_back, depth_back, kept, mirrored, *arrived)
-
+    scratch = [
+        pltpu.VMEM((parts, 2, eight, wide), F32),
+        pltpu.VMEM((2, eight, depth, lanes), F32),
+        pltpu.VMEM((VIEWS, eight, depth, lanes), F32),
+    ]
+    first, second, partial = call(
+        project_outer,
+        (struct(side, deep, lanes),) * 2 + (struct(rows, VIEWS * depth, lanes),),
+        [SMEM] * 3 + [VMEM] * (6 + chips),
+        scratch,
+        pl.CostEstimate(flops=2_000_000_000, bytes_accessed=4_000_000, transcendentals=0),
+    )(quarter_turns, row_taps, column_taps, predicted, lane_back, depth_back, kept, outer, mine, swapped,
+      *[moved[0, k] for k in range(1, chips)])
     first, second = lax.ppermute(first, "gx", even_x), lax.ppermute(second, "gx", odd_x)
+    middle = call(
+        project_inner,
+        struct(rows, deep, lanes),
+        [SMEM] * 3 + [VMEM] * (6 + chips),
+        [*scratch, pltpu.VMEM((depth, eight, lanes), F32)],
+        pl.CostEstimate(flops=2_000_000_000, bytes_accessed=4_000_000, transcendentals=0),
+    )(quarter_turns, row_taps, column_taps, predicted, lane_back, depth_back, kept, partial, mine, swapped,
+      *[moved[1, k] for k in range(1, chips)])
     own, third, fourth = call(
         gather_sides,
         (struct(rows, depth, lanes), struct(rows * reach, lanes), struct(rows * reach, lanes)),

time: 63.2 us -> 54.4 us (0.86)
  the two profiles are of different devices: /device:TPU:12 before, /device:TPU:4 now
where the time goes in v2:
time: 54.4 us; the launch traced here: 54.2 us
  starting transfers between devices  29 us (53%)
  waiting for transfers between devices  11.8 us (22%)
  Pallas kernels  9.63 us (18%)
  local copies, waits for them, and re-layouts  3.51 us (6%)
    ppermute x6, starting transfers between devices, shards(): lax.ppermute(messages[chunk * (chips - 1) + k - 1], 'gx', [(i, i ^ 2 * k)...  15.5 us
    ppermute x2, starting transfers between devices, shards(): lax.ppermute(fourth, 'gy', odd_y)  6.26 us
    ppermute x6, waiting for transfers between devices, shards(): lax.ppermute(messages[chunk * (chips - 1) + k - 1], 'gx', [(i, i ^ 2 * k)...  5.72 us
    ppermute x2, waiting for transfers between devices, shards(): lax.ppermute(fourth, 'gy', odd_y)  4.22 us
    ppermute x1, starting transfers between devices, shards(): outer = lax.ppermute(outer, 'gx', mirror)  3.53 us
    unnamed x22, local copies, waits for them, and re-layouts  3.51 us
    pallas_call x1, Pallas kernels, shards(): call(predict, (struct(VIEWS, rows, depth, lanes), struct(VIEWS, 2, lanes,...  2.84 us
    pallas_call x1, Pallas kernels, shards(): call(project_inner, struct(rows, deep, lanes), [SMEM] * 3 + [VMEM] * (6 +...  1.93 us
  transfers between devices with their start and end apart: 16, of which 4 were waited for; matrix products, arithmetic and copies ran while one was open for 0% of the time, Pallas kernels for 14%

profile of v2, /device:TPU:4, one launch (start us, length us, event | category | flops | bytes accessed | tf_op | source)
XLA Modules:
  0.0 54.2 jit_solution(12746480864368739964)
XLA Ops:
  0.0 0.0 copy-start
  0.0 1.2 %copy-done = f32[4,32,16,128]{3,2,1,0:T(8,128)S(1)} copy-done((f32[4,32,16,128]{3,2,1,0:T(8,128)S(1)}, f32[4,32,16,128]{3,2,1,0:T(8,128)}, u32[]{:S(2)}) %copy-start) | copy-done | bytes 1048600
  1.2 0.0 copy-start.4
  1.2 0.7 %copy-done.4 = s32[4]{0:T(128)S(1)} copy-done((s32[4]{0:T(128)S(1)}, s32[4]{0:T(128)}, u32[]{:S(2)}) %copy-start.4) | copy-done | bytes 40
  1.9 0.0 copy-start.6
  1.9 0.7 %copy-done.6 = s32[4]{0:T(128)S(1)} copy-done((s32[4]{0:T(128)S(1)}, s32[4]{0:T(128)}, u32[]{:S(2)}) %copy-start.6) | copy-done | bytes 40
  2.5 0.0 copy-start.1
  2.5 0.9 %shard_map.76 = (f32[32,16,128]{2,1,0:T(8,128)S(1)}, f32[4,2,2,8,512]{4,3,2,1,0:T(8,128)S(1)}, f32[192,512]{1,0:T(8,128)S(1)}) custom-call(s32[4]{0:T(128)S(1)} %copy-done.4, s32[4]{0:T(128)S(1)} %copy-done.6, f32[4,32,16,128]{3,2,1,0:T(8,128)S(1)} %copy-done), custom_call_target="tpu_custom_call" | custom-call | tf_op jit(solution)/shard_map/pallas_call | solution.py:401
  3.5 0.1 collective-permute-start.5
  3.6 0.0 copy-start.2
  3.6 0.9 %copy-done.2 = f32[32,16,128]{2,1,0:T(8,128)S(1)} copy-done((f32[32,16,128]{2,1,0:T(8,128)S(1)}, f32[32,16,128]{2,1,0:T(8,128)}, u32[]{:S(2)}) %copy-start.2) | copy-done | bytes 262168
  4.5 0.1 shard_map.73
  4.6 0.6 %collective-permute-start = (f32[4,32,128]{2,1,0:T(8,128)S(1)}, f32[4,32,128]{2,1,0:T(8,128)S(1)}, u32[]{:S(2)}, u32[]{:S(2)}) collective-permute-start(f32[4,32,128]{2,1,0:T(8,128)S(1)} %get-tuple-element.27), channel_id=1, source_target_pairs={{0,1},{1,0},{2,3},{3,2},{4,5},{5,4},{6,7},{7,6},{8,9},{9,8},{10,11... | collective-permute-start | bytes 196616 | tf_op jit(solution)/shard_map/ppermute | solution.py:385
  5.2 0.7 %collective-permute-start.1 = (f32[4,32,128]{2,1,0:T(8,128)S(1)}, f32[4,32,128]{2,1,0:T(8,128)S(1)}, u32[]{:S(2)}, u32[]{:S(2)}) collective-permute-start(f32[4,32,128]{2,1,0:T(8,128)S(1)} %get-tuple-element.28), channel_id=1, source_target_pairs={{1,2},{2,1},{3,4},{4,3},{5,6},{6,5},{9,10},{10,9},{11,12},{12,11},... | collective-permute-start | bytes 196616 | tf_op jit(solution)/shard_map/ppermute | solution.py:385
  5.9 0.2 collective-permute-done.from_even.even_x
  6.1 0.0 collective-permute-done.1.from_odd.odd_x
  6.1 0.3 shard_map.74
  6.4 0.0 copy-start.5
  6.4 1.6 %collective-permute-start.2 = (f32[480,128]{1,0:T(8,128)S(1)}, f32[480,128]{1,0:T(8,128)S(1)}, u32[]{:S(2)}, u32[]{:S(2)}) collective-permute-start(f32[480,128]{1,0:T(8,128)S(1)} %get-tuple-element.29), channel_id=1, source_target_pairs={{0,8},{8,0},{16,24},{24,16},{1,9},{9,1},{17,25},{25,17},{2,10},{10... | collective-permute-start | bytes 737288 | tf_op jit(solution)/shard_map/ppermute | solution.py:414
  7.9 1.9 %collective-permute-start.3 = (f32[480,128]{1,0:T(8,128)S(1)}, f32[480,128]{1,0:T(8,128)S(1)}, u32[]{:S(2)}, u32[]{:S(2)}) collective-permute-start(f32[480,128]{1,0:T(8,128)S(1)} %get-tuple-element.30), channel_id=1, source_target_pairs={{8,16},{16,8},{9,17},{17,9},{10,18},{18,10},{11,19},{19,11},{12,20... | collective-permute-start | bytes 737288 | tf_op jit(solution)/shard_map/ppermute | solution.py:414
  9.8 0.0 copy-done.1
  9.9 0.0 copy-done.5
  9.9 0.6 %shard_map.77 = f32[32,8,128]{2,1,0:T(8,128)S(1)} custom-call(s32[4]{0:T(128)S(1)} %copy-done.5, f32[4,32,16,128]{3,2,1,0:T(8,128)S(1)} %copy-done.1), custom_call_target="tpu_custom_call" | custom-call | tf_op jit(solution)/shard_map/pallas_call | solution.py:387
  10.4 3.5 %collective-permute-start.4 = (f32[32,8,128]{2,1,0:T(8,128)S(1)}, f32[32,8,128]{2,1,0:T(8,128)S(1)}, u32[]{:S(2)}, u32[]{:S(2)}) collective-permute-start(f32[32,8,128]{2,1,0:T(8,128)S(1)} %shard_map.77), channel_id=1, source_target_pairs={{0,7},{1,6},{2,5},{3,4},{4,3},{5,2},{6,1},{7,0},{8,15},{9,14},{10,... | collective-permute-start | bytes 393224 | tf_op jit(solution)/shard_map/ppermute | solution.py:398
  14.0 0.0 collective-permute-done.5.swapped
  14.0 0.0 copy-start.3
  14.0 0.0 copy-start.10
  14.0 4.0 %collective-permute-start.6 = (f32[32,512]{1,0:T(8,128)S(1)}, f32[32,512]{1,0:T(8,128)S(1)}, u32[]{:S(2)}, u32[]{:S(2)}) collective-permute-start(f32[32,512]{1,0:T(8,128)S(1)} %get-tuple-element.37), channel_id=1, source_target_pairs={{0,2},{1,3},{2,0},{3,1},{4,6},{5,7},{6,4},{7,5},{8,10},{9,11},{10,... | collective-permute-start | bytes 196616 | tf_op jit(solution)/shard_map/ppermute | solution.py:417
  18.1 0.0 copy-start.9
  18.1 0.0 copy-start.8
  18.1 1.9 %collective-permute-start.7 = (f32[32,512]{1,0:T(8,128)S(1)}, f32[32,512]{1,0:T(8,128)S(1)}, u32[]{:S(2)}, u32[]{:S(2)}) collective-permute-start(f32[32,512]{1,0:T(8,128)S(1)} %get-tuple-element.38), channel_id=1, source_target_pairs={{0,4},{1,5},{2,6},{3,7},{4,0},{5,1},{6,2},{7,3},{8,12},{9,13},{10,... | collective-permute-start | bytes 196616 | tf_op jit(solution)/shard_map/ppermute | solution.py:417
  20.0 0.0 collective-permute-done.2.even_y
  20.0 0.0 copy-start.7
  20.0 0.9 %collective-permute-start.8 = (f32[32,512]{1,0:T(8,128)S(1)}, f32[32,512]{1,0:T(8,128)S(1)}, u32[]{:S(2)}, u32[]{:S(2)}) collective-permute-start(f32[32,512]{1,0:T(8,128)S(1)} %get-tuple-element.39), channel_id=1, source_target_pairs={{0,6},{1,7},{2,4},{3,5},{4,2},{5,3},{6,0},{7,1},{8,14},{9,15},{10,... | collective-permute-start | bytes 196616 | tf_op jit(solution)/shard_map/ppermute | solution.py:417
  20.9 0.0 collective-permute-done.3.odd_y
  20.9 4.3 %collective-permute-start.11 = (f32[96,512]{1,0:T(8,128)S(1)}, f32[96,512]{1,0:T(8,128)S(1)}, u32[]{:S(2)}, u32[]{:S(2)}) collective-permute-start(f32[96,512]{1,0:T(8,128)S(1)} %get-tuple-element.43), channel_id=1, source_target_pairs={{0,6},{1,7},{2,4},{3,5},{4,2},{5,3},{6,0},{7,1},{8,14},{9,15},{10,... | collective-permute-start | bytes 589832 | tf_op jit(solution)/shard_map/ppermute | solution.py:417
  25.2 0.0 copy-done.3
  25.2 0.0 copy-done.10
  25.2 0.0 copy-done.9
  25.2 0.0 copy-done.8
  25.2 0.0 copy-done.7
  25.2 2.8 %shard_map.75 = (f32[4,16,32,128]{3,2,1,0:T(8,128)S(1)}, bf16[4,2,128,128]{3,2,1,0:T(8,128)(2,1)S(1)}, bf16[2,80,128]{2,1,0:T(8,128)(2,1)S(1)}) custom-call(s32[4]{0:T(128)S(1)} %copy-done.5, s32[4]{0:T(128)S(1)} %copy-done.7, f32[4,41]{1,0:T(4,128)S(1)} %copy-done.8, f32[4,9]{1,0:T(4,128)S(1)} %copy-done.9, f32[4,9]{1,0:T(4,128)S(1)} %copy-done.10, ...), custom_call_target="tpu_custom_call" | custom-call | flops 4000000000 | bytes 4000000 | tf_op jit(solution)/shard_map/pallas_call | solution.py:424
  28.1 0.0 collective-permute-done.4.mirrored
  28.1 2.3 %collective-permute-start.9 = (f32[32,512]{1,0:T(8,128)S(1)}, f32[32,512]{1,0:T(8,128)S(1)}, u32[]{:S(2)}, u32[]{:S(2)}) collective-permute-start(f32[32,512]{1,0:T(8,128)S(1)} %get-tuple-element.41), channel_id=1, source_target_pairs={{0,2},{1,3},{2,0},{3,1},{4,6},{5,7},{6,4},{7,5},{8,10},{9,11},{10,... | collective-permute-start | bytes 196616 | tf_op jit(solution)/shard_map/ppermute | solution.py:417
  30.4 0.0 collective-permute-done.6.rest_0_
  30.4 2.0 %collective-permute-start.10 = (f32[32,512]{1,0:T(8,128)S(1)}, f32[32,512]{1,0:T(8,128)S(1)}, u32[]{:S(2)}, u32[]{:S(2)}) collective-permute-start(f32[32,512]{1,0:T(8,128)S(1)} %get-tuple-element.42), channel_id=1, source_target_pairs={{0,4},{1,5},{2,6},{3,7},{4,0},{5,1},{6,2},{7,3},{8,12},{9,13},{10,... | collective-permute-start | bytes 196616 | tf_op jit(solution)/shard_map/ppermute | solution.py:417
  32.5 0.0 collective-permute-done.7.rest_1_
  32.5 0.0 collective-permute-done.8.rest_2_
  32.5 1.8 %shard_map.79 = (f32[4,72,128]{2,1,0:T(8,128)S(1)}, f32[4,72,128]{2,1,0:T(8,128)S(1)}, f32[16,128,128]{2,1,0:T(8,128)S(1)}) custom-call(s32[4]{0:T(128)S(1)} %copy-done.5, f32[4,9]{1,0:T(4,128)S(1)} %copy-done.9, f32[4,9]{1,0:T(4,128)S(1)} %copy-done.10, f32[4,16,32,128]{3,2,1,0:T(8,128)S(1)} %get-tuple-element.31.predicted, ...), custom_call_target="tpu_custom_call" | custom-call | flops 2000000000 | bytes 4000000 | tf_op jit(solution)/shard_map/pallas_call | solution.py:444
  34.3 0.1 collective-permute-start.12
  34.4 0.7 %collective-permute-start.13 = (f32[4,72,128]{2,1,0:T(8,128)S(1)}, f32[4,72,128]{2,1,0:T(8,128)S(1)}, u32[]{:S(2)}, u32[]{:S(2)}) collective-permute-start(f32[4,72,128]{2,1,0:T(8,128)S(1)} %get-tuple-element.45), channel_id=1, source_target_pairs={{1,2},{2,1},{3,4},{4,3},{5,6},{6,5},{9,10},{10,9},{11,12},{12,11},... | collective-permute-start | bytes 442376 | tf_op jit(solution)/shard_map/ppermute | solution.py:452
  35.1 0.0 collective-permute-done.9.rest_0_
  35.1 5.7 %collective-permute-done.10.rest_1_ = f32[32,512]{1,0:T(8,128)S(1)} collective-permute-done((f32[32,512]{1,0:T(8,128)S(1)}, f32[32,512]{1,0:T(8,128)S(1)}, u32[]{:S(2)}, u32[]{:S(2)}) %collective-permute-start.10) | collective-permute-done | bytes 65568 | tf_op jit(solution)/shard_map/ppermute | solution.py:417
  40.8 0.0 collective-permute-done.11.rest_2_
  40.8 1.9 %shard_map.80.middle = f32[16,72,128]{2,1,0:T(8,128)S(1)} custom-call(s32[4]{0:T(128)S(1)} %copy-done.5, f32[4,9]{1,0:T(4,128)S(1)} %copy-done.9, f32[4,9]{1,0:T(4,128)S(1)} %copy-done.10, f32[4,16,32,128]{3,2,1,0:T(8,128)S(1)} %get-tuple-element.31.predicted, bf16[4,2,128,128]{3,2,1,0:T(8,128)(2,1)S(1)} %get-tuple-element.32.lane_back, ...), custom_call_target="tpu_custom_call" | custom-call | flops 2000000000 | bytes 4000000 | tf_op jit(solution)/shard_map/pallas_call | solution.py:453
  42.7 0.0 collective-permute-done.12.even_x
  42.7 0.0 collective-permute-done.13.odd_x
  42.7 0.1 shard_map.81
  42.8 0.1 collective-permute-start.14
  42.9 4.4 %collective-permute-start.15 = (f32[320,128]{1,0:T(8,128)S(1)}, f32[320,128]{1,0:T(8,128)S(1)}, u32[]{:S(2)}, u32[]{:S(2)}) collective-permute-start(f32[320,128]{1,0:T(8,128)S(1)} %get-tuple-element.48), channel_id=1, source_target_pairs={{8,16},{16,8},{9,17},{17,9},{10,18},{18,10},{11,19},{19,11},{12,20... | collective-permute-start | bytes 491528 | tf_op jit(solution)/shard_map/ppermute | solution.py:466
  47.3 1.6 %collective-permute-done.14.even_y = f32[320,128]{1,0:T(8,128)S(1)} collective-permute-done((f32[320,128]{1,0:T(8,128)S(1)}, f32[320,128]{1,0:T(8,128)S(1)}, u32[]{:S(2)}, u32[]{:S(2)}) %collective-permute-start.14) | collective-permute-done | bytes 163872 | tf_op jit(solution)/shard_map/ppermute | solution.py:466
  48.9 4.2 %collective-permute-done.15.odd_y = f32[320,128]{1,0:T(8,128)S(1)} collective-permute-done((f32[320,128]{1,0:T(8,128)S(1)}, f32[320,128]{1,0:T(8,128)S(1)}, u32[]{:S(2)}, u32[]{:S(2)}) %collective-permute-start.15) | collective-permute-done | bytes 163872 | tf_op jit(solution)/shard_map/ppermute | solution.py:466
  53.1 1.0 %shard_map.82 = f32[32,16,128]{2,1,0:T(8,128)} custom-call(f32[32,16,128]{2,1,0:T(8,128)S(1)} %copy-done.3, f32[16,32,128]{2,1,0:T(8,128)S(1)} %get-tuple-element.46.own, f32[320,128]{1,0:T(8,128)S(1)} %collective-permute-done.14.even_y, f32[320,128]{1,0:T(8,128)S(1)} %collective-permute-done.15.odd_y), custom_call_target="tpu_custom_call" | custom-call | tf_op jit(solution)/shard_map/pallas_call | solution.py:467
  (1 shorter events, 0.0 us)
Async XLA Ops:
  0.0 1.2 %copy-start = (f32[4,32,16,128]{3,2,1,0:T(8,128)S(1)}, f32[4,32,16,128]{3,2,1,0:T(8,128)}, u32[]{:S(2)}) copy-start(f32[4,32,16,128]{3,2,1,0:T(8,128)} %recorded.3) | copy-start | bytes 3145732
  1.2 0.7 %copy-start.4 = (s32[4]{0:T(128)S(1)}, s32[4]{0:T(128)}, u32[]{:S(2)}) copy-start(s32[4]{0:T(128)} %turns.9) | copy-start | bytes 52
  1.9 0.7 %copy-start.6 = (s32[4]{0:T(128)S(1)}, s32[4]{0:T(128)}, u32[]{:S(2)}) copy-start(s32[4]{0:T(128)} %offsets.3) | copy-start | bytes 52
  2.5 7.3 %copy-start.1 = (f32[4,32,16,128]{3,2,1,0:T(8,128)S(1)}, f32[4,32,16,128]{3,2,1,0:T(8,128)}, u32[]{:S(2)}) copy-start(f32[4,32,16,128]{3,2,1,0:T(8,128)} %recorded.3) | copy-start | bytes 3145732
  3.5 10.5 %collective-permute-start.5 = (f32[192,512]{1,0:T(8,128)S(1)}, f32[192,512]{1,0:T(8,128)S(1)}, u32[]{:S(2)}, u32[]{:S(2)}) collective-permute-start(f32[192,512]{1,0:T(8,128)S(1)} %get-tuple-element.36), channel_id=1, source_target_pairs={{0,1},{1,0},{2,3},{3,2},{4,5},{5,4},{6,7},{7,6},{8,9},{9,8},{10,11... | collective-permute-start | bytes 1179656 | tf_op jit(solution)/shard_map/ppermute | solution.py:407
  3.6 1.0 %copy-start.2 = (f32[32,16,128]{2,1,0:T(8,128)S(1)}, f32[32,16,128]{2,1,0:T(8,128)}, u32[]{:S(2)}) copy-start(f32[32,16,128]{2,1,0:T(8,128)} %estimate.1) | copy-start | bytes 786436
  4.6 1.5 %collective-permute-start = (f32[4,32,128]{2,1,0:T(8,128)S(1)}, f32[4,32,128]{2,1,0:T(8,128)S(1)}, u32[]{:S(2)}, u32[]{:S(2)}) collective-permute-start(f32[4,32,128]{2,1,0:T(8,128)S(1)} %get-tuple-element.27), channel_id=1, source_target_pairs={{0,1},{1,0},{2,3},{3,2},{4,5},{5,4},{6,7},{7,6},{8,9},{9,8},{10,11... | collective-permute-start | bytes 196616 | tf_op jit(solution)/shard_map/ppermute | solution.py:385
  5.2 0.9 %collective-permute-start.1 = (f32[4,32,128]{2,1,0:T(8,128)S(1)}, f32[4,32,128]{2,1,0:T(8,128)S(1)}, u32[]{:S(2)}, u32[]{:S(2)}) collective-permute-start(f32[4,32,128]{2,1,0:T(8,128)S(1)} %get-tuple-element.28), channel_id=1, source_target_pairs={{1,2},{2,1},{3,4},{4,3},{5,6},{6,5},{9,10},{10,9},{11,12},{12,11},... | collective-permute-start | bytes 196616 | tf_op jit(solution)/shard_map/ppermute | solution.py:385
  6.4 3.5 %copy-start.5 = (s32[4]{0:T(128)S(1)}, s32[4]{0:T(128)}, u32[]{:S(2)}) copy-start(s32[4]{0:T(128)} %turns.9) | copy-start | bytes 52
  6.4 13.6 %collective-permute-start.2 = (f32[480,128]{1,0:T(8,128)S(1)}, f32[480,128]{1,0:T(8,128)S(1)}, u32[]{:S(2)}, u32[]{:S(2)}) collective-permute-start(f32[480,128]{1,0:T(8,128)S(1)} %get-tuple-element.29), channel_id=1, source_target_pairs={{0,8},{8,0},{16,24},{24,16},{1,9},{9,1},{17,25},{25,17},{2,10},{10... | collective-permute-start | bytes 737288 | tf_op jit(solution)/shard_map/ppermute | solution.py:414
  7.9 13.0 %collective-permute-start.3 = (f32[480,128]{1,0:T(8,128)S(1)}, f32[480,128]{1,0:T(8,128)S(1)}, u32[]{:S(2)}, u32[]{:S(2)}) collective-permute-start(f32[480,128]{1,0:T(8,128)S(1)} %get-tuple-element.30), channel_id=1, source_target_pairs={{8,16},{16,8},{9,17},{17,9},{10,18},{18,10},{11,19},{19,11},{12,20... | collective-permute-start | bytes 737288 | tf_op jit(solution)/shard_map/ppermute | solution.py:414
  10.4 17.6 %collective-permute-start.4 = (f32[32,8,128]{2,1,0:T(8,128)S(1)}, f32[32,8,128]{2,1,0:T(8,128)S(1)}, u32[]{:S(2)}, u32[]{:S(2)}) collective-permute-start(f32[32,8,128]{2,1,0:T(8,128)S(1)} %shard_map.77), channel_id=1, source_target_pairs={{0,7},{1,6},{2,5},{3,4},{4,3},{5,2},{6,1},{7,0},{8,15},{9,14},{10,... | collective-permute-start | bytes 393224 | tf_op jit(solution)/shard_map/ppermute | solution.py:398
  14.0 11.2 %copy-start.3 = (f32[32,16,128]{2,1,0:T(8,128)S(1)}, f32[32,16,128]{2,1,0:T(8,128)}, u32[]{:S(2)}) copy-start(f32[32,16,128]{2,1,0:T(8,128)} %estimate.1) | copy-start | bytes 786436
  14.0 11.2 %copy-start.10 = (f32[4,9]{1,0:T(4,128)S(1)}, f32[4,9]{1,0:T(4,128)}, u32[]{:S(2)}) copy-start(f32[4,9]{1,0:T(4,128)} %column_taps.5) | copy-start | bytes 436
  14.0 16.4 %collective-permute-start.6 = (f32[32,512]{1,0:T(8,128)S(1)}, f32[32,512]{1,0:T(8,128)S(1)}, u32[]{:S(2)}, u32[]{:S(2)}) collective-permute-start(f32[32,512]{1,0:T(8,128)S(1)} %get-tuple-element.37), channel_id=1, source_target_pairs={{0,2},{1,3},{2,0},{3,1},{4,6},{5,7},{6,4},{7,5},{8,10},{9,11},{10,... | collective-permute-start | bytes 196616 | tf_op jit(solution)/shard_map/ppermute | solution.py:417
  18.1 7.1 %copy-start.9 = (f32[4,9]{1,0:T(4,128)S(1)}, f32[4,9]{1,0:T(4,128)}, u32[]{:S(2)}) copy-start(f32[4,9]{1,0:T(4,128)} %row_taps.5) | copy-start | bytes 436
  18.1 7.1 %copy-start.8 = (f32[4,41]{1,0:T(4,128)S(1)}, f32[4,41]{1,0:T(4,128)}, u32[]{:S(2)}) copy-start(f32[4,41]{1,0:T(4,128)} %depth_taps.1) | copy-start | bytes 1972
  18.1 14.4 %collective-permute-start.7 = (f32[32,512]{1,0:T(8,128)S(1)}, f32[32,512]{1,0:T(8,128)S(1)}, u32[]{:S(2)}, u32[]{:S(2)}) collective-permute-start(f32[32,512]{1,0:T(8,128)S(1)} %get-tuple-element.38), channel_id=1, source_target_pairs={{0,4},{1,5},{2,6},{3,7},{4,0},{5,1},{6,2},{7,3},{8,12},{9,13},{10,... | collective-permute-start | bytes 196616 | tf_op jit(solution)/shard_map/ppermute | solution.py:417
  20.0 5.2 %copy-start.7 = (s32[4]{0:T(128)S(1)}, s32[4]{0:T(128)}, u32[]{:S(2)}) copy-start(s32[4]{0:T(128)} %offsets.3) | copy-start | bytes 52
  20.0 12.5 %collective-permute-start.8 = (f32[32,512]{1,0:T(8,128)S(1)}, f32[32,512]{1,0:T(8,128)S(1)}, u32[]{:S(2)}, u32[]{:S(2)}) collective-permute-start(f32[32,512]{1,0:T(8,128)S(1)} %get-tuple-element.39), channel_id=1, source_target_pairs={{0,6},{1,7},{2,4},{3,5},{4,2},{5,3},{6,0},{7,1},{8,14},{9,15},{10,... | collective-permute-start | bytes 196616 | tf_op jit(solution)/shard_map/ppermute | solution.py:417
  20.9 19.9 %collective-permute-start.11 = (f32[96,512]{1,0:T(8,128)S(1)}, f32[96,512]{1,0:T(8,128)S(1)}, u32[]{:S(2)}, u32[]{:S(2)}) collective-permute-start(f32[96,512]{1,0:T(8,128)S(1)} %get-tuple-element.43), channel_id=1, source_target_pairs={{0,6},{1,7},{2,4},{3,5},{4,2},{5,3},{6,0},{7,1},{8,14},{9,15},{10,... | collective-permute-start | bytes 589832 | tf_op jit(solution)/shard_map/ppermute | solution.py:417
  28.1 7.0 %collective-permute-start.9 = (f32[32,512]{1,0:T(8,128)S(1)}, f32[32,512]{1,0:T(8,128)S(1)}, u32[]{:S(2)}, u32[]{:S(2)}) collective-permute-start(f32[32,512]{1,0:T(8,128)S(1)} %get-tuple-element.41), channel_id=1, source_target_pairs={{0,2},{1,3},{2,0},{3,1},{4,6},{5,7},{6,4},{7,5},{8,10},{9,11},{10,... | collective-permute-start | bytes 196616 | tf_op jit(solution)/shard_map/ppermute | solution.py:417
  30.4 10.4 %collective-permute-start.10 = (f32[32,512]{1,0:T(8,128)S(1)}, f32[32,512]{1,0:T(8,128)S(1)}, u32[]{:S(2)}, u32[]{:S(2)}) collective-permute-start(f32[32,512]{1,0:T(8,128)S(1)} %get-tuple-element.42), channel_id=1, source_target_pairs={{0,4},{1,5},{2,6},{3,7},{4,0},{5,1},{6,2},{7,3},{8,12},{9,13},{10,... | collective-permute-start | bytes 196616 | tf_op jit(solution)/shard_map/ppermute | solution.py:417
  34.3 8.4 %collective-permute-start.12 = (f32[4,72,128]{2,1,0:T(8,128)S(1)}, f32[4,72,128]{2,1,0:T(8,128)S(1)}, u32[]{:S(2)}, u32[]{:S(2)}) collective-permute-start(f32[4,72,128]{2,1,0:T(8,128)S(1)} %get-tuple-element.44), channel_id=1, source_target_pairs={{0,1},{1,0},{2,3},{3,2},{4,5},{5,4},{6,7},{7,6},{8,9},{9,8},{10,11... | collective-permute-start | bytes 442376 | tf_op jit(solution)/shard_map/ppermute | solution.py:452
  34.4 8.3 %collective-permute-start.13 = (f32[4,72,128]{2,1,0:T(8,128)S(1)}, f32[4,72,128]{2,1,0:T(8,128)S(1)}, u32[]{:S(2)}, u32[]{:S(2)}) collective-permute-start(f32[4,72,128]{2,1,0:T(8,128)S(1)} %get-tuple-element.45), channel_id=1, source_target_pairs={{1,2},{2,1},{3,4},{4,3},{5,6},{6,5},{9,10},{10,9},{11,12},{12,11},... | collective-permute-start | bytes 442376 | tf_op jit(solution)/shard_map/ppermute | solution.py:452
  42.8 6.1 %collective-permute-start.14 = (f32[320,128]{1,0:T(8,128)S(1)}, f32[320,128]{1,0:T(8,128)S(1)}, u32[]{:S(2)}, u32[]{:S(2)}) collective-permute-start(f32[320,128]{1,0:T(8,128)S(1)} %get-tuple-element.47), channel_id=1, source_target_pairs={{0,8},{8,0},{16,24},{24,16},{1,9},{9,1},{17,25},{25,17},{2,10},{10... | collective-permute-start | bytes 491528 | tf_op jit(solution)/shard_map/ppermute | solution.py:466
  42.9 10.2 %collective-permute-start.15 = (f32[320,128]{1,0:T(8,128)S(1)}, f32[320,128]{1,0:T(8,128)S(1)}, u32[]{:S(2)}, u32[]{:S(2)}) collective-permute-start(f32[320,128]{1,0:T(8,128)S(1)} %get-tuple-element.48), channel_id=1, source_target_pairs={{8,16},{16,8},{9,17},{17,9},{10,18},{18,10},{11,19},{19,11},{12,20... | collective-permute-start | bytes 491528 | tf_op jit(solution)/shard_map/ppermute | solution.py:466

commit v3 on v1

v3 whole, which is shorter than its diff:
```python
import functools

import jax
import jax.numpy as jnp
from jax import lax
from jax.experimental import pallas as pl
from jax.experimental.pallas import tpu as pltpu
from jax.sharding import PartitionSpec as P

VIEWS = 4
LANES = 128
VMEM = pl.BlockSpec(memory_space=pltpu.VMEM)
ORDER = pl.BlockSpec(memory_space=pl.ANY)
SMEM = pl.BlockSpec(memory_space=pltpu.SMEM)
PARAMS = pltpu.CompilerParams(vmem_limit_bytes=24 * 1024 * 1024)
F32 = jnp.float32
BF16 = jnp.bfloat16
COST = pl.CostEstimate(flops=1, bytes_accessed=1, transcendentals=0)


def struct(*shape, dtype=F32):
    return jax.ShapeDtypeStruct(shape, dtype)


def view_of(turns_ref, turn):
    found = jnp.int32(0)
    for view in range(1, VIEWS):
        found = jnp.where(turns_ref[view] == turn, jnp.int32(view), found)
    return found


def split(value):
    high = value.astype(BF16)
    return high, (value - high.astype(F32)).astype(BF16)


def dot(left, right):
    return jnp.dot(left, right, preferred_element_type=F32)


def pairs(width):
    def swaps(initial):
        return [p for i in range(initial, width - 1, 2) for p in ((i, i + 1), (i + 1, i))]

    return swaps(0), swaps(1)


def is_odd(axis):
    return lax.rem(lax.axis_index(axis), 2) == 1


def pick(turns, recorded, later, outer, inner):
    rows = recorded.shape[2]
    half = outer.shape[1] // 2
    outer[:, :half] = recorded[0, :, :half]
    outer[:, half:] = recorded[0, :, rows - half :]
    inner[...] = recorded[0, :, half : rows - half]


def prepare(turns, offsets, recorded, later, kept, mine, theirs, across):
    depth, rows, lanes = recorded.shape[1:]
    chips, _, _, wide = mine.shape
    me = lax.axis_index("gx")
    kept[...] = recorded[view_of(turns, 0)]
    for slot, turn in enumerate((1, 3)):
        view = view_of(turns, turn)
        volume = recorded[view].reshape(depth * rows, lanes)
        volume = pltpu.roll(volume, lax.rem(lanes - offsets[view], lanes), 1)
        across[...] = volume.T
        for k in range(2 * chips):
            to = lax.bitwise_xor(me, k)
            part = 2 * chips - 1 - to if turn == 1 else to
            block = across[pl.ds(pl.multiple_of(part * rows, rows), rows)]
            if k % 2 == 0:
                mine[k // 2, slot] = block
            else:
                theirs[k // 2, slot] = block


def merge(mine, swapped, inner, inner_out, *outs):
    depth, count, lanes = inner.shape
    inner_out[: depth * count] = inner[...].reshape(depth * count, lanes)
    inner_out[depth * count :] = jnp.zeros((inner_out.shape[0] - depth * count, lanes), F32)
    for k in range(1, mine.shape[0]):
        for slot in range(2):
            outs[k - 1][0, slot] = mine[k, slot]
            outs[k - 1][1, slot] = swapped[k, slot]


def ends(own, even_pair, odd_pair):
    reach = even_pair.shape[0]
    first, last = own[:reach], own[own.shape[0] - reach :]
    odd = is_odd("gy")
    even_pair[...] = jnp.where(odd, first, last)
    odd_pair[...] = jnp.where(odd, last, first)


def edges(own, even_y, odd_y, later, later_too, even_pair, odd_pair):
    depth, rows, _ = own.shape
    reach = even_y.shape[0]
    side = even_pair.shape[0]
    flip_x, flip_y = is_odd("gx"), is_odd("gy")
    for i in range(side):
        first, last = i, rows - side + i
        for start, upper, lower in (
            (0, own[:, first], own[:, last]),
            (depth, jnp.where(flip_y, even_y[:, first], odd_y[:, first]), jnp.where(flip_y, even_y[:, last], odd_y[:, last])),
            (depth + reach, jnp.where(flip_y, odd_y[:, first], even_y[:, first]), jnp.where(flip_y, odd_y[:, last], even_y[:, last])),
        ):
            stop = start + upper.shape[0]
            even_pair[i, start:stop] = jnp.where(flip_x, upper, lower)
            odd_pair[i, start:stop] = jnp.where(flip_x, lower, upper)


def row_taps_of(turn, view, row_taps, column_taps, width):
    source = column_taps if turn % 2 else row_taps
    flipped = turn in (1, 2)
    return [source[view, width - 1 - s if flipped else s] for s in range(width)]


def predict(turns, offsets, depth_taps, row_taps, column_taps, own, even_x, odd_x, even_y, odd_y,
            predicted, lane_back, depth_back, half_back, extended, blurred):
    depth, rows, lanes = own.shape
    side = even_x.shape[0]
    reach = even_y.shape[0]
    width = 2 * side + 1
    deep = depth + 2 * reach
    padded = extended.shape[1]
    views = [view_of(turns, turn) for turn in range(VIEWS)]

    column = lax.broadcasted_iota(jnp.int32, (depth, LANES), 1)
    row = lax.broadcasted_iota(jnp.int32, (depth, LANES), 0)
    layer = jnp.where(column < depth, column, jnp.where(column < depth + reach, column - depth - reach, column - reach))
    tap = jnp.where(column < deep, layer - row + reach, -1)
    stacked = []
    for view in views:
        matrix = jnp.zeros((depth, LANES), F32)
        for t in range(2 * reach + 1):
            matrix = jnp.where(tap == t, depth_taps[view, t], matrix)
        stacked.append(matrix)
    matrix = jnp.concatenate(stacked, axis=0)
    back_high, back_low = split(matrix.T[:padded])
    depth_back[0] = back_high
    depth_back[1] = back_low
    half = slice(2 * depth, 3 * depth)
    half_back[...] = jnp.concatenate([back_high[:, half], back_low[:, half], back_high[:, half]], axis=1)
    high, low = split(matrix)
    depth_high, depth_low = high[:, :padded], low[:, :padded]

    flip_x, flip_y = is_odd("gx"), is_odd("gy")
    for e in range(rows + 2 * side):
        if side <= e < side + rows:
            i = e - side
            even, odd = even_y[:, i], odd_y[:, i]
            extended[e, 0:depth] = own[:, i]
            extended[e, depth : depth + reach] = jnp.where(flip_y, even, odd)
            extended[e, depth + reach : deep] = jnp.where(flip_y, odd, even)
        elif e < side:
            extended[e, 0:deep] = jnp.where(flip_x, even_x[e], odd_x[e])
        else:
            i = e - side - rows
            extended[e, 0:deep] = jnp.where(flip_x, odd_x[i], even_x[i])
        if padded > deep:
            extended[e, deep:padded] = jnp.zeros((padded - deep, lanes), F32)

    for i in range(rows + 2 * side):
        e_high, e_low = split(extended[i])
        blurred[i] = dot(depth_high, e_high) + dot(depth_high, e_low) + dot(depth_low, e_high)

    inward = lax.broadcasted_iota(jnp.int32, (lanes, lanes), 0)
    outward = lax.broadcasted_iota(jnp.int32, (lanes, lanes), 1)
    for turn, view in enumerate(views):
        place = outward
        if turn % 2 == 0:
            place = outward - offsets[view]
            place = jnp.where(place < 0, place + lanes, place)
        tap = (lanes - 1 - place - inward if turn >= 2 else inward - place) + side
        source = row_taps if turn % 2 else column_taps
        matrix = jnp.zeros((lanes, lanes), F32)
        for r in range(width):
            matrix = jnp.where(tap == r, source[view, r], matrix)
        high, low = split(matrix)
        back_high, back_low = split(matrix.T)
        lane_back[turn, 0] = back_high
        lane_back[turn, 1] = back_low
        both = jnp.concatenate([high, high], axis=0)
        factor = row_taps_of(turn, view, row_taps, column_taps, width)
        for i in range(rows):
            layers = pl.ds(turn * depth, depth)
            total = factor[0] * blurred[i, layers]
            for s in range(1, width):
                total = total + factor[s] * blurred[i + s, layers]
            t_high, t_low = split(total)
            predicted[turn, i] = dot(jnp.concatenate([t_high, t_low], axis=1), both) + dot(t_high, low)


def turned(mine, swapped, received, arrived, data):
    parts, _, rows, wide = arrived.shape
    group = LANES // rows
    me = lax.axis_index("gx")
    for k in range(parts // 2):
        for core in range(2):
            source = lax.bitwise_xor(me, 2 * k + core)
            if k > 0:
                arrived[source] = received[k - 1][core]
            else:
                arrived[source] = swapped[0] if core else mine[0]
    granule = lax.broadcasted_iota(jnp.int32, (8, LANES), 1) // rows
    for slot in range(2):
        for part in range(0, parts, group):
            for eight in range(0, rows, 8):
                for piece in range(wide // LANES):
                    held = [
                        arrived[part + s, slot, eight : eight + 8, piece * LANES : (piece + 1) * LANES]
                        for s in range(group)
                    ]
                    step = 1
                    while step < group:
                        upper = (granule // step) % 2 == 1
                        crossed = list(held)
                        for s in range(group):
                            if s & step == 0:
                                one, two = held[s], held[s + step]
                                crossed[s] = jnp.where(upper, pltpu.roll(two, step * rows, 1), one)
                                crossed[s + step] = jnp.where(upper, two, pltpu.roll(one, LANES - step * rows, 1))
                        held = crossed
                        step *= 2
                    for s in range(group):
                        data[slot, eight : eight + 8, piece * group + s, part * rows : part * rows + LANES] = held[s]


def lane_blur(recorded, predicted, back):
    high, low = back[0], back[1]
    r_high, r_low = split(recorded / predicted)
    both = jnp.concatenate([high, high], axis=0)
    return dot(jnp.concatenate([r_high, r_low], axis=1), both) + dot(r_high, low)


def spread_row(e, factor, row_list, backed):
    total = None
    for i in row_list:
        if 0 <= e - i < len(factor):
            term = factor[e - i] * backed[i]
            total = term if total is None else total + term
    return jnp.zeros(backed.shape[1:], F32) if total is None else total


def project(turns, row_taps, column_taps, predicted, lane_back, depth_back, kept, outer, mine, swapped, *rest):
    received, (middle, even_pair, odd_pair, arrived, data, backed) = rest[:-6], rest[-6:]
    _, rows, depth, lanes = predicted.shape
    side, deep, _ = even_pair.shape
    turned(mine, swapped, received, arrived, data)
    row_lists = [range(rows)] * VIEWS
    row_lists[2] = [*range(side), *range(rows - side, rows)]
    for turn in range(VIEWS):
        for j, i in enumerate(row_lists[turn]):
            if turn == 0:
                recorded = kept[:, i]
            elif turn == 2:
                recorded = outer[:, 2 * side - 1 - j]
            else:
                recorded = data[turn // 2, rows - 1 - i if turn == 1 else i]
            backed[turn, i] = lane_blur(recorded, predicted[turn, i], lane_back.at[turn])
    factors = [
        row_taps_of(turn, view_of(turns, turn), row_taps, column_taps, 2 * side + 1) for turn in range(VIEWS)
    ]
    high, low = depth_back[0], depth_back[1]
    both = jnp.concatenate([high, low], axis=1)
    results = []
    for e in range(rows + 2 * side):
        value = jnp.concatenate(
            [spread_row(e, factors[turn], row_lists[turn], backed.at[turn]) for turn in range(VIEWS)], axis=0
        )
        s_high, s_low = split(value)
        result = dot(both, jnp.concatenate([s_high, s_high], axis=0)) + dot(high, s_low)
        if side <= e < side + rows:
            middle[e - side] = result[:deep]
        else:
            results.append(result[:deep])
    odd = is_odd("gx")
    for i in range(side):
        first, last = results[i], results[side + i]
        even_pair[i] = jnp.where(odd, first, last)
        odd_pair[i] = jnp.where(odd, last, first)


def project_half(turns, row_taps, column_taps, predicted, lane_back, half_back, flat, partial, middle, backed, inner):
    _, rows, depth, lanes = predicted.shape
    deep = middle.shape[1]
    side = (rows - inner.shape[1]) // 2
    inner[...] = flat[: depth * inner.shape[1]].reshape(inner.shape)
    row_list = range(side, rows - side)
    for i in row_list:
        backed[i] = lane_blur(inner[:, rows - side - 1 - i], predicted[2, i], lane_back.at[2])
    factor = row_taps_of(2, view_of(turns, 2), row_taps, column_taps, 2 * side + 1)
    back = half_back[...]
    for e in range(rows):
        s_high, s_low = split(spread_row(e + side, factor, row_list, backed))
        result = dot(back, jnp.concatenate([s_high, s_high, s_low], axis=0))
        middle[e] = partial[e] + result[:deep]


def gather_sides(middle, even_x, odd_x, own, even_pair, odd_pair):
    rows = middle.shape[0]
    side = even_x.shape[0]
    depth = own.shape[1]
    reach = even_pair.shape[0] // rows
    flip_x, flip_y = is_odd("gx"), is_odd("gy")
    for i in range(rows):
        value = middle[i]
        if i < side:
            value = value + jnp.where(flip_x, even_x[i], odd_x[i])
        if i >= rows - side:
            j = i - rows + side
            value = value + jnp.where(flip_x, odd_x[j], even_x[j])
        own[i] = value[:depth]
        before, after = value[depth : depth + reach], value[depth + reach : depth + 2 * reach]
        even_pair[i * reach : (i + 1) * reach] = jnp.where(flip_y, before, after)
        odd_pair[i * reach : (i + 1) * reach] = jnp.where(flip_y, after, before)


def finish(estimate, own, even_y, odd_y, out):
    rows, depth, lanes = own.shape
    reach = even_y.shape[0] // rows
    flip_y = is_odd("gy")
    rest = jnp.zeros((depth - reach, lanes), F32)
    for i in range(rows):
        even, odd = even_y[i * reach : (i + 1) * reach], odd_y[i * reach : (i + 1) * reach]
        first, last = jnp.where(flip_y, even, odd), jnp.where(flip_y, odd, even)
        value = own[i] + jnp.concatenate([first, rest], axis=0) + jnp.concatenate([rest, last], axis=0)
        out[:, i] = estimate[:, i] * value * (1.0 / VIEWS)


def call(body, out_shape, specs, scratch=()):
    return pl.pallas_call(
        body,
        out_shape=out_shape,
        in_specs=specs,
        out_specs=jax.tree.map(lambda _: VMEM, out_shape),
        scratch_shapes=scratch,
        compiler_params=PARAMS,
        cost_estimate=COST,
    )


def shards(estimate, recorded, quarter_turns, offsets, depth_taps, row_taps, column_taps):
    depth, rows, lanes = estimate.shape
    reach = (depth_taps.shape[1] - 1) // 2
    side = (row_taps.shape[1] - 1) // 2
    deep = depth + 2 * reach
    padded = -(-deep // 16) * 16
    parts = lax.axis_size("gx")
    even_y, odd_y = pairs(lax.axis_size("gy"))
    even_x, odd_x = pairs(parts)

    third, fourth = call(ends, (struct(reach, rows, lanes),) * 2, [VMEM])(estimate)
    outer, inner = pl.pallas_call(
        pick,
        out_shape=(struct(depth, 2 * side, lanes), struct(depth, rows - 2 * side, lanes)),
        grid_spec=pltpu.PrefetchScalarGridSpec(
            num_scalar_prefetch=1,
            grid=(1,),
            in_specs=[
                pl.BlockSpec((1, depth, rows, lanes), lambda i, turns: (view_of(turns, 2), 0, 0, 0)),
                ORDER,
            ],
            out_specs=[
                pl.BlockSpec((depth, 2 * side, lanes), lambda i, turns: (0, 0, 0)),
                pl.BlockSpec((depth, rows - 2 * side, lanes), lambda i, turns: (0, 0, 0)),
            ],
        ),
        compiler_params=PARAMS,
        cost_estimate=COST,
    )(quarter_turns, recorded, third)
    wide, chips = depth * rows, parts // 2
    kept, mine, theirs = call(
        prepare,
        (struct(depth, rows, lanes),) + (struct(chips, 2, rows, wide),) * 2,
        [SMEM, SMEM, VMEM, ORDER],
        [pltpu.VMEM((lanes, wide), F32)],
    )(quarter_turns, offsets, recorded, outer)
    third, fourth = lax.ppermute(third, "gy", even_y), lax.ppermute(fourth, "gy", odd_y)
    mirror = [(i, parts - 1 - i) for i in range(parts)]
    outer = lax.ppermute(outer, "gx", mirror)
    swapped = lax.ppermute(theirs, "gx", [(i, i ^ 1) for i in range(parts)])
    inner, *messages = call(
        merge,
        (struct(side * deep + 8, lanes),) + (struct(2, 2, rows, wide),) * (chips - 1),
        [VMEM] * 3,
    )(mine, swapped, inner)
    moved = {
        k: lax.ppermute(messages[k - 1], "gx", [(i, i ^ (2 * k)) for i in range(parts)])
        for k in range(chips - 1, 0, -1)
    }
    inner = lax.ppermute(inner, "gx", mirror)
    first, second = call(edges, (struct(side, deep, lanes),) * 2, [VMEM] * 3 + [ORDER] * 2)(
        estimate, third, fourth, outer, messages[0]
    )
    first, second = lax.ppermute(first, "gx", even_x), lax.ppermute(second, "gx", odd_x)

    predicted, lane_back, depth_back, half_back = call(
        predict,
        (
            struct(VIEWS, rows, depth, lanes),
            struct(VIEWS, 2, lanes, lanes, dtype=BF16),
            struct(2, padded, VIEWS * depth, dtype=BF16),
            struct(padded, 3 * depth, dtype=BF16),
        ),
        [SMEM] * 5 + [VMEM] * 5,
        [
            pltpu.VMEM((rows + 2 * side, padded, lanes), F32),
            pltpu.VMEM((rows + 2 * side, VIEWS * depth, lanes), F32),
        ],
    )(quarter_turns, offsets, depth_taps, row_taps, column_taps, estimate, first, second, third, fourth)

    middle, first, second = call(
        project,
        (struct(rows, deep, lanes), struct(side, deep, lanes), struct(side, deep, lanes)),
        [SMEM] * 3 + [VMEM] * (6 + chips),
        [
            pltpu.VMEM((parts, 2, rows, wide), F32),
            pltpu.VMEM((2, rows, depth, lanes), F32),
            pltpu.VMEM((VIEWS, rows, depth, lanes), F32),
        ],
    )(quarter_turns, row_taps, column_taps, predicted, lane_back, depth_back, kept, outer, mine, swapped,
      *[moved[k] for k in range(1, chips)])
    first, second = lax.ppermute(first, "gx", even_x), lax.ppermute(second, "gx", odd_x)
    middle = call(
        project_half,
        struct(rows, deep, lanes),
        [SMEM] * 3 + [VMEM] * 5,
        [pltpu.VMEM((rows, depth, lanes), F32), pltpu.VMEM((depth, rows - 2 * side, lanes), F32)],
    )(quarter_turns, row_taps, column_taps, predicted, lane_back, half_back, inner, middle)
    own, third, fourth = call(
        gather_sides,
        (struct(rows, depth, lanes), struct(rows * reach, lanes), struct(rows * reach, lanes)),
        [VMEM] * 3,
    )(middle, first, second)
    third, fourth = lax.ppermute(third, "gy", even_y), lax.ppermute(fourth, "gy", odd_y)
    return call(finish, struct(depth, rows, lanes), [VMEM] * 4)(estimate, own, third, fourth)


def solution(mesh):
    in_specs = (P("gy", "gx", None), P(None, "gy", "gx", None), P(), P(), P(), P(), P())
    out_specs = P("gy", "gx", None)
    return jax.shard_map(shards, mesh=mesh, in_specs=in_specs, out_specs=out_specs, check_vma=False)
```

time: 63.2 us -> 61.8 us (0.978)
  starting transfers between devices: 21.8 us -> 18.9 us
  waiting for transfers between devices: 30.4 us -> 28.5 us
  Pallas kernels: 8.17 us -> 9.82 us
  local copies, waits for them, and re-layouts: 2.2 us -> 3.57 us
    ppermute x2, waiting for transfers between devices: 7.64 us -> 4.2 us  [shards(): lax.ppermute(second, 'gx', odd_x)]
    ppermute x8 -> x6, starting transfers between devices: 8.68 us -> 5.85 us  [the longest x3 3.7 us: shards(): lax.ppermute(messages[k - 1], 'gx', [(i, i ^ 2 * k) for i in range(parts)])]
    ppermute x8 -> x6, waiting for transfers between devices: 16.5 us -> 18.2 us  [the longest x3 10.8 us: shards(): lax.ppermute(messages[k - 1], 'gx', [(i, i ^ 2 * k) for i in range(parts)])]
    pallas_call x3 -> x6, Pallas kernels: 1.3 us -> 2.98 us  [the longest x1 1.11 us: shards(): call(project_half, struct(rows, deep, lanes), [SMEM] * 3 + [VMEM] * 5, [p...]
    unnamed x16 -> x18, local copies, waits for them, and re-layouts: 2.2 us -> 3.57 us
  transfers between devices with their start and end apart: 16 -> 14, of which waited for: 9 -> 7; matrix products, arithmetic and copies ran while one was open for 0% -> 0% of each run, Pallas kernels for 6% -> 11%
where the time goes in v3:
time: 61.8 us; the launch traced here: 60.9 us
  waiting for transfers between devices  28.5 us (46%)
  starting transfers between devices  18.9 us (31%)
  Pallas kernels  9.82 us (16%)
  local copies, waits for them, and re-layouts  3.57 us (6%)
    ppermute x3, waiting for transfers between devices, shards(): lax.ppermute(messages[k - 1], 'gx', [(i, i ^ 2 * k) for i in range(parts)])  10.8 us
    ppermute x1, waiting for transfers between devices, shards(): outer = lax.ppermute(outer, 'gx', mirror)  7.36 us
    ppermute x2, starting transfers between devices, shards(): lax.ppermute(fourth, 'gy', odd_y)  6.73 us
    ppermute x2, waiting for transfers between devices, shards(): lax.ppermute(fourth, 'gy', odd_y)  4.22 us
    ppermute x2, waiting for transfers between devices, shards(): lax.ppermute(second, 'gx', odd_x)  4.2 us
    ppermute x2, starting transfers between devices, shards(): lax.ppermute(second, 'gx', odd_x)  3.95 us
    ppermute x3, starting transfers between devices, shards(): lax.ppermute(messages[k - 1], 'gx', [(i, i ^ 2 * k) for i in range(parts)])  3.7 us
    unnamed x18, local copies, waits for them, and re-layouts  3.57 us
  transfers between devices with their start and end apart: 14, of which 7 were waited for; matrix products, arithmetic and copies ran while one was open for 0% of the time, Pallas kernels for 11%

profile of v3, /device:TPU:12, one launch (start us, length us, event | category | flops | bytes accessed | tf_op | source)
XLA Modules:
  0.0 60.9 jit_solution(4511728500813127502)
XLA Ops:
  0.0 0.0 copy-start.2
  0.0 0.9 %copy-done.2 = f32[32,16,128]{2,1,0:T(8,128)S(1)} copy-done((f32[32,16,128]{2,1,0:T(8,128)S(1)}, f32[32,16,128]{2,1,0:T(8,128)}, u32[]{:S(2)}) %copy-start.2) | copy-done | bytes 262168
  1.0 0.0 copy-start.6
  1.0 0.6 %copy-done.6 = s32[4]{0:T(128)S(1)} copy-done((s32[4]{0:T(128)S(1)}, s32[4]{0:T(128)}, u32[]{:S(2)}) %copy-start.6) | copy-done | bytes 40
  1.6 0.0 copy-start
  1.7 1.2 %copy-done = f32[4,32,16,128]{3,2,1,0:T(8,128)S(1)} copy-done((f32[4,32,16,128]{3,2,1,0:T(8,128)S(1)}, f32[4,32,16,128]{3,2,1,0:T(8,128)}, u32[]{:S(2)}) %copy-start) | copy-done | bytes 1048600
  2.9 0.0 copy-start.1
  2.9 0.6 shard_map.74
  3.5 0.0 copy-start.8
  3.5 0.6 %copy-done.1 = f32[4,32,16,128]{3,2,1,0:T(8,128)S(1)} copy-done((f32[4,32,16,128]{3,2,1,0:T(8,128)S(1)}, f32[4,32,16,128]{3,2,1,0:T(8,128)}, u32[]{:S(2)}) %copy-start.1) | copy-done | bytes 1048600
  4.1 0.1 copy-done.8
  4.2 0.9 %shard_map.75 = (f32[32,16,128]{2,1,0:T(8,128)S(1)}, f32[4,2,16,512]{3,2,1,0:T(8,128)S(1)}, f32[4,2,16,512]{3,2,1,0:T(8,128)S(1)}) custom-call(s32[4]{0:T(128)S(1)} %copy-done.6, s32[4]{0:T(128)S(1)} %copy-done.8, f32[4,32,16,128]{3,2,1,0:T(8,128)S(1)} %copy-done.1, f32[32,8,128]{2,1,0:T(8,128)S(1)} %get-tuple-element.30.later), custom_call_target="tpu_custom_call" | custom-call | flops 1 | bytes 1 | tf_op jit(solution)/shard_map/pallas_call | solution.py:376
  5.1 0.1 collective-permute-start.3
  5.2 1.6 %collective-permute-start = (f32[20,16,128]{2,1,0:T(8,128)S(1)}, f32[20,16,128]{2,1,0:T(8,128)S(1)}, u32[]{:S(2)}, u32[]{:S(2)}) collective-permute-start(f32[20,16,128]{2,1,0:T(8,128)S(1)} %get-tuple-element.28.later), channel_id=1, source_target_pairs={{0,8},{8,0},{16,24},{24,16},{1,9},{9,1},{17,25},{25,17},{2,10},{10... | collective-permute-start | bytes 491528 | tf_op jit(solution)/shard_map/ppermute | solution.py:382
  6.8 2.4 %collective-permute-start.1 = (f32[20,16,128]{2,1,0:T(8,128)S(1)}, f32[20,16,128]{2,1,0:T(8,128)S(1)}, u32[]{:S(2)}, u32[]{:S(2)}) collective-permute-start(f32[20,16,128]{2,1,0:T(8,128)S(1)} %get-tuple-element.29), channel_id=1, source_target_pairs={{8,16},{16,8},{9,17},{17,9},{10,18},{18,10},{11,19},{19,11},{12,20... | collective-permute-start | bytes 491528 | tf_op jit(solution)/shard_map/ppermute | solution.py:382
  9.1 1.1 %collective-permute-start.2 = (f32[32,8,128]{2,1,0:T(8,128)S(1)}, f32[32,8,128]{2,1,0:T(8,128)S(1)}, u32[]{:S(2)}, u32[]{:S(2)}) collective-permute-start(f32[32,8,128]{2,1,0:T(8,128)S(1)} %get-tuple-element.30.later), channel_id=1, source_target_pairs={{0,7},{1,6},{2,5},{3,4},{4,3},{5,2},{6,1},{7,0},{8,15},{9,14},{10,... | collective-permute-start | bytes 393224 | tf_op jit(solution)/shard_map/ppermute | solution.py:384
  10.3 0.0 collective-permute-done.3.swapped
  10.3 0.0 copy-start.3
  10.3 7.4 %collective-permute-done.2.later.outer = f32[32,8,128]{2,1,0:T(8,128)S(1)} collective-permute-done((f32[32,8,128]{2,1,0:T(8,128)S(1)}, f32[32,8,128]{2,1,0:T(8,128)S(1)}, u32[]{:S(2)}, u32[]{:S(2)}) %collective-permute-start.2) | collective-permute-done | bytes 131104 | tf_op jit(solution)/shard_map/ppermute | solution.py:384
  17.7 0.0 collective-permute-done.even_y
  17.7 0.0 collective-permute-done.1.odd_y
  17.7 0.0 copy-done.3
  17.7 0.3 shard_map.77
  18.0 0.2 collective-permute-start.4
  18.2 0.0 copy-start.7
  18.2 2.0 %collective-permute-start.5 = (f32[4,72,128]{2,1,0:T(8,128)S(1)}, f32[4,72,128]{2,1,0:T(8,128)S(1)}, u32[]{:S(2)}, u32[]{:S(2)}) collective-permute-start(f32[4,72,128]{2,1,0:T(8,128)S(1)} %get-tuple-element.36), channel_id=1, source_target_pairs={{1,2},{2,1},{3,4},{4,3},{5,6},{6,5},{9,10},{10,9},{11,12},{12,11},... | collective-permute-start | bytes 442376 | tf_op jit(solution)/shard_map/ppermute | solution.py:399
  20.2 0.1 collective-permute-start.7
  20.3 0.0 copy-start.5
  20.3 0.0 copy-start.4
  20.3 3.4 %collective-permute-start.8 = (f32[2,2,16,512]{3,2,1,0:T(8,128)S(1)}, f32[2,2,16,512]{3,2,1,0:T(8,128)S(1)}, u32[]{:S(2)}, u32[]{:S(2)}) collective-permute-start(f32[2,2,16,512]{3,2,1,0:T(8,128)S(1)} %get-tuple-element.43), channel_id=1, source_target_pairs={{0,4},{1,5},{2,6},{3,7},{4,0},{5,1},{6,2},{7,3},{8,12},{9,13},{10,... | collective-permute-start | bytes 393224 | tf_op jit(solution)/shard_map/ppermute | solution.py:392
  23.8 0.2 collective-permute-start.9
  24.0 0.0 collective-permute-done.4.even_x
  24.0 1.0 %collective-permute-start.6 = (f32[296,128]{1,0:T(8,128)S(1)}, f32[296,128]{1,0:T(8,128)S(1)}, u32[]{:S(2)}, u32[]{:S(2)}) collective-permute-start(f32[296,128]{1,0:T(8,128)S(1)} %get-tuple-element.40), channel_id=1, source_target_pairs={{0,7},{1,6},{2,5},{3,4},{4,3},{5,2},{6,1},{7,0},{8,15},{9,14},{10,... | collective-permute-start | bytes 454664 | tf_op jit(solution)/shard_map/ppermute | solution.py:395
  24.9 0.8 %collective-permute-done.5.odd_x = f32[4,72,128]{2,1,0:T(8,128)S(1)} collective-permute-done((f32[4,72,128]{2,1,0:T(8,128)S(1)}, f32[4,72,128]{2,1,0:T(8,128)S(1)}, u32[]{:S(2)}, u32[]{:S(2)}) %collective-permute-start.5) | collective-permute-done | bytes 147488 | tf_op jit(solution)/shard_map/ppermute | solution.py:399
  25.7 0.0 copy-done.7
  25.7 0.0 copy-done.5
  25.7 0.0 copy-done.4
  25.7 3.1 %shard_map.78 = (f32[4,16,32,128]{3,2,1,0:T(8,128)S(1)}, bf16[4,2,128,128]{3,2,1,0:T(8,128)(2,1)S(1)}, bf16[2,80,128]{2,1,0:T(8,128)(2,1)S(1)}, bf16[80,96]{1,0:T(8,128)(2,1)S(1)}) custom-call(s32[4]{0:T(128)S(1)} %copy-done.6, s32[4]{0:T(128)S(1)} %copy-done.8, f32[4,41]{1,0:T(4,128)S(1)} %copy-done.7, f32[4,9]{1,0:T(4,128)S(1)} %copy-done.4, ...), custom_call_target="tpu_custom_call" | custom-call | flops 1 | bytes 1 | tf_op jit(solution)/shard_map/pallas_call | solution.py:401
  28.9 0.0 collective-permute-done.7.rest_0_
  28.9 7.7 %collective-permute-done.8.rest_1_ = f32[2,2,16,512]{3,2,1,0:T(8,128)S(1)} collective-permute-done((f32[2,2,16,512]{3,2,1,0:T(8,128)S(1)}, f32[2,2,16,512]{3,2,1,0:T(8,128)S(1)}, u32[]{:S(2)}, u32[]{:S(2)}) %collective-permute-start.8) | collective-permute-done | bytes 131104 | tf_op jit(solution)/shard_map/ppermute | solution.py:392
  36.6 3.1 %collective-permute-done.9.rest_2_ = f32[2,2,16,512]{3,2,1,0:T(8,128)S(1)} collective-permute-done((f32[2,2,16,512]{3,2,1,0:T(8,128)S(1)}, f32[2,2,16,512]{3,2,1,0:T(8,128)S(1)}, u32[]{:S(2)}, u32[]{:S(2)}) %collective-permute-start.9) | collective-permute-done | bytes 131104 | tf_op jit(solution)/shard_map/ppermute | solution.py:392
  39.7 2.6 %shard_map.79 = (f32[16,72,128]{2,1,0:T(8,128)S(1)}, f32[4,72,128]{2,1,0:T(8,128)S(1)}, f32[4,72,128]{2,1,0:T(8,128)S(1)}) custom-call(s32[4]{0:T(128)S(1)} %copy-done.6, f32[4,9]{1,0:T(4,128)S(1)} %copy-done.4, f32[4,9]{1,0:T(4,128)S(1)} %copy-done.5, f32[4,16,32,128]{3,2,1,0:T(8,128)S(1)} %get-tuple-element.37.predicted, ...), custom_call_target="tpu_custom_call" | custom-call | flops 1 | bytes 1 | tf_op jit(solution)/shard_map/pallas_call | solution.py:416
  42.3 0.5 collective-permute-start.10
  42.8 1.9 %collective-permute-start.11 = (f32[4,72,128]{2,1,0:T(8,128)S(1)}, f32[4,72,128]{2,1,0:T(8,128)S(1)}, u32[]{:S(2)}, u32[]{:S(2)}) collective-permute-start(f32[4,72,128]{2,1,0:T(8,128)S(1)} %get-tuple-element.47), channel_id=1, source_target_pairs={{1,2},{2,1},{3,4},{4,3},{5,6},{6,5},{9,10},{10,9},{11,12},{12,11},... | collective-permute-start | bytes 442376 | tf_op jit(solution)/shard_map/ppermute | solution.py:427
  44.8 0.0 collective-permute-done.6.flat
  44.8 1.1 %shard_map.80.middle = f32[16,72,128]{2,1,0:T(8,128)S(1)} custom-call(s32[4]{0:T(128)S(1)} %copy-done.6, f32[4,9]{1,0:T(4,128)S(1)} %copy-done.4, f32[4,9]{1,0:T(4,128)S(1)} %copy-done.5, f32[4,16,32,128]{3,2,1,0:T(8,128)S(1)} %get-tuple-element.37.predicted, bf16[4,2,128,128]{3,2,1,0:T(8,128)(2,1)S(1)} %get-tuple-element.38.lane_back, ...), custom_call_target="tpu_custom_call" | custom-call | flops 1 | bytes 1 | tf_op jit(solution)/shard_map/pallas_call | solution.py:428
  45.9 0.0 collective-permute-done.10.even_x
  45.9 3.4 %collective-permute-done.11.odd_x = f32[4,72,128]{2,1,0:T(8,128)S(1)} collective-permute-done((f32[4,72,128]{2,1,0:T(8,128)S(1)}, f32[4,72,128]{2,1,0:T(8,128)S(1)}, u32[]{:S(2)}, u32[]{:S(2)}) %collective-permute-start.11) | collective-permute-done | bytes 147488 | tf_op jit(solution)/shard_map/ppermute | solution.py:427
  49.3 0.1 shard_map.81
  49.4 0.1 collective-permute-start.12
  49.4 4.4 %collective-permute-start.13 = (f32[320,128]{1,0:T(8,128)S(1)}, f32[320,128]{1,0:T(8,128)S(1)}, u32[]{:S(2)}, u32[]{:S(2)}) collective-permute-start(f32[320,128]{1,0:T(8,128)S(1)} %get-tuple-element.50), channel_id=1, source_target_pairs={{8,16},{16,8},{9,17},{17,9},{10,18},{18,10},{11,19},{19,11},{12,20... | collective-permute-start | bytes 491528 | tf_op jit(solution)/shard_map/ppermute | solution.py:439
  53.8 1.8 %collective-permute-done.12.even_y = f32[320,128]{1,0:T(8,128)S(1)} collective-permute-done((f32[320,128]{1,0:T(8,128)S(1)}, f32[320,128]{1,0:T(8,128)S(1)}, u32[]{:S(2)}, u32[]{:S(2)}) %collective-permute-start.12) | collective-permute-done | bytes 163872 | tf_op jit(solution)/shard_map/ppermute | solution.py:439
  55.7 4.2 %collective-permute-done.13.odd_y = f32[320,128]{1,0:T(8,128)S(1)} collective-permute-done((f32[320,128]{1,0:T(8,128)S(1)}, f32[320,128]{1,0:T(8,128)S(1)}, u32[]{:S(2)}, u32[]{:S(2)}) %collective-permute-start.13) | collective-permute-done | bytes 163872 | tf_op jit(solution)/shard_map/ppermute | solution.py:439
  59.9 1.0 %shard_map.82 = f32[32,16,128]{2,1,0:T(8,128)} custom-call(f32[32,16,128]{2,1,0:T(8,128)S(1)} %copy-done.3, f32[16,32,128]{2,1,0:T(8,128)S(1)} %get-tuple-element.48.own, f32[320,128]{1,0:T(8,128)S(1)} %collective-permute-done.12.even_y, f32[320,128]{1,0:T(8,128)S(1)} %collective-permute-done.13.odd_y), custom_call_target="tpu_custom_call" | custom-call | flops 1 | bytes 1 | tf_op jit(solution)/shard_map/pallas_call | solution.py:440
  (2 shorter events, 0.1 us)
Async XLA Ops:
  0.0 0.9 %copy-start.2 = (f32[32,16,128]{2,1,0:T(8,128)S(1)}, f32[32,16,128]{2,1,0:T(8,128)}, u32[]{:S(2)}) copy-start(f32[32,16,128]{2,1,0:T(8,128)} %estimate.1) | copy-start | bytes 786436
  1.0 0.7 %copy-start.6 = (s32[4]{0:T(128)S(1)}, s32[4]{0:T(128)}, u32[]{:S(2)}) copy-start(s32[4]{0:T(128)} %turns.9) | copy-start | bytes 52
  1.6 1.2 %copy-start = (f32[4,32,16,128]{3,2,1,0:T(8,128)S(1)}, f32[4,32,16,128]{3,2,1,0:T(8,128)}, u32[]{:S(2)}) copy-start(f32[4,32,16,128]{3,2,1,0:T(8,128)} %recorded.3) | copy-start | bytes 3145732
  2.9 1.2 %copy-start.1 = (f32[4,32,16,128]{3,2,1,0:T(8,128)S(1)}, f32[4,32,16,128]{3,2,1,0:T(8,128)}, u32[]{:S(2)}) copy-start(f32[4,32,16,128]{3,2,1,0:T(8,128)} %recorded.3) | copy-start | bytes 3145732
  3.5 0.7 %copy-start.8 = (s32[4]{0:T(128)S(1)}, s32[4]{0:T(128)}, u32[]{:S(2)}) copy-start(s32[4]{0:T(128)} %offsets.3) | copy-start | bytes 52
  5.1 5.2 %collective-permute-start.3 = (f32[4,2,16,512]{3,2,1,0:T(8,128)S(1)}, f32[4,2,16,512]{3,2,1,0:T(8,128)S(1)}, u32[]{:S(2)}, u32[]{:S(2)}) collective-permute-start(f32[4,2,16,512]{3,2,1,0:T(8,128)S(1)} %get-tuple-element.32), channel_id=1, source_target_pairs={{0,1},{1,0},{2,3},{3,2},{4,5},{5,4},{6,7},{7,6},{8,9},{9,8},{10,11... | collective-permute-start | bytes 786440 | tf_op jit(solution)/shard_map/ppermute | solution.py:385
  5.2 12.5 %collective-permute-start = (f32[20,16,128]{2,1,0:T(8,128)S(1)}, f32[20,16,128]{2,1,0:T(8,128)S(1)}, u32[]{:S(2)}, u32[]{:S(2)}) collective-permute-start(f32[20,16,128]{2,1,0:T(8,128)S(1)} %get-tuple-element.28.later), channel_id=1, source_target_pairs={{0,8},{8,0},{16,24},{24,16},{1,9},{9,1},{17,25},{25,17},{2,10},{10... | collective-permute-start | bytes 491528 | tf_op jit(solution)/shard_map/ppermute | solution.py:382
  6.8 10.9 %collective-permute-start.1 = (f32[20,16,128]{2,1,0:T(8,128)S(1)}, f32[20,16,128]{2,1,0:T(8,128)S(1)}, u32[]{:S(2)}, u32[]{:S(2)}) collective-permute-start(f32[20,16,128]{2,1,0:T(8,128)S(1)} %get-tuple-element.29), channel_id=1, source_target_pairs={{8,16},{16,8},{9,17},{17,9},{10,18},{18,10},{11,19},{19,11},{12,20... | collective-permute-start | bytes 491528 | tf_op jit(solution)/shard_map/ppermute | solution.py:382
  9.1 8.5 %collective-permute-start.2 = (f32[32,8,128]{2,1,0:T(8,128)S(1)}, f32[32,8,128]{2,1,0:T(8,128)S(1)}, u32[]{:S(2)}, u32[]{:S(2)}) collective-permute-start(f32[32,8,128]{2,1,0:T(8,128)S(1)} %get-tuple-element.30.later), channel_id=1, source_target_pairs={{0,7},{1,6},{2,5},{3,4},{4,3},{5,2},{6,1},{7,0},{8,15},{9,14},{10,... | collective-permute-start | bytes 393224 | tf_op jit(solution)/shard_map/ppermute | solution.py:384
  10.3 7.4 %copy-start.3 = (f32[32,16,128]{2,1,0:T(8,128)S(1)}, f32[32,16,128]{2,1,0:T(8,128)}, u32[]{:S(2)}) copy-start(f32[32,16,128]{2,1,0:T(8,128)} %estimate.1) | copy-start | bytes 786436
  18.0 6.0 %collective-permute-start.4 = (f32[4,72,128]{2,1,0:T(8,128)S(1)}, f32[4,72,128]{2,1,0:T(8,128)S(1)}, u32[]{:S(2)}, u32[]{:S(2)}) collective-permute-start(f32[4,72,128]{2,1,0:T(8,128)S(1)} %get-tuple-element.35), channel_id=1, source_target_pairs={{0,1},{1,0},{2,3},{3,2},{4,5},{5,4},{6,7},{7,6},{8,9},{9,8},{10,11... | collective-permute-start | bytes 442376 | tf_op jit(solution)/shard_map/ppermute | solution.py:399
  18.2 7.5 %copy-start.7 = (f32[4,41]{1,0:T(4,128)S(1)}, f32[4,41]{1,0:T(4,128)}, u32[]{:S(2)}) copy-start(f32[4,41]{1,0:T(4,128)} %depth_taps.1) | copy-start | bytes 1972
  18.2 7.5 %collective-permute-start.5 = (f32[4,72,128]{2,1,0:T(8,128)S(1)}, f32[4,72,128]{2,1,0:T(8,128)S(1)}, u32[]{:S(2)}, u32[]{:S(2)}) collective-permute-start(f32[4,72,128]{2,1,0:T(8,128)S(1)} %get-tuple-element.36), channel_id=1, source_target_pairs={{1,2},{2,1},{3,4},{4,3},{5,6},{6,5},{9,10},{10,9},{11,12},{12,11},... | collective-permute-start | bytes 442376 | tf_op jit(solution)/shard_map/ppermute | solution.py:399
  20.2 8.6 %collective-permute-start.7 = (f32[2,2,16,512]{3,2,1,0:T(8,128)S(1)}, f32[2,2,16,512]{3,2,1,0:T(8,128)S(1)}, u32[]{:S(2)}, u32[]{:S(2)}) collective-permute-start(f32[2,2,16,512]{3,2,1,0:T(8,128)S(1)} %get-tuple-element.34.later_too), channel_id=1, source_target_pairs={{0,2},{1,3},{2,0},{3,1},{4,6},{5,7},{6,4},{7,5},{8,10},{9,11},{10,... | collective-permute-start | bytes 393224 | tf_op jit(solution)/shard_map/ppermute | solution.py:392
  20.3 5.4 %copy-start.5 = (f32[4,9]{1,0:T(4,128)S(1)}, f32[4,9]{1,0:T(4,128)}, u32[]{:S(2)}) copy-start(f32[4,9]{1,0:T(4,128)} %column_taps.5) | copy-start | bytes 436
  20.3 5.4 %copy-start.4 = (f32[4,9]{1,0:T(4,128)S(1)}, f32[4,9]{1,0:T(4,128)}, u32[]{:S(2)}) copy-start(f32[4,9]{1,0:T(4,128)} %row_taps.5) | copy-start | bytes 436
  20.3 16.2 %collective-permute-start.8 = (f32[2,2,16,512]{3,2,1,0:T(8,128)S(1)}, f32[2,2,16,512]{3,2,1,0:T(8,128)S(1)}, u32[]{:S(2)}, u32[]{:S(2)}) collective-permute-start(f32[2,2,16,512]{3,2,1,0:T(8,128)S(1)} %get-tuple-element.43), channel_id=1, source_target_pairs={{0,4},{1,5},{2,6},{3,7},{4,0},{5,1},{6,2},{7,3},{8,12},{9,13},{10,... | collective-permute-start | bytes 393224 | tf_op jit(solution)/shard_map/ppermute | solution.py:392
  23.8 15.9 %collective-permute-start.9 = (f32[2,2,16,512]{3,2,1,0:T(8,128)S(1)}, f32[2,2,16,512]{3,2,1,0:T(8,128)S(1)}, u32[]{:S(2)}, u32[]{:S(2)}) collective-permute-start(f32[2,2,16,512]{3,2,1,0:T(8,128)S(1)} %get-tuple-element.44), channel_id=1, source_target_pairs={{0,6},{1,7},{2,4},{3,5},{4,2},{5,3},{6,0},{7,1},{8,14},{9,15},{10,... | collective-permute-start | bytes 393224 | tf_op jit(solution)/shard_map/ppermute | solution.py:392
  24.0 20.8 %collective-permute-start.6 = (f32[296,128]{1,0:T(8,128)S(1)}, f32[296,128]{1,0:T(8,128)S(1)}, u32[]{:S(2)}, u32[]{:S(2)}) collective-permute-start(f32[296,128]{1,0:T(8,128)S(1)} %get-tuple-element.40), channel_id=1, source_target_pairs={{0,7},{1,6},{2,5},{3,4},{4,3},{5,2},{6,1},{7,0},{8,15},{9,14},{10,... | collective-permute-start | bytes 454664 | tf_op jit(solution)/shard_map/ppermute | solution.py:395
  42.3 3.6 %collective-permute-start.10 = (f32[4,72,128]{2,1,0:T(8,128)S(1)}, f32[4,72,128]{2,1,0:T(8,128)S(1)}, u32[]{:S(2)}, u32[]{:S(2)}) collective-permute-start(f32[4,72,128]{2,1,0:T(8,128)S(1)} %get-tuple-element.46), channel_id=1, source_target_pairs={{0,1},{1,0},{2,3},{3,2},{4,5},{5,4},{6,7},{7,6},{8,9},{9,8},{10,11... | collective-permute-start | bytes 442376 | tf_op jit(solution)/shard_map/ppermute | solution.py:427
  42.8 6.5 %collective-permute-start.11 = (f32[4,72,128]{2,1,0:T(8,128)S(1)}, f32[4,72,128]{2,1,0:T(8,128)S(1)}, u32[]{:S(2)}, u32[]{:S(2)}) collective-permute-start(f32[4,72,128]{2,1,0:T(8,128)S(1)} %get-tuple-element.47), channel_id=1, source_target_pairs={{1,2},{2,1},{3,4},{4,3},{5,6},{6,5},{9,10},{10,9},{11,12},{12,11},... | collective-permute-start | bytes 442376 | tf_op jit(solution)/shard_map/ppermute | solution.py:427
  49.4 6.3 %collective-permute-start.12 = (f32[320,128]{1,0:T(8,128)S(1)}, f32[320,128]{1,0:T(8,128)S(1)}, u32[]{:S(2)}, u32[]{:S(2)}) collective-permute-start(f32[320,128]{1,0:T(8,128)S(1)} %get-tuple-element.49), channel_id=1, source_target_pairs={{0,8},{8,0},{16,24},{24,16},{1,9},{9,1},{17,25},{25,17},{2,10},{10... | collective-permute-start | bytes 491528 | tf_op jit(solution)/shard_map/ppermute | solution.py:439
  49.4 10.4 %collective-permute-start.13 = (f32[320,128]{1,0:T(8,128)S(1)}, f32[320,128]{1,0:T(8,128)S(1)}, u32[]{:S(2)}, u32[]{:S(2)}) collective-permute-start(f32[320,128]{1,0:T(8,128)S(1)} %get-tuple-element.50), channel_id=1, source_target_pairs={{8,16},{16,8},{9,17},{17,9},{10,18},{18,10},{11,19},{19,11},{12,20... | collective-permute-start | bytes 491528 | tf_op jit(solution)/shard_map/ppermute | solution.py:439

commit v4 on v3

--- a/solution.py
+++ b/solution.py
@@ -77,39 +77,45 @@
                 theirs[k // 2, slot] = block
 
 
-def merge(mine, swapped, inner, inner_out, *outs):
-    depth, count, lanes = inner.shape
-    inner_out[: depth * count] = inner[...].reshape(depth * count, lanes)
-    inner_out[depth * count :] = jnp.zeros((inner_out.shape[0] - depth * count, lanes), F32)
+def merge(mine, swapped, *outs):
     for k in range(1, mine.shape[0]):
         for slot in range(2):
             outs[k - 1][0, slot] = mine[k, slot]
             outs[k - 1][1, slot] = swapped[k, slot]
 
 
-def ends(own, even_pair, odd_pair):
-    reach = even_pair.shape[0]
-    first, last = own[:reach], own[own.shape[0] - reach :]
-    odd = is_odd("gy")
-    even_pair[...] = jnp.where(odd, first, last)
-    odd_pair[...] = jnp.where(odd, last, first)
-
-
-def edges(own, even_y, odd_y, later, later_too, even_pair, odd_pair):
+def hold(inner, *rest):
+    flat = rest[-1]
+    depth, count, lanes = inner.shape
+    flat[: depth * count] = inner[...].reshape(depth * count, lanes)
+    flat[depth * count :] = jnp.zeros((flat.shape[0] - depth * count, lanes), F32)
+
+
+def edges(own, even_pair, odd_pair):
+    rows = own.shape[1]
+    side = even_pair.shape[0]
+    odd = is_odd("gx")
+    for i in range(side):
+        first, last = own[:, i], own[:, rows - side + i]
+        even_pair[i] = jnp.where(odd, first, last)
+        odd_pair[i] = jnp.where(odd, last, first)
+
+
+def layers_out(own, from_even, from_odd, even_pair, odd_pair):
     depth, rows, _ = own.shape
-    reach = even_y.shape[0]
-    side = even_pair.shape[0]
-    flip_x, flip_y = is_odd("gx"), is_odd("gy")
-    for i in range(side):
-        first, last = i, rows - side + i
-        for start, upper, lower in (
-            (0, own[:, first], own[:, last]),
-            (depth, jnp.where(flip_y, even_y[:, first], odd_y[:, first]), jnp.where(flip_y, even_y[:, last], odd_y[:, last])),
-            (depth + reach, jnp.where(flip_y, odd_y[:, first], even_y[:, first]), jnp.where(flip_y, odd_y[:, last], even_y[:, last])),
-        ):
-            stop = start + upper.shape[0]
-            even_pair[i, start:stop] = jnp.where(flip_x, upper, lower)
-            odd_pair[i, start:stop] = jnp.where(flip_x, lower, upper)
+    side = from_even.shape[0]
+    reach = even_pair.shape[0] // (rows + 2 * side)
+    odd_x, odd_y = is_odd("gx"), is_odd("gy")
+    for e in range(rows + 2 * side):
+        if e < side:
+            value = jnp.where(odd_x, from_even[e], from_odd[e])
+        elif e < side + rows:
+            value = own[:, e - side]
+        else:
+            value = jnp.where(odd_x, from_odd[e - side - rows], from_even[e - side - rows])
+        first, last = value[:reach], value[depth - reach :]
+        even_pair[e * reach : (e + 1) * reach] = jnp.where(odd_y, first, last)
+        odd_pair[e * reach : (e + 1) * reach] = jnp.where(odd_y, last, first)
 
 
 def row_taps_of(turn, view, row_taps, column_taps, width):
@@ -122,7 +128,7 @@
             predicted, lane_back, depth_back, half_back, extended, blurred):
     depth, rows, lanes = own.shape
     side = even_x.shape[0]
-    reach = even_y.shape[0]
+    reach = even_y.shape[0] // (rows + 2 * side)
     width = 2 * side + 1
     deep = depth + 2 * reach
     padded = extended.shape[1]
@@ -149,17 +155,15 @@
 
     flip_x, flip_y = is_odd("gx"), is_odd("gy")
     for e in range(rows + 2 * side):
-        if side <= e < side + rows:
-            i = e - side
-            even, odd = even_y[:, i], odd_y[:, i]
-            extended[e, 0:depth] = own[:, i]
-            extended[e, depth : depth + reach] = jnp.where(flip_y, even, odd)
-            extended[e, depth + reach : deep] = jnp.where(flip_y, odd, even)
-        elif e < side:
-            extended[e, 0:deep] = jnp.where(flip_x, even_x[e], odd_x[e])
+        if e < side:
+            extended[e, 0:depth] = jnp.where(flip_x, even_x[e], odd_x[e])
+        elif e < side + rows:
+            extended[e, 0:depth] = own[:, e - side]
         else:
-            i = e - side - rows
-            extended[e, 0:deep] = jnp.where(flip_x, odd_x[i], even_x[i])
+            extended[e, 0:depth] = jnp.where(flip_x, odd_x[e - side - rows], even_x[e - side - rows])
+        even, odd = even_y[e * reach : (e + 1) * reach], odd_y[e * reach : (e + 1) * reach]
+        extended[e, depth : depth + reach] = jnp.where(flip_y, even, odd)
+        extended[e, depth + reach : deep] = jnp.where(flip_y, odd, even)
         if padded > deep:
             extended[e, deep:padded] = jnp.zeros((padded - deep, lanes), F32)
 
@@ -236,52 +240,77 @@
     return dot(jnp.concatenate([r_high, r_low], axis=1), both) + dot(r_high, low)
 
 
-def spread_row(e, factor, row_list, backed):
+def depth_blur(back, parts):
+    high, low = back[0], back[1]
+    s_high, s_low = split(jnp.concatenate(parts, axis=0))
+    both = jnp.concatenate([high, low], axis=1)
+    return dot(both, jnp.concatenate([s_high, s_high], axis=0)) + dot(high, s_low)
+
+
+def spread_row(e, factor, places, backed):
     total = None
-    for i in row_list:
+    for i, place in places.items():
         if 0 <= e - i < len(factor):
-            term = factor[e - i] * backed[i]
+            term = factor[e - i] * backed[place]
             total = term if total is None else total + term
     return jnp.zeros(backed.shape[1:], F32) if total is None else total
 
 
-def project(turns, row_taps, column_taps, predicted, lane_back, depth_back, kept, outer, mine, swapped, *rest):
-    received, (middle, even_pair, odd_pair, arrived, data, backed) = rest[:-6], rest[-6:]
+def project_sides(turns, row_taps, column_taps, predicted, lane_back, depth_back, kept, outer, mine, swapped, *rest):
+    received, (even_pair, odd_pair, data, backed, arrived) = rest[:-5], rest[-5:]
     _, rows, depth, lanes = predicted.shape
     side, deep, _ = even_pair.shape
     turned(mine, swapped, received, arrived, data)
-    row_lists = [range(rows)] * VIEWS
-    row_lists[2] = [*range(side), *range(rows - side, rows)]
+    row_list = [*range(side), *range(rows - side, rows)]
     for turn in range(VIEWS):
-        for j, i in enumerate(row_lists[turn]):
+        for j, i in enumerate(row_list):
             if turn == 0:
                 recorded = kept[:, i]
             elif turn == 2:
                 recorded = outer[:, 2 * side - 1 - j]
             else:
                 recorded = data[turn // 2, rows - 1 - i if turn == 1 else i]
-            backed[turn, i] = lane_blur(recorded, predicted[turn, i], lane_back.at[turn])
+            backed[turn, j] = lane_blur(recorded, predicted[turn, i], lane_back.at[turn])
     factors = [
         row_taps_of(turn, view_of(turns, turn), row_taps, column_taps, 2 * side + 1) for turn in range(VIEWS)
     ]
-    high, low = depth_back[0], depth_back[1]
-    both = jnp.concatenate([high, low], axis=1)
-    results = []
-    for e in range(rows + 2 * side):
-        value = jnp.concatenate(
-            [spread_row(e, factors[turn], row_lists[turn], backed.at[turn]) for turn in range(VIEWS)], axis=0
-        )
-        s_high, s_low = split(value)
-        result = dot(both, jnp.concatenate([s_high, s_high], axis=0)) + dot(high, s_low)
-        if side <= e < side + rows:
-            middle[e - side] = result[:deep]
-        else:
-            results.append(result[:deep])
+    places = {i: j for j, i in enumerate(row_list)}
+    results = [
+        depth_blur(depth_back, [spread_row(e, factors[turn], places, backed.at[turn]) for turn in range(VIEWS)])[:deep]
+        for e in [*range(side), *range(rows + side, rows + 2 * side)]
+    ]
     odd = is_odd("gx")
     for i in range(side):
         first, last = results[i], results[side + i]
         even_pair[i] = jnp.where(odd, first, last)
         odd_pair[i] = jnp.where(odd, last, first)
+
+
+def project(turns, row_taps, column_taps, predicted, lane_back, depth_back, kept, data, outer_backed, middle, backed):
+    _, rows, depth, lanes = predicted.shape
+    deep = middle.shape[1]
+    side = outer_backed.shape[1] // 2
+    row_list = [*range(side), *range(rows - side, rows)]
+    for turn in range(VIEWS):
+        for j, i in enumerate(row_list):
+            backed[turn, i] = outer_backed[turn, j]
+        for i in range(side, rows - side):
+            if turn == 0:
+                recorded = kept[:, i]
+            elif turn == 2:
+                continue
+            else:
+                recorded = data[turn // 2, rows - 1 - i if turn == 1 else i]
+            backed[turn, i] = lane_blur(recorded, predicted[turn, i], lane_back.at[turn])
+    factors = [
+        row_taps_of(turn, view_of(turns, turn), row_taps, column_taps, 2 * side + 1) for turn in range(VIEWS)
+    ]
+    every, half = {i: i for i in range(rows)}, {i: i for i in row_list}
+    for e in range(rows):
+        parts = [
+            spread_row(e + side, factors[turn], half if turn == 2 else every, backed.at[turn]) for turn in range(VIEWS)
+        ]
+        middle[e] = depth_blur(depth_back, parts)[:deep]
 
 
 def project_half(turns, row_taps, column_taps, predicted, lane_back, half_back, flat, partial, middle, backed, inner):
@@ -295,7 +324,7 @@
     factor = row_taps_of(2, view_of(turns, 2), row_taps, column_taps, 2 * side + 1)
     back = half_back[...]
     for e in range(rows):
-        s_high, s_low = split(spread_row(e + side, factor, row_list, backed))
+        s_high, s_low = split(spread_row(e + side, factor, {i: i for i in row_list}, backed))
         result = dot(back, jnp.concatenate([s_high, s_high, s_low], axis=0))
         middle[e] = partial[e] + result[:deep]
 
@@ -353,7 +382,18 @@
     even_y, odd_y = pairs(lax.axis_size("gy"))
     even_x, odd_x = pairs(parts)
 
-    third, fourth = call(ends, (struct(reach, rows, lanes),) * 2, [VMEM])(estimate)
+    wide, chips = depth * rows, parts // 2
+    edge, second = call(edges, (struct(side, depth, lanes),) * 2, [VMEM])(estimate)
+    first, second = lax.ppermute(edge, "gx", even_x), lax.ppermute(second, "gx", odd_x)
+    kept, mine, theirs = call(
+        prepare,
+        (struct(depth, rows, lanes),) + (struct(chips, 2, rows, wide),) * 2,
+        [SMEM, SMEM, VMEM, ORDER],
+        [pltpu.VMEM((lanes, wide), F32)],
+    )(quarter_turns, offsets, recorded, first)
+    mirror = [(i, parts - 1 - i) for i in range(parts)]
+    swapped = lax.ppermute(theirs, "gx", [(i, i ^ 1) for i in range(parts)])
+    messages = call(merge, (struct(2, 2, rows, wide),) * (chips - 1), [VMEM] * 2)(mine, swapped)
     outer, inner = pl.pallas_call(
         pick,
         out_shape=(struct(depth, 2 * side, lanes), struct(depth, rows - 2 * side, lanes)),
@@ -371,32 +411,14 @@
         ),
         compiler_params=PARAMS,
         cost_estimate=COST,
-    )(quarter_turns, recorded, third)
-    wide, chips = depth * rows, parts // 2
-    kept, mine, theirs = call(
-        prepare,
-        (struct(depth, rows, lanes),) + (struct(chips, 2, rows, wide),) * 2,
-        [SMEM, SMEM, VMEM, ORDER],
-        [pltpu.VMEM((lanes, wide), F32)],
-    )(quarter_turns, offsets, recorded, outer)
+    )(quarter_turns, recorded, messages[0])
+    outer = lax.ppermute(outer, "gx", mirror)
+    third, fourth = call(layers_out, (struct((rows + 2 * side) * reach, lanes),) * 2, [VMEM] * 3)(estimate, first, second)
     third, fourth = lax.ppermute(third, "gy", even_y), lax.ppermute(fourth, "gy", odd_y)
-    mirror = [(i, parts - 1 - i) for i in range(parts)]
-    outer = lax.ppermute(outer, "gx", mirror)
-    swapped = lax.ppermute(theirs, "gx", [(i, i ^ 1) for i in range(parts)])
-    inner, *messages = call(
-        merge,
-        (struct(side * deep + 8, lanes),) + (struct(2, 2, rows, wide),) * (chips - 1),
-        [VMEM] * 3,
-    )(mine, swapped, inner)
     moved = {
         k: lax.ppermute(messages[k - 1], "gx", [(i, i ^ (2 * k)) for i in range(parts)])
         for k in range(chips - 1, 0, -1)
     }
-    inner = lax.ppermute(inner, "gx", mirror)
-    first, second = call(edges, (struct(side, deep, lanes),) * 2, [VMEM] * 3 + [ORDER] * 2)(
-        estimate, third, fourth, outer, messages[0]
-    )
-    first, second = lax.ppermute(first, "gx", even_x), lax.ppermute(second, "gx", odd_x)
 
     predicted, lane_back, depth_back, half_back = call(
         predict,
@@ -413,18 +435,22 @@
         ],
     )(quarter_turns, offsets, depth_taps, row_taps, column_taps, estimate, first, second, third, fourth)
 
-    middle, first, second = call(
-        project,
-        (struct(rows, deep, lanes), struct(side, deep, lanes), struct(side, deep, lanes)),
+    inner = call(hold, struct(side * deep + 8, lanes), [VMEM] + [ORDER] * (chips + 1))(inner, predicted, outer, *moved.values())
+    inner = lax.ppermute(inner, "gx", mirror)
+    first, second, data, backed = call(
+        project_sides,
+        (struct(side, deep, lanes),) * 2 + (struct(2, rows, depth, lanes), struct(VIEWS, 2 * side, depth, lanes)),
         [SMEM] * 3 + [VMEM] * (6 + chips),
-        [
-            pltpu.VMEM((parts, 2, rows, wide), F32),
-            pltpu.VMEM((2, rows, depth, lanes), F32),
-            pltpu.VMEM((VIEWS, rows, depth, lanes), F32),
-        ],
+        [pltpu.VMEM((parts, 2, rows, wide), F32)],
     )(quarter_turns, row_taps, column_taps, predicted, lane_back, depth_back, kept, outer, mine, swapped,
       *[moved[k] for k in range(1, chips)])
     first, second = lax.ppermute(first, "gx", even_x), lax.ppermute(second, "gx", odd_x)
+    middle = call(
+        project,
+        struct(rows, deep, lanes),
+        [SMEM] * 3 + [VMEM] * 6,
+        [pltpu.VMEM((VIEWS, rows, depth, lanes), F32)],
+    )(quarter_turns, row_taps, column_taps, predicted, lane_back, depth_back, kept, data, backed)
     middle = call(
         project_half,
         struct(rows, deep, lanes),

time: 61.8 us -> 52.6 us (0.85)
  waiting for transfers between devices: 28.5 us -> 18.1 us
  starting transfers between devices: 18.9 us -> 21.1 us
  local copies, waits for them, and re-layouts: 3.57 us -> 2.2 us
  Pallas kernels: 9.82 us -> 10.6 us
    ppermute x3, waiting for transfers between devices: 10.8 us -> 4.4 us  [shards(): lax.ppermute(messages[k - 1], 'gx', [(i, i ^ 2 * k) for i in range(parts)])]
    ppermute x1, waiting for transfers between devices: 7.36 us -> 1.72 us  [shards(): outer = lax.ppermute(outer, 'gx', mirror)]
    ppermute x2, waiting for transfers between devices: 4.22 us -> 8.88 us  [shards(): lax.ppermute(fourth, 'gy', odd_y)]
    ppermute x2, waiting for transfers between devices: 4.2 us -> 0.01 us  [shards(): lax.ppermute(second, 'gx', odd_x)]
    ppermute x2, starting transfers between devices: 3.95 us -> 5.43 us  [shards(): lax.ppermute(second, 'gx', odd_x)]
    unnamed x18, local copies, waits for them, and re-layouts: 3.57 us -> 2.2 us
    ppermute x1, starting transfers between devices: 0.07 us -> 1.22 us  [shards(): swapped = lax.ppermute(theirs, 'gx', [(i, i ^ 1) for i in range(parts)])]
    pallas_call x4 -> x6, Pallas kernels: 2.97 us -> 4 us  [the longest x1 1.91 us: shards(): call(project_sides, (struct(side, deep, lanes),) * 2 + (struct(2, rows, d...]
  transfers between devices with their start and end apart: 14 -> 14, of which waited for: 7 -> 7; matrix products, arithmetic and copies ran while one was open for 0% -> 0% of each run, Pallas kernels for 11% -> 18%
where the time goes in v4:
time: 52.6 us; the launch traced here: 52.2 us
  starting transfers between devices  21.1 us (40%)
  waiting for transfers between devices  18.1 us (34%)
  Pallas kernels  10.6 us (20%)
  local copies, waits for them, and re-layouts  2.2 us (4%)
    ppermute x2, waiting for transfers between devices, shards(): lax.ppermute(fourth, 'gy', odd_y)  8.88 us
    ppermute x2, starting transfers between devices, shards(): lax.ppermute(fourth, 'gy', odd_y)  6.73 us
    ppermute x2, starting transfers between devices, shards(): lax.ppermute(second, 'gx', odd_x)  5.43 us
    ppermute x3, waiting for transfers between devices, shards(): lax.ppermute(messages[k - 1], 'gx', [(i, i ^ 2 * k) for i in range(parts)])  4.4 us
    ppermute x3, starting transfers between devices, shards(): lax.ppermute(messages[k - 1], 'gx', [(i, i ^ 2 * k) for i in range(parts)])  3.83 us
    pallas_call x1, Pallas kernels, shards(): call(predict, (struct(VIEWS, rows, depth, lanes), struct(VIEWS, 2, lanes,...  2.89 us
    ppermute x2, waiting for transfers between devices, shards(): lax.ppermute(third, 'gy', even_y)  2.28 us
    unnamed x18, local copies, waits for them, and re-layouts  2.2 us
  transfers between devices with their start and end apart: 14, of which 7 were waited for; matrix products, arithmetic and copies ran while one was open for 0% of the time, Pallas kernels for 18%

profile of v4, /device:TPU:12, one launch (start us, length us, event | category | flops | bytes accessed | tf_op | source)
XLA Modules:
  0.0 52.2 jit_solution(6938452134072420278)
XLA Ops:
  0.0 0.0 copy-start.2
  0.0 0.9 %copy-done.2 = f32[32,16,128]{2,1,0:T(8,128)S(1)} copy-done((f32[32,16,128]{2,1,0:T(8,128)S(1)}, f32[32,16,128]{2,1,0:T(8,128)}, u32[]{:S(2)}) %copy-start.2) | copy-done | bytes 262168
  1.0 0.0 copy-start.3
  1.0 0.1 shard_map.73
  1.1 0.0 copy-start.6
  1.1 0.0 copy-start.7
  1.1 0.1 collective-permute-start
  1.2 2.4 %collective-permute-start.1 = (f32[4,32,128]{2,1,0:T(8,128)S(1)}, f32[4,32,128]{2,1,0:T(8,128)S(1)}, u32[]{:S(2)}, u32[]{:S(2)}) collective-permute-start(f32[4,32,128]{2,1,0:T(8,128)S(1)} %get-tuple-element.29), channel_id=1, source_target_pairs={{1,2},{2,1},{3,4},{4,3},{5,6},{6,5},{9,10},{10,9},{11,12},{12,11},... | collective-permute-start | bytes 196616 | tf_op jit(solution)/shard_map/ppermute | solution.py:387
  3.6 0.0 collective-permute-done.from_even.even_x.later
  3.6 0.0 copy-done.6
  3.7 0.0 copy-done.7
  3.7 0.0 copy-start
  3.7 1.2 %copy-done = f32[4,32,16,128]{3,2,1,0:T(8,128)S(1)} copy-done((f32[4,32,16,128]{3,2,1,0:T(8,128)S(1)}, f32[4,32,16,128]{3,2,1,0:T(8,128)}, u32[]{:S(2)}) %copy-start) | copy-done | bytes 1048600
  4.9 0.0 copy-start.1
  4.9 0.9 %shard_map.76 = (f32[32,16,128]{2,1,0:T(8,128)S(1)}, f32[4,2,16,512]{3,2,1,0:T(8,128)S(1)}, f32[4,2,16,512]{3,2,1,0:T(8,128)S(1)}) custom-call(s32[4]{0:T(128)S(1)} %copy-done.6, s32[4]{0:T(128)S(1)} %copy-done.7, f32[4,32,16,128]{3,2,1,0:T(8,128)S(1)} %copy-done, f32[4,32,128]{2,1,0:T(8,128)S(1)} %collective-permute-done.from_even.even_x.later), custom_call_target="tpu_custom_call" | custom-call | flops 1 | bytes 1 | tf_op jit(solution)/shard_map/pallas_call | solution.py:388
  5.8 1.2 %collective-permute-start.4 = (f32[4,2,16,512]{3,2,1,0:T(8,128)S(1)}, f32[4,2,16,512]{3,2,1,0:T(8,128)S(1)}, u32[]{:S(2)}, u32[]{:S(2)}) collective-permute-start(f32[4,2,16,512]{3,2,1,0:T(8,128)S(1)} %get-tuple-element.36), channel_id=1, source_target_pairs={{0,1},{1,0},{2,3},{3,2},{4,5},{5,4},{6,7},{7,6},{8,9},{9,8},{10,11... | collective-permute-start | bytes 786440 | tf_op jit(solution)/shard_map/ppermute | solution.py:395
  7.0 0.0 collective-permute-done.1.from_odd.odd_x
  7.1 0.0 copy-done.3
  7.1 0.3 shard_map.74
  7.3 1.6 %collective-permute-start.2 = (f32[480,128]{1,0:T(8,128)S(1)}, f32[480,128]{1,0:T(8,128)S(1)}, u32[]{:S(2)}, u32[]{:S(2)}) collective-permute-start(f32[480,128]{1,0:T(8,128)S(1)} %get-tuple-element.30), channel_id=1, source_target_pairs={{0,8},{8,0},{16,24},{24,16},{1,9},{9,1},{17,25},{25,17},{2,10},{10... | collective-permute-start | bytes 737288 | tf_op jit(solution)/shard_map/ppermute | solution.py:417
  8.9 2.4 %collective-permute-start.3 = (f32[480,128]{1,0:T(8,128)S(1)}, f32[480,128]{1,0:T(8,128)S(1)}, u32[]{:S(2)}, u32[]{:S(2)}) collective-permute-start(f32[480,128]{1,0:T(8,128)S(1)} %get-tuple-element.31), channel_id=1, source_target_pairs={{8,16},{16,8},{9,17},{17,9},{10,18},{18,10},{11,19},{19,11},{12,20... | collective-permute-start | bytes 737288 | tf_op jit(solution)/shard_map/ppermute | solution.py:417
  11.3 0.0 collective-permute-done.4.swapped
  11.3 1.6 %collective-permute-start.6 = (f32[2,2,16,512]{3,2,1,0:T(8,128)S(1)}, f32[2,2,16,512]{3,2,1,0:T(8,128)S(1)}, u32[]{:S(2)}, u32[]{:S(2)}) collective-permute-start(f32[2,2,16,512]{3,2,1,0:T(8,128)S(1)} %get-tuple-element.40), channel_id=1, source_target_pairs={{0,6},{1,7},{2,4},{3,5},{4,2},{5,3},{6,0},{7,1},{8,14},{9,15},{10,... | collective-permute-start | bytes 393224 | tf_op jit(solution)/shard_map/ppermute | solution.py:419
  12.9 1.2 %collective-permute-start.7 = (f32[2,2,16,512]{3,2,1,0:T(8,128)S(1)}, f32[2,2,16,512]{3,2,1,0:T(8,128)S(1)}, u32[]{:S(2)}, u32[]{:S(2)}) collective-permute-start(f32[2,2,16,512]{3,2,1,0:T(8,128)S(1)} %get-tuple-element.41), channel_id=1, source_target_pairs={{0,4},{1,5},{2,6},{3,7},{4,0},{5,1},{6,2},{7,3},{8,12},{9,13},{10,... | collective-permute-start | bytes 393224 | tf_op jit(solution)/shard_map/ppermute | solution.py:419
  14.2 1.0 %collective-permute-start.8 = (f32[2,2,16,512]{3,2,1,0:T(8,128)S(1)}, f32[2,2,16,512]{3,2,1,0:T(8,128)S(1)}, u32[]{:S(2)}, u32[]{:S(2)}) collective-permute-start(f32[2,2,16,512]{3,2,1,0:T(8,128)S(1)} %get-tuple-element.37.later), channel_id=1, source_target_pairs={{0,2},{1,3},{2,0},{3,1},{4,6},{5,7},{6,4},{7,5},{8,10},{9,11},{10,... | collective-permute-start | bytes 393224 | tf_op jit(solution)/shard_map/ppermute | solution.py:419
  15.1 0.0 copy-done.1
  15.1 0.0 copy-start.4
  15.1 0.0 copy-start.5
  15.1 0.0 copy-start.8
  15.1 0.6 %shard_map.78 = (f32[32,8,128]{2,1,0:T(8,128)S(1)}, f32[32,8,128]{2,1,0:T(8,128)S(1)}) custom-call(s32[4]{0:T(128)S(1)} %copy-done.6, f32[4,32,16,128]{3,2,1,0:T(8,128)S(1)} %copy-done.1, f32[2,2,16,512]{3,2,1,0:T(8,128)S(1)} %get-tuple-element.37.later), custom_call_target="tpu_custom_call" | custom-call | flops 1 | bytes 1 | tf_op jit(solution)/shard_map/pallas_call | solution.py:397
  15.7 0.0 collective-permute-done.2.even_y
  15.7 0.3 collective-permute-start.5
  16.0 4.7 %collective-permute-done.3.odd_y = f32[480,128]{1,0:T(8,128)S(1)} collective-permute-done((f32[480,128]{1,0:T(8,128)S(1)}, f32[480,128]{1,0:T(8,128)S(1)}, u32[]{:S(2)}, u32[]{:S(2)}) %collective-permute-start.3) | collective-permute-done | bytes 245792 | tf_op jit(solution)/shard_map/ppermute | solution.py:417
  20.6 0.0 copy-done.4
  20.7 0.0 copy-done.5
  20.7 0.0 copy-done.8
  20.7 2.9 %shard_map.75 = (f32[4,16,32,128]{3,2,1,0:T(8,128)S(1)}, bf16[4,2,128,128]{3,2,1,0:T(8,128)(2,1)S(1)}, bf16[2,80,128]{2,1,0:T(8,128)(2,1)S(1)}, bf16[80,96]{1,0:T(8,128)(2,1)S(1)}) custom-call(s32[4]{0:T(128)S(1)} %copy-done.6, s32[4]{0:T(128)S(1)} %copy-done.7, f32[4,41]{1,0:T(4,128)S(1)} %copy-done.8, f32[4,9]{1,0:T(4,128)S(1)} %copy-done.4, ...), custom_call_target="tpu_custom_call" | custom-call | flops 1 | bytes 1 | tf_op jit(solution)/shard_map/pallas_call | solution.py:423
  23.6 2.0 %collective-permute-done.6.rest_2_ = f32[2,2,16,512]{3,2,1,0:T(8,128)S(1)} collective-permute-done((f32[2,2,16,512]{3,2,1,0:T(8,128)S(1)}, f32[2,2,16,512]{3,2,1,0:T(8,128)S(1)}, u32[]{:S(2)}, u32[]{:S(2)}) %collective-permute-start.6) | collective-permute-done | bytes 131104 | tf_op jit(solution)/shard_map/ppermute | solution.py:419
  25.6 2.4 %collective-permute-done.7.rest_3_.rest_1_ = f32[2,2,16,512]{3,2,1,0:T(8,128)S(1)} collective-permute-done((f32[2,2,16,512]{3,2,1,0:T(8,128)S(1)}, f32[2,2,16,512]{3,2,1,0:T(8,128)S(1)}, u32[]{:S(2)}, u32[]{:S(2)}) %collective-permute-start.7) | collective-permute-done | bytes 131104 | tf_op jit(solution)/shard_map/ppermute | solution.py:419
  28.0 0.0 collective-permute-done.8.rest_4_.rest_0_
  28.0 1.7 %collective-permute-done.5.rest_1_.outer = f32[32,8,128]{2,1,0:T(8,128)S(1)} collective-permute-done((f32[32,8,128]{2,1,0:T(8,128)S(1)}, f32[32,8,128]{2,1,0:T(8,128)S(1)}, u32[]{:S(2)}, u32[]{:S(2)}) %collective-permute-start.5) | collective-permute-done | bytes 131104 | tf_op jit(solution)/shard_map/ppermute | solution.py:415
  29.7 1.8 %collective-permute-start.9 = (f32[296,128]{1,0:T(8,128)S(1)}, f32[296,128]{1,0:T(8,128)S(1)}, u32[]{:S(2)}, u32[]{:S(2)}) collective-permute-start(f32[296,128]{1,0:T(8,128)S(1)} %shard_map.79), channel_id=1, source_target_pairs={{0,7},{1,6},{2,5},{3,4},{4,3},{5,2},{6,1},{7,0},{8,15},{9,14},{10,... | collective-permute-start | bytes 454664 | tf_op jit(solution)/shard_map/ppermute | solution.py:439
  31.5 1.9 %shard_map.80 = (f32[4,72,128]{2,1,0:T(8,128)S(1)}, f32[4,72,128]{2,1,0:T(8,128)S(1)}, f32[2,16,32,128]{3,2,1,0:T(8,128)S(1)}, f32[4,8,32,128]{3,2,1,0:T(8,128)S(1)}) custom-call(s32[4]{0:T(128)S(1)} %copy-done.6, f32[4,9]{1,0:T(4,128)S(1)} %copy-done.4, f32[4,9]{1,0:T(4,128)S(1)} %copy-done.5, f32[4,16,32,128]{3,2,1,0:T(8,128)S(1)} %get-tuple-element.32.rest_0_.predicted, ...), custom_call_target="tpu_custom_call" | custom-call | flops 1 | bytes 1 | tf_op jit(solution)/shard_map/pallas_call | solution.py:440
  33.5 0.1 collective-permute-start.10
  33.5 3.0 %collective-permute-start.11 = (f32[4,72,128]{2,1,0:T(8,128)S(1)}, f32[4,72,128]{2,1,0:T(8,128)S(1)}, u32[]{:S(2)}, u32[]{:S(2)}) collective-permute-start(f32[4,72,128]{2,1,0:T(8,128)S(1)} %get-tuple-element.47), channel_id=1, source_target_pairs={{1,2},{2,1},{3,4},{4,3},{5,6},{6,5},{9,10},{10,9},{11,12},{12,11},... | collective-permute-start | bytes 442376 | tf_op jit(solution)/shard_map/ppermute | solution.py:447
  36.5 1.7 %shard_map.81.partial = f32[16,72,128]{2,1,0:T(8,128)S(1)} custom-call(s32[4]{0:T(128)S(1)} %copy-done.6, f32[4,9]{1,0:T(4,128)S(1)} %copy-done.4, f32[4,9]{1,0:T(4,128)S(1)} %copy-done.5, f32[4,16,32,128]{3,2,1,0:T(8,128)S(1)} %get-tuple-element.32.rest_0_.predicted, bf16[4,2,128,128]{3,2,1,0:T(8,128)(2,1)S(1)} %get-tuple-element.33.lane_back, ...), custom_call_target="tpu_custom_call" | custom-call | flops 1 | bytes 1 | tf_op jit(solution)/shard_map/pallas_call | solution.py:448
  38.2 0.8 %collective-permute-done.9.flat = f32[296,128]{1,0:T(8,128)S(1)} collective-permute-done((f32[296,128]{1,0:T(8,128)S(1)}, f32[296,128]{1,0:T(8,128)S(1)}, u32[]{:S(2)}, u32[]{:S(2)}) %collective-permute-start.9) | collective-permute-done | bytes 151584 | tf_op jit(solution)/shard_map/ppermute | solution.py:439
  39.0 1.1 %shard_map.82.middle = f32[16,72,128]{2,1,0:T(8,128)S(1)} custom-call(s32[4]{0:T(128)S(1)} %copy-done.6, f32[4,9]{1,0:T(4,128)S(1)} %copy-done.4, f32[4,9]{1,0:T(4,128)S(1)} %copy-done.5, f32[4,16,32,128]{3,2,1,0:T(8,128)S(1)} %get-tuple-element.32.rest_0_.predicted, bf16[4,2,128,128]{3,2,1,0:T(8,128)(2,1)S(1)} %get-tuple-element.33.lane_back, ...), custom_call_target="tpu_custom_call" | custom-call | flops 1 | bytes 1 | tf_op jit(solution)/shard_map/pallas_call | solution.py:454
  40.1 0.0 collective-permute-done.10.even_x
  40.1 0.0 collective-permute-done.11.odd_x
  40.1 0.1 shard_map.83
  40.2 0.1 collective-permute-start.12
  40.3 4.4 %collective-permute-start.13 = (f32[320,128]{1,0:T(8,128)S(1)}, f32[320,128]{1,0:T(8,128)S(1)}, u32[]{:S(2)}, u32[]{:S(2)}) collective-permute-start(f32[320,128]{1,0:T(8,128)S(1)} %get-tuple-element.50), channel_id=1, source_target_pairs={{8,16},{16,8},{9,17},{17,9},{10,18},{18,10},{11,19},{19,11},{12,20... | collective-permute-start | bytes 491528 | tf_op jit(solution)/shard_map/ppermute | solution.py:465
  44.6 2.3 %collective-permute-done.12.even_y = f32[320,128]{1,0:T(8,128)S(1)} collective-permute-done((f32[320,128]{1,0:T(8,128)S(1)}, f32[320,128]{1,0:T(8,128)S(1)}, u32[]{:S(2)}, u32[]{:S(2)}) %collective-permute-start.12) | collective-permute-done | bytes 163872 | tf_op jit(solution)/shard_map/ppermute | solution.py:465
  46.9 4.2 %collective-permute-done.13.odd_y = f32[320,128]{1,0:T(8,128)S(1)} collective-permute-done((f32[320,128]{1,0:T(8,128)S(1)}, f32[320,128]{1,0:T(8,128)S(1)}, u32[]{:S(2)}, u32[]{:S(2)}) %collective-permute-start.13) | collective-permute-done | bytes 163872 | tf_op jit(solution)/shard_map/ppermute | solution.py:465
  51.1 1.0 %shard_map.84 = f32[32,16,128]{2,1,0:T(8,128)} custom-call(f32[32,16,128]{2,1,0:T(8,128)S(1)} %copy-done.3, f32[16,32,128]{2,1,0:T(8,128)S(1)} %get-tuple-element.48.own, f32[320,128]{1,0:T(8,128)S(1)} %collective-permute-done.12.even_y, f32[320,128]{1,0:T(8,128)S(1)} %collective-permute-done.13.odd_y), custom_call_target="tpu_custom_call" | custom-call | flops 1 | bytes 1 | tf_op jit(solution)/shard_map/pallas_call | solution.py:466
  (2 shorter events, 0.0 us)
Async XLA Ops:
  0.0 0.9 %copy-start.2 = (f32[32,16,128]{2,1,0:T(8,128)S(1)}, f32[32,16,128]{2,1,0:T(8,128)}, u32[]{:S(2)}) copy-start(f32[32,16,128]{2,1,0:T(8,128)} %estimate.1) | copy-start | bytes 786436
  1.0 6.1 %copy-start.3 = (f32[32,16,128]{2,1,0:T(8,128)S(1)}, f32[32,16,128]{2,1,0:T(8,128)}, u32[]{:S(2)}) copy-start(f32[32,16,128]{2,1,0:T(8,128)} %estimate.1) | copy-start | bytes 786436
  1.1 2.6 %copy-start.6 = (s32[4]{0:T(128)S(1)}, s32[4]{0:T(128)}, u32[]{:S(2)}) copy-start(s32[4]{0:T(128)} %turns.11) | copy-start | bytes 52
  1.1 2.6 %copy-start.7 = (s32[4]{0:T(128)S(1)}, s32[4]{0:T(128)}, u32[]{:S(2)}) copy-start(s32[4]{0:T(128)} %offsets.3) | copy-start | bytes 52
  1.1 2.5 %collective-permute-start = (f32[4,32,128]{2,1,0:T(8,128)S(1)}, f32[4,32,128]{2,1,0:T(8,128)S(1)}, u32[]{:S(2)}, u32[]{:S(2)}) collective-permute-start(f32[4,32,128]{2,1,0:T(8,128)S(1)} %get-tuple-element.28), channel_id=1, source_target_pairs={{0,1},{1,0},{2,3},{3,2},{4,5},{5,4},{6,7},{7,6},{8,9},{9,8},{10,11... | collective-permute-start | bytes 196616 | tf_op jit(solution)/shard_map/ppermute | solution.py:387
  1.2 5.9 %collective-permute-start.1 = (f32[4,32,128]{2,1,0:T(8,128)S(1)}, f32[4,32,128]{2,1,0:T(8,128)S(1)}, u32[]{:S(2)}, u32[]{:S(2)}) collective-permute-start(f32[4,32,128]{2,1,0:T(8,128)S(1)} %get-tuple-element.29), channel_id=1, source_target_pairs={{1,2},{2,1},{3,4},{4,3},{5,6},{6,5},{9,10},{10,9},{11,12},{12,11},... | collective-permute-start | bytes 196616 | tf_op jit(solution)/shard_map/ppermute | solution.py:387
  3.7 1.2 %copy-start = (f32[4,32,16,128]{3,2,1,0:T(8,128)S(1)}, f32[4,32,16,128]{3,2,1,0:T(8,128)}, u32[]{:S(2)}) copy-start(f32[4,32,16,128]{3,2,1,0:T(8,128)} %recorded.3) | copy-start | bytes 3145732
  4.9 10.2 %copy-start.1 = (f32[4,32,16,128]{3,2,1,0:T(8,128)S(1)}, f32[4,32,16,128]{3,2,1,0:T(8,128)}, u32[]{:S(2)}) copy-start(f32[4,32,16,128]{3,2,1,0:T(8,128)} %recorded.3) | copy-start | bytes 3145732
  5.8 5.4 %collective-permute-start.4 = (f32[4,2,16,512]{3,2,1,0:T(8,128)S(1)}, f32[4,2,16,512]{3,2,1,0:T(8,128)S(1)}, u32[]{:S(2)}, u32[]{:S(2)}) collective-permute-start(f32[4,2,16,512]{3,2,1,0:T(8,128)S(1)} %get-tuple-element.36), channel_id=1, source_target_pairs={{0,1},{1,0},{2,3},{3,2},{4,5},{5,4},{6,7},{7,6},{8,9},{9,8},{10,11... | collective-permute-start | bytes 786440 | tf_op jit(solution)/shard_map/ppermute | solution.py:395
  7.3 8.4 %collective-permute-start.2 = (f32[480,128]{1,0:T(8,128)S(1)}, f32[480,128]{1,0:T(8,128)S(1)}, u32[]{:S(2)}, u32[]{:S(2)}) collective-permute-start(f32[480,128]{1,0:T(8,128)S(1)} %get-tuple-element.30), channel_id=1, source_target_pairs={{0,8},{8,0},{16,24},{24,16},{1,9},{9,1},{17,25},{25,17},{2,10},{10... | collective-permute-start | bytes 737288 | tf_op jit(solution)/shard_map/ppermute | solution.py:417
  8.9 11.8 %collective-permute-start.3 = (f32[480,128]{1,0:T(8,128)S(1)}, f32[480,128]{1,0:T(8,128)S(1)}, u32[]{:S(2)}, u32[]{:S(2)}) collective-permute-start(f32[480,128]{1,0:T(8,128)S(1)} %get-tuple-element.31), channel_id=1, source_target_pairs={{8,16},{16,8},{9,17},{17,9},{10,18},{18,10},{11,19},{19,11},{12,20... | collective-permute-start | bytes 737288 | tf_op jit(solution)/shard_map/ppermute | solution.py:417
  11.3 14.3 %collective-permute-start.6 = (f32[2,2,16,512]{3,2,1,0:T(8,128)S(1)}, f32[2,2,16,512]{3,2,1,0:T(8,128)S(1)}, u32[]{:S(2)}, u32[]{:S(2)}) collective-permute-start(f32[2,2,16,512]{3,2,1,0:T(8,128)S(1)} %get-tuple-element.40), channel_id=1, source_target_pairs={{0,6},{1,7},{2,4},{3,5},{4,2},{5,3},{6,0},{7,1},{8,14},{9,15},{10,... | collective-permute-start | bytes 393224 | tf_op jit(solution)/shard_map/ppermute | solution.py:419
  12.9 15.0 %collective-permute-start.7 = (f32[2,2,16,512]{3,2,1,0:T(8,128)S(1)}, f32[2,2,16,512]{3,2,1,0:T(8,128)S(1)}, u32[]{:S(2)}, u32[]{:S(2)}) collective-permute-start(f32[2,2,16,512]{3,2,1,0:T(8,128)S(1)} %get-tuple-element.41), channel_id=1, source_target_pairs={{0,4},{1,5},{2,6},{3,7},{4,0},{5,1},{6,2},{7,3},{8,12},{9,13},{10,... | collective-permute-start | bytes 393224 | tf_op jit(solution)/shard_map/ppermute | solution.py:419
  14.2 13.8 %collective-permute-start.8 = (f32[2,2,16,512]{3,2,1,0:T(8,128)S(1)}, f32[2,2,16,512]{3,2,1,0:T(8,128)S(1)}, u32[]{:S(2)}, u32[]{:S(2)}) collective-permute-start(f32[2,2,16,512]{3,2,1,0:T(8,128)S(1)} %get-tuple-element.37.later), channel_id=1, source_target_pairs={{0,2},{1,3},{2,0},{3,1},{4,6},{5,7},{6,4},{7,5},{8,10},{9,11},{10,... | collective-permute-start | bytes 393224 | tf_op jit(solution)/shard_map/ppermute | solution.py:419
  15.1 5.5 %copy-start.4 = (f32[4,9]{1,0:T(4,128)S(1)}, f32[4,9]{1,0:T(4,128)}, u32[]{:S(2)}) copy-start(f32[4,9]{1,0:T(4,128)} %row_taps.7) | copy-start | bytes 436
  15.1 5.5 %copy-start.5 = (f32[4,9]{1,0:T(4,128)S(1)}, f32[4,9]{1,0:T(4,128)}, u32[]{:S(2)}) copy-start(f32[4,9]{1,0:T(4,128)} %column_taps.7) | copy-start | bytes 436
  15.1 5.5 %copy-start.8 = (f32[4,41]{1,0:T(4,128)S(1)}, f32[4,41]{1,0:T(4,128)}, u32[]{:S(2)}) copy-start(f32[4,41]{1,0:T(4,128)} %depth_taps.1) | copy-start | bytes 1972
  15.7 13.9 %collective-permute-start.5 = (f32[32,8,128]{2,1,0:T(8,128)S(1)}, f32[32,8,128]{2,1,0:T(8,128)S(1)}, u32[]{:S(2)}, u32[]{:S(2)}) collective-permute-start(f32[32,8,128]{2,1,0:T(8,128)S(1)} %get-tuple-element.39), channel_id=1, source_target_pairs={{0,7},{1,6},{2,5},{3,4},{4,3},{5,2},{6,1},{7,0},{8,15},{9,14},{10,... | collective-permute-start | bytes 393224 | tf_op jit(solution)/shard_map/ppermute | solution.py:415
  29.7 9.3 %collective-permute-start.9 = (f32[296,128]{1,0:T(8,128)S(1)}, f32[296,128]{1,0:T(8,128)S(1)}, u32[]{:S(2)}, u32[]{:S(2)}) collective-permute-start(f32[296,128]{1,0:T(8,128)S(1)} %shard_map.79), channel_id=1, source_target_pairs={{0,7},{1,6},{2,5},{3,4},{4,3},{5,2},{6,1},{7,0},{8,15},{9,14},{10,... | collective-permute-start | bytes 454664 | tf_op jit(solution)/shard_map/ppermute | solution.py:439
  33.5 6.7 %collective-permute-start.10 = (f32[4,72,128]{2,1,0:T(8,128)S(1)}, f32[4,72,128]{2,1,0:T(8,128)S(1)}, u32[]{:S(2)}, u32[]{:S(2)}) collective-permute-start(f32[4,72,128]{2,1,0:T(8,128)S(1)} %get-tuple-element.46), channel_id=1, source_target_pairs={{0,1},{1,0},{2,3},{3,2},{4,5},{5,4},{6,7},{7,6},{8,9},{9,8},{10,11... | collective-permute-start | bytes 442376 | tf_op jit(solution)/shard_map/ppermute | solution.py:447
  33.5 6.6 %collective-permute-start.11 = (f32[4,72,128]{2,1,0:T(8,128)S(1)}, f32[4,72,128]{2,1,0:T(8,128)S(1)}, u32[]{:S(2)}, u32[]{:S(2)}) collective-permute-start(f32[4,72,128]{2,1,0:T(8,128)S(1)} %get-tuple-element.47), channel_id=1, source_target_pairs={{1,2},{2,1},{3,4},{4,3},{5,6},{6,5},{9,10},{10,9},{11,12},{12,11},... | collective-permute-start | bytes 442376 | tf_op jit(solution)/shard_map/ppermute | solution.py:447
  40.2 6.7 %collective-permute-start.12 = (f32[320,128]{1,0:T(8,128)S(1)}, f32[320,128]{1,0:T(8,128)S(1)}, u32[]{:S(2)}, u32[]{:S(2)}) collective-permute-start(f32[320,128]{1,0:T(8,128)S(1)} %get-tuple-element.49), channel_id=1, source_target_pairs={{0,8},{8,0},{16,24},{24,16},{1,9},{9,1},{17,25},{25,17},{2,10},{10... | collective-permute-start | bytes 491528 | tf_op jit(solution)/shard_map/ppermute | solution.py:465
  40.3 10.9 %collective-permute-start.13 = (f32[320,128]{1,0:T(8,128)S(1)}, f32[320,128]{1,0:T(8,128)S(1)}, u32[]{:S(2)}, u32[]{:S(2)}) collective-permute-start(f32[320,128]{1,0:T(8,128)S(1)} %get-tuple-element.50), channel_id=1, source_target_pairs={{8,16},{16,8},{9,17},{17,9},{10,18},{18,10},{11,19},{19,11},{12,20... | collective-permute-start | bytes 491528 | tf_op jit(solution)/shard_map/ppermute | solution.py:465

commit v5 on v4

--- a/solution.py
+++ b/solution.py
@@ -124,7 +124,7 @@
     return [source[view, width - 1 - s if flipped else s] for s in range(width)]
 
 
-def predict(turns, offsets, depth_taps, row_taps, column_taps, own, even_x, odd_x, even_y, odd_y,
+def predict(turns, offsets, depth_taps, row_taps, column_taps, own, even_x, odd_x, even_y, odd_y, later,
             predicted, lane_back, depth_back, half_back, extended, blurred):
     depth, rows, lanes = own.shape
     side = even_x.shape[0]
@@ -198,7 +198,12 @@
             predicted[turn, i] = dot(jnp.concatenate([t_high, t_low], axis=1), both) + dot(t_high, low)
 
 
-def turned(mine, swapped, received, arrived, data):
+def gate(*rest):
+    rest[-1][...] = jnp.zeros(rest[-1].shape, F32)
+
+
+def turned(mine, swapped, *rest):
+    received, (data, arrived) = rest[:-2], rest[-2:]
     parts, _, rows, wide = arrived.shape
     group = LANES // rows
     me = lax.axis_index("gx")
@@ -256,11 +261,9 @@
     return jnp.zeros(backed.shape[1:], F32) if total is None else total
 
 
-def project_sides(turns, row_taps, column_taps, predicted, lane_back, depth_back, kept, outer, mine, swapped, *rest):
-    received, (even_pair, odd_pair, data, backed, arrived) = rest[:-5], rest[-5:]
+def project_sides(turns, row_taps, column_taps, predicted, lane_back, depth_back, kept, outer, data, even_pair, odd_pair, backed):
     _, rows, depth, lanes = predicted.shape
     side, deep, _ = even_pair.shape
-    turned(mine, swapped, received, arrived, data)
     row_list = [*range(side), *range(rows - side, rows)]
     for turn in range(VIEWS):
         for j, i in enumerate(row_list):
@@ -420,6 +423,15 @@
         for k in range(chips - 1, 0, -1)
     }
 
+    arrivals = list(moved.values())
+    passed = call(gate, struct(8, LANES), [ORDER] * len(arrivals))(*arrivals)
+    data = call(
+        turned,
+        struct(2, rows, depth, lanes),
+        [VMEM] * (1 + chips),
+        [pltpu.VMEM((parts, 2, rows, wide), F32)],
+    )(mine, swapped, *[moved[k] for k in range(1, chips)])
+
     predicted, lane_back, depth_back, half_back = call(
         predict,
         (
@@ -428,22 +440,20 @@
             struct(2, padded, VIEWS * depth, dtype=BF16),
             struct(padded, 3 * depth, dtype=BF16),
         ),
-        [SMEM] * 5 + [VMEM] * 5,
+        [SMEM] * 5 + [VMEM] * 5 + [ORDER],
         [
             pltpu.VMEM((rows + 2 * side, padded, lanes), F32),
             pltpu.VMEM((rows + 2 * side, VIEWS * depth, lanes), F32),
         ],
-    )(quarter_turns, offsets, depth_taps, row_taps, column_taps, estimate, first, second, third, fourth)
-
-    inner = call(hold, struct(side * deep + 8, lanes), [VMEM] + [ORDER] * (chips + 1))(inner, predicted, outer, *moved.values())
+    )(quarter_turns, offsets, depth_taps, row_taps, column_taps, estimate, first, second, third, fourth, passed)
+
+    inner = call(hold, struct(side * deep + 8, lanes), [VMEM] + [ORDER] * 2)(inner, predicted, outer)
     inner = lax.ppermute(inner, "gx", mirror)
-    first, second, data, backed = call(
+    first, second, backed = call(
         project_sides,
-        (struct(side, deep, lanes),) * 2 + (struct(2, rows, depth, lanes), struct(VIEWS, 2 * side, depth, lanes)),
-        [SMEM] * 3 + [VMEM] * (6 + chips),
-        [pltpu.VMEM((parts, 2, rows, wide), F32)],
-    )(quarter_turns, row_taps, column_taps, predicted, lane_back, depth_back, kept, outer, mine, swapped,
-      *[moved[k] for k in range(1, chips)])
+        (struct(side, deep, lanes),) * 2 + (struct(VIEWS, 2 * side, depth, lanes),),
+        [SMEM] * 3 + [VMEM] * 6,
+    )(quarter_turns, row_taps, column_taps, predicted, lane_back, depth_back, kept, outer, data)
     first, second = lax.ppermute(first, "gx", even_x), lax.ppermute(second, "gx", odd_x)
     middle = call(
         project,

time: 52.6 us -> 51.3 us (0.975)
  waiting for transfers between devices: 18.1 us -> 15 us
  Pallas kernels: 10.6 us -> 11.7 us
    ppermute x2, waiting for transfers between devices: 8.88 us -> 4.22 us  [shards(): lax.ppermute(fourth, 'gy', odd_y)]
    ppermute x3, waiting for transfers between devices: 4.4 us -> 6.43 us  [shards(): lax.ppermute(messages[k - 1], 'gx', [(i, i ^ 2 * k) for i in range(parts)])]
    ppermute x2, starting transfers between devices: 1.63 us -> 3.5 us  [shards(): lax.ppermute(third, 'gy', even_y)]
    ppermute x1, waiting for transfers between devices: 1.72 us -> 0.01 us  [shards(): outer = lax.ppermute(outer, 'gx', mirror)]
    ppermute x2, waiting for transfers between devices: 0.01 us -> 1.58 us  [shards(): lax.ppermute(second, 'gx', odd_x)]
    ppermute x2, starting transfers between devices: 6.73 us -> 5.32 us  [shards(): lax.ppermute(fourth, 'gy', odd_y)]
    ppermute x1, waiting for transfers between devices: 0.01 us -> 1.24 us  [shards(): lax.ppermute(edge, 'gx', even_x)]
    pallas_call x2 -> x4, Pallas kernels: 1.92 us -> 3.04 us  [the longest x1 1.56 us: shards(): call(project_sides, (struct(side, deep, lanes),) * 2 + (struct(VIEWS, 2 *...]
  transfers between devices with their start and end apart: 14 -> 14, of which waited for: 7 -> 6; matrix products, arithmetic and copies ran while one was open for 0% -> 0% of each run, Pallas kernels for 18% -> 19%
where the time goes in v5:
time: 51.3 us; the launch traced here: 50.8 us
  starting transfers between devices  21.6 us (42%)
  waiting for transfers between devices  15 us (29%)
  Pallas kernels  11.7 us (23%)
  local copies, waits for them, and re-layouts  2.22 us (4%)
    ppermute x3, waiting for transfers between devices, shards(): lax.ppermute(messages[k - 1], 'gx', [(i, i ^ 2 * k) for i in range(parts)])  6.43 us
    ppermute x2, starting transfers between devices, shards(): lax.ppermute(second, 'gx', odd_x)  6.18 us
    ppermute x2, starting transfers between devices, shards(): lax.ppermute(fourth, 'gy', odd_y)  5.32 us
    ppermute x3, starting transfers between devices, shards(): lax.ppermute(messages[k - 1], 'gx', [(i, i ^ 2 * k) for i in range(parts)])  4.74 us
    ppermute x2, waiting for transfers between devices, shards(): lax.ppermute(fourth, 'gy', odd_y)  4.22 us
    ppermute x2, starting transfers between devices, shards(): lax.ppermute(third, 'gy', even_y)  3.5 us
    pallas_call x1, Pallas kernels, shards(): call(predict, (struct(VIEWS, rows, depth, lanes), struct(VIEWS, 2, lanes,...  2.88 us
    unnamed x18, local copies, waits for them, and re-layouts  2.22 us
  transfers between devices with their start and end apart: 14, of which 6 were waited for; matrix products, arithmetic and copies ran while one was open for 0% of the time, Pallas kernels for 19%

profile of v5, /device:TPU:12, one launch (start us, length us, event | category | flops | bytes accessed | tf_op | source)
XLA Modules:
  0.0 50.8 jit_solution(4424800003209840080)
XLA Ops:
  0.0 0.0 copy-start.2
  0.0 0.9 %copy-done.2 = f32[32,16,128]{2,1,0:T(8,128)S(1)} copy-done((f32[32,16,128]{2,1,0:T(8,128)S(1)}, f32[32,16,128]{2,1,0:T(8,128)}, u32[]{:S(2)}) %copy-start.2) | copy-done | bytes 262168
  1.0 0.1 shard_map.73
  1.1 0.0 copy-start.6
  1.1 0.0 copy-start.7
  1.1 0.1 collective-permute-start
  1.2 1.2 %collective-permute-done.from_even.later.even_x = f32[4,32,128]{2,1,0:T(8,128)S(1)} collective-permute-done((f32[4,32,128]{2,1,0:T(8,128)S(1)}, f32[4,32,128]{2,1,0:T(8,128)S(1)}, u32[]{:S(2)}, u32[]{:S(2)}) %collective-permute-start) | collective-permute-done | bytes 65568 | tf_op jit(solution)/shard_map/ppermute | solution.py:390
  2.4 0.0 copy-done.6
  2.4 0.0 copy-done.7
  2.4 0.0 copy-start
  2.4 1.2 %copy-done = f32[4,32,16,128]{3,2,1,0:T(8,128)S(1)} copy-done((f32[4,32,16,128]{3,2,1,0:T(8,128)S(1)}, f32[4,32,16,128]{3,2,1,0:T(8,128)}, u32[]{:S(2)}) %copy-start) | copy-done | bytes 1048600
  3.6 0.0 copy-start.1
  3.6 0.9 %shard_map.75 = (f32[32,16,128]{2,1,0:T(8,128)S(1)}, f32[4,2,16,512]{3,2,1,0:T(8,128)S(1)}, f32[4,2,16,512]{3,2,1,0:T(8,128)S(1)}) custom-call(s32[4]{0:T(128)S(1)} %copy-done.6, s32[4]{0:T(128)S(1)} %copy-done.7, f32[4,32,16,128]{3,2,1,0:T(8,128)S(1)} %copy-done, f32[4,32,128]{2,1,0:T(8,128)S(1)} %collective-permute-done.from_even.later.even_x), custom_call_target="tpu_custom_call" | custom-call | flops 1 | bytes 1 | tf_op jit(solution)/shard_map/pallas_call | solution.py:391
  4.6 0.2 collective-permute-start.4
  4.8 2.3 %collective-permute-start.1 = (f32[4,32,128]{2,1,0:T(8,128)S(1)}, f32[4,32,128]{2,1,0:T(8,128)S(1)}, u32[]{:S(2)}, u32[]{:S(2)}) collective-permute-start(f32[4,32,128]{2,1,0:T(8,128)S(1)} %get-tuple-element.28), channel_id=1, source_target_pairs={{1,2},{2,1},{3,4},{4,3},{5,6},{6,5},{9,10},{10,9},{11,12},{12,11},... | collective-permute-start | bytes 196616 | tf_op jit(solution)/shard_map/ppermute | solution.py:390
  7.1 0.0 collective-permute-done.4.swapped
  7.1 0.0 copy-start.3
  7.2 1.6 %collective-permute-start.5 = (f32[2,2,16,512]{3,2,1,0:T(8,128)S(1)}, f32[2,2,16,512]{3,2,1,0:T(8,128)S(1)}, u32[]{:S(2)}, u32[]{:S(2)}) collective-permute-start(f32[2,2,16,512]{3,2,1,0:T(8,128)S(1)} %get-tuple-element.33), channel_id=1, source_target_pairs={{0,6},{1,7},{2,4},{3,5},{4,2},{5,3},{6,0},{7,1},{8,14},{9,15},{10,... | collective-permute-start | bytes 393224 | tf_op jit(solution)/shard_map/ppermute | solution.py:422
  8.8 1.6 %collective-permute-done.1.from_odd.odd_x = f32[4,32,128]{2,1,0:T(8,128)S(1)} collective-permute-done((f32[4,32,128]{2,1,0:T(8,128)S(1)}, f32[4,32,128]{2,1,0:T(8,128)S(1)}, u32[]{:S(2)}, u32[]{:S(2)}) %collective-permute-start.1) | collective-permute-done | bytes 65568 | tf_op jit(solution)/shard_map/ppermute | solution.py:390
  10.4 0.0 copy-done.3
  10.4 0.3 shard_map.74
  10.7 1.6 %collective-permute-start.2 = (f32[480,128]{1,0:T(8,128)S(1)}, f32[480,128]{1,0:T(8,128)S(1)}, u32[]{:S(2)}, u32[]{:S(2)}) collective-permute-start(f32[480,128]{1,0:T(8,128)S(1)} %get-tuple-element.29), channel_id=1, source_target_pairs={{0,8},{8,0},{16,24},{24,16},{1,9},{9,1},{17,25},{25,17},{2,10},{10... | collective-permute-start | bytes 737288 | tf_op jit(solution)/shard_map/ppermute | solution.py:420
  12.2 2.4 %collective-permute-start.3 = (f32[480,128]{1,0:T(8,128)S(1)}, f32[480,128]{1,0:T(8,128)S(1)}, u32[]{:S(2)}, u32[]{:S(2)}) collective-permute-start(f32[480,128]{1,0:T(8,128)S(1)} %get-tuple-element.30), channel_id=1, source_target_pairs={{8,16},{16,8},{9,17},{17,9},{10,18},{18,10},{11,19},{19,11},{12,20... | collective-permute-start | bytes 737288 | tf_op jit(solution)/shard_map/ppermute | solution.py:420
  14.6 2.7 %collective-permute-start.6 = (f32[2,2,16,512]{3,2,1,0:T(8,128)S(1)}, f32[2,2,16,512]{3,2,1,0:T(8,128)S(1)}, u32[]{:S(2)}, u32[]{:S(2)}) collective-permute-start(f32[2,2,16,512]{3,2,1,0:T(8,128)S(1)} %get-tuple-element.34), channel_id=1, source_target_pairs={{0,4},{1,5},{2,6},{3,7},{4,0},{5,1},{6,2},{7,3},{8,12},{9,13},{10,... | collective-permute-start | bytes 393224 | tf_op jit(solution)/shard_map/ppermute | solution.py:422
  17.2 0.4 collective-permute-start.7
  17.7 0.0 copy-done.1
  17.7 0.6 %shard_map.79 = (f32[32,8,128]{2,1,0:T(8,128)S(1)}, f32[32,8,128]{2,1,0:T(8,128)S(1)}) custom-call(s32[4]{0:T(128)S(1)} %copy-done.6, f32[4,32,16,128]{3,2,1,0:T(8,128)S(1)} %copy-done.1, f32[2,2,16,512]{3,2,1,0:T(8,128)S(1)} %get-tuple-element.35.later), custom_call_target="tpu_custom_call" | custom-call | flops 1 | bytes 1 | tf_op jit(solution)/shard_map/pallas_call | solution.py:400
  18.3 0.0 collective-permute-done.5.rest_0_.rest_2_
  18.3 0.0 copy-start.4
  18.3 0.0 copy-start.5
  18.3 0.0 copy-start.8
  18.3 0.1 collective-permute-start.8
  18.4 4.7 %collective-permute-done.6.rest_1_ = f32[2,2,16,512]{3,2,1,0:T(8,128)S(1)} collective-permute-done((f32[2,2,16,512]{3,2,1,0:T(8,128)S(1)}, f32[2,2,16,512]{3,2,1,0:T(8,128)S(1)}, u32[]{:S(2)}, u32[]{:S(2)}) %collective-permute-start.6) | collective-permute-done | bytes 131104 | tf_op jit(solution)/shard_map/ppermute | solution.py:422
  23.1 1.7 %collective-permute-done.7.rest_2_.rest_0_ = f32[2,2,16,512]{3,2,1,0:T(8,128)S(1)} collective-permute-done((f32[2,2,16,512]{3,2,1,0:T(8,128)S(1)}, f32[2,2,16,512]{3,2,1,0:T(8,128)S(1)}, u32[]{:S(2)}, u32[]{:S(2)}) %collective-permute-start.7) | collective-permute-done | bytes 131104 | tf_op jit(solution)/shard_map/ppermute | solution.py:422
  24.8 0.0 collective-permute-done.2.even_y
  24.8 0.0 collective-permute-done.3.odd_y
  24.8 0.0 copy-done.4
  24.8 0.0 copy-done.5
  24.9 0.0 copy-done.8
  24.9 2.9 %shard_map.78 = (f32[4,16,32,128]{3,2,1,0:T(8,128)S(1)}, bf16[4,2,128,128]{3,2,1,0:T(8,128)(2,1)S(1)}, bf16[2,80,128]{2,1,0:T(8,128)(2,1)S(1)}, bf16[80,96]{1,0:T(8,128)(2,1)S(1)}) custom-call(s32[4]{0:T(128)S(1)} %copy-done.6, s32[4]{0:T(128)S(1)} %copy-done.7, f32[4,41]{1,0:T(4,128)S(1)} %copy-done.8, f32[4,9]{1,0:T(4,128)S(1)} %copy-done.4, ...), custom_call_target="tpu_custom_call" | custom-call | flops 1 | bytes 1 | tf_op jit(solution)/shard_map/pallas_call | solution.py:435
  27.8 0.0 collective-permute-done.8.rest_1_.outer
  27.8 1.4 %collective-permute-start.9 = (f32[296,128]{1,0:T(8,128)S(1)}, f32[296,128]{1,0:T(8,128)S(1)}, u32[]{:S(2)}, u32[]{:S(2)}) collective-permute-start(f32[296,128]{1,0:T(8,128)S(1)} %shard_map.80), channel_id=1, source_target_pairs={{0,7},{1,6},{2,5},{3,4},{4,3},{5,2},{6,1},{7,0},{8,15},{9,14},{10,... | collective-permute-start | bytes 454664 | tf_op jit(solution)/shard_map/ppermute | solution.py:451
  29.2 1.5 %shard_map.81.data = f32[2,16,32,128]{3,2,1,0:T(8,128)S(1)} custom-call(f32[4,2,16,512]{3,2,1,0:T(8,128)S(1)} %get-tuple-element.31.mine, f32[4,2,16,512]{3,2,1,0:T(8,128)S(1)} %collective-permute-done.4.swapped, f32[2,2,16,512]{3,2,1,0:T(8,128)S(1)} %collective-permute-done.7.rest_2_.rest_0_, f32[2,2,16,512]{3,2,1,0:T(8,128)S(1)} %collective-permute-done.6.rest_1_, ...), custom_call_target="tpu_custom_call" | custom-call | flops 1 | bytes 1 | tf_op jit(solution)/shard_map/pallas_call | solution.py:428
  30.7 1.6 %shard_map.82 = (f32[4,72,128]{2,1,0:T(8,128)S(1)}, f32[4,72,128]{2,1,0:T(8,128)S(1)}, f32[4,8,32,128]{3,2,1,0:T(8,128)S(1)}) custom-call(s32[4]{0:T(128)S(1)} %copy-done.6, f32[4,9]{1,0:T(4,128)S(1)} %copy-done.4, f32[4,9]{1,0:T(4,128)S(1)} %copy-done.5, f32[4,16,32,128]{3,2,1,0:T(8,128)S(1)} %get-tuple-element.36.rest_0_.predicted, ...), custom_call_target="tpu_custom_call" | custom-call | flops 1 | bytes 1 | tf_op jit(solution)/shard_map/pallas_call | solution.py:452
  32.3 0.1 collective-permute-start.10
  32.3 3.9 %collective-permute-start.11 = (f32[4,72,128]{2,1,0:T(8,128)S(1)}, f32[4,72,128]{2,1,0:T(8,128)S(1)}, u32[]{:S(2)}, u32[]{:S(2)}) collective-permute-start(f32[4,72,128]{2,1,0:T(8,128)S(1)} %get-tuple-element.45), channel_id=1, source_target_pairs={{1,2},{2,1},{3,4},{4,3},{5,6},{6,5},{9,10},{10,9},{11,12},{12,11},... | collective-permute-start | bytes 442376 | tf_op jit(solution)/shard_map/ppermute | solution.py:457
  36.2 1.6 %shard_map.83.partial = f32[16,72,128]{2,1,0:T(8,128)S(1)} custom-call(s32[4]{0:T(128)S(1)} %copy-done.6, f32[4,9]{1,0:T(4,128)S(1)} %copy-done.4, f32[4,9]{1,0:T(4,128)S(1)} %copy-done.5, f32[4,16,32,128]{3,2,1,0:T(8,128)S(1)} %get-tuple-element.36.rest_0_.predicted, bf16[4,2,128,128]{3,2,1,0:T(8,128)(2,1)S(1)} %get-tuple-element.37.lane_back, ...), custom_call_target="tpu_custom_call" | custom-call | flops 1 | bytes 1 | tf_op jit(solution)/shard_map/pallas_call | solution.py:458
  37.9 0.0 collective-permute-done.9.flat
  37.9 1.1 %shard_map.84.middle = f32[16,72,128]{2,1,0:T(8,128)S(1)} custom-call(s32[4]{0:T(128)S(1)} %copy-done.6, f32[4,9]{1,0:T(4,128)S(1)} %copy-done.4, f32[4,9]{1,0:T(4,128)S(1)} %copy-done.5, f32[4,16,32,128]{3,2,1,0:T(8,128)S(1)} %get-tuple-element.36.rest_0_.predicted, bf16[4,2,128,128]{3,2,1,0:T(8,128)(2,1)S(1)} %get-tuple-element.37.lane_back, ...), custom_call_target="tpu_custom_call" | custom-call | flops 1 | bytes 1 | tf_op jit(solution)/shard_map/pallas_call | solution.py:464
  39.0 0.0 collective-permute-done.10.even_x
  39.0 0.0 collective-permute-done.11.odd_x
  39.0 0.1 shard_map.85
  39.1 1.9 %collective-permute-start.12 = (f32[320,128]{1,0:T(8,128)S(1)}, f32[320,128]{1,0:T(8,128)S(1)}, u32[]{:S(2)}, u32[]{:S(2)}) collective-permute-start(f32[320,128]{1,0:T(8,128)S(1)} %get-tuple-element.47), channel_id=1, source_target_pairs={{0,8},{8,0},{16,24},{24,16},{1,9},{9,1},{17,25},{25,17},{2,10},{10... | collective-permute-start | bytes 491528 | tf_op jit(solution)/shard_map/ppermute | solution.py:475
  41.1 3.0 %collective-permute-start.13 = (f32[320,128]{1,0:T(8,128)S(1)}, f32[320,128]{1,0:T(8,128)S(1)}, u32[]{:S(2)}, u32[]{:S(2)}) collective-permute-start(f32[320,128]{1,0:T(8,128)S(1)} %get-tuple-element.48), channel_id=1, source_target_pairs={{8,16},{16,8},{9,17},{17,9},{10,18},{18,10},{11,19},{19,11},{12,20... | collective-permute-start | bytes 491528 | tf_op jit(solution)/shard_map/ppermute | solution.py:475
  44.0 1.5 %collective-permute-done.12.even_y = f32[320,128]{1,0:T(8,128)S(1)} collective-permute-done((f32[320,128]{1,0:T(8,128)S(1)}, f32[320,128]{1,0:T(8,128)S(1)}, u32[]{:S(2)}, u32[]{:S(2)}) %collective-permute-start.12) | collective-permute-done | bytes 163872 | tf_op jit(solution)/shard_map/ppermute | solution.py:475
  45.5 4.2 %collective-permute-done.13.odd_y = f32[320,128]{1,0:T(8,128)S(1)} collective-permute-done((f32[320,128]{1,0:T(8,128)S(1)}, f32[320,128]{1,0:T(8,128)S(1)}, u32[]{:S(2)}, u32[]{:S(2)}) %collective-permute-start.13) | collective-permute-done | bytes 163872 | tf_op jit(solution)/shard_map/ppermute | solution.py:475
  49.8 1.0 %shard_map.86 = f32[32,16,128]{2,1,0:T(8,128)} custom-call(f32[32,16,128]{2,1,0:T(8,128)S(1)} %copy-done.3, f32[16,32,128]{2,1,0:T(8,128)S(1)} %get-tuple-element.46.own, f32[320,128]{1,0:T(8,128)S(1)} %collective-permute-done.12.even_y, f32[320,128]{1,0:T(8,128)S(1)} %collective-permute-done.13.odd_y), custom_call_target="tpu_custom_call" | custom-call | flops 1 | bytes 1 | tf_op jit(solution)/shard_map/pallas_call | solution.py:476
  (3 shorter events, 0.0 us)
Async XLA Ops:
  0.0 0.9 %copy-start.2 = (f32[32,16,128]{2,1,0:T(8,128)S(1)}, f32[32,16,128]{2,1,0:T(8,128)}, u32[]{:S(2)}) copy-start(f32[32,16,128]{2,1,0:T(8,128)} %estimate.1) | copy-start | bytes 786436
  1.1 1.3 %copy-start.6 = (s32[4]{0:T(128)S(1)}, s32[4]{0:T(128)}, u32[]{:S(2)}) copy-start(s32[4]{0:T(128)} %turns.11) | copy-start | bytes 52
  1.1 1.3 %copy-start.7 = (s32[4]{0:T(128)S(1)}, s32[4]{0:T(128)}, u32[]{:S(2)}) copy-start(s32[4]{0:T(128)} %offsets.3) | copy-start | bytes 52
  1.1 1.3 %collective-permute-start = (f32[4,32,128]{2,1,0:T(8,128)S(1)}, f32[4,32,128]{2,1,0:T(8,128)S(1)}, u32[]{:S(2)}, u32[]{:S(2)}) collective-permute-start(f32[4,32,128]{2,1,0:T(8,128)S(1)} %get-tuple-element.27), channel_id=1, source_target_pairs={{0,1},{1,0},{2,3},{3,2},{4,5},{5,4},{6,7},{7,6},{8,9},{9,8},{10,11... | collective-permute-start | bytes 196616 | tf_op jit(solution)/shard_map/ppermute | solution.py:390
  2.4 1.2 %copy-start = (f32[4,32,16,128]{3,2,1,0:T(8,128)S(1)}, f32[4,32,16,128]{3,2,1,0:T(8,128)}, u32[]{:S(2)}) copy-start(f32[4,32,16,128]{3,2,1,0:T(8,128)} %recorded.3) | copy-start | bytes 3145732
  3.6 14.1 %copy-start.1 = (f32[4,32,16,128]{3,2,1,0:T(8,128)S(1)}, f32[4,32,16,128]{3,2,1,0:T(8,128)}, u32[]{:S(2)}) copy-start(f32[4,32,16,128]{3,2,1,0:T(8,128)} %recorded.3) | copy-start | bytes 3145732
  4.6 2.5 %collective-permute-start.4 = (f32[4,2,16,512]{3,2,1,0:T(8,128)S(1)}, f32[4,2,16,512]{3,2,1,0:T(8,128)S(1)}, u32[]{:S(2)}, u32[]{:S(2)}) collective-permute-start(f32[4,2,16,512]{3,2,1,0:T(8,128)S(1)} %get-tuple-element.32), channel_id=1, source_target_pairs={{0,1},{1,0},{2,3},{3,2},{4,5},{5,4},{6,7},{7,6},{8,9},{9,8},{10,11... | collective-permute-start | bytes 786440 | tf_op jit(solution)/shard_map/ppermute | solution.py:398
  4.8 5.6 %collective-permute-start.1 = (f32[4,32,128]{2,1,0:T(8,128)S(1)}, f32[4,32,128]{2,1,0:T(8,128)S(1)}, u32[]{:S(2)}, u32[]{:S(2)}) collective-permute-start(f32[4,32,128]{2,1,0:T(8,128)S(1)} %get-tuple-element.28), channel_id=1, source_target_pairs={{1,2},{2,1},{3,4},{4,3},{5,6},{6,5},{9,10},{10,9},{11,12},{12,11},... | collective-permute-start | bytes 196616 | tf_op jit(solution)/shard_map/ppermute | solution.py:390
  7.1 3.3 %copy-start.3 = (f32[32,16,128]{2,1,0:T(8,128)S(1)}, f32[32,16,128]{2,1,0:T(8,128)}, u32[]{:S(2)}) copy-start(f32[32,16,128]{2,1,0:T(8,128)} %estimate.1) | copy-start | bytes 786436
  7.2 11.1 %collective-permute-start.5 = (f32[2,2,16,512]{3,2,1,0:T(8,128)S(1)}, f32[2,2,16,512]{3,2,1,0:T(8,128)S(1)}, u32[]{:S(2)}, u32[]{:S(2)}) collective-permute-start(f32[2,2,16,512]{3,2,1,0:T(8,128)S(1)} %get-tuple-element.33), channel_id=1, source_target_pairs={{0,6},{1,7},{2,4},{3,5},{4,2},{5,3},{6,0},{7,1},{8,14},{9,15},{10,... | collective-permute-start | bytes 393224 | tf_op jit(solution)/shard_map/ppermute | solution.py:422
  10.7 14.2 %collective-permute-start.2 = (f32[480,128]{1,0:T(8,128)S(1)}, f32[480,128]{1,0:T(8,128)S(1)}, u32[]{:S(2)}, u32[]{:S(2)}) collective-permute-start(f32[480,128]{1,0:T(8,128)S(1)} %get-tuple-element.29), channel_id=1, source_target_pairs={{0,8},{8,0},{16,24},{24,16},{1,9},{9,1},{17,25},{25,17},{2,10},{10... | collective-permute-start | bytes 737288 | tf_op jit(solution)/shard_map/ppermute | solution.py:420
  12.2 12.6 %collective-permute-start.3 = (f32[480,128]{1,0:T(8,128)S(1)}, f32[480,128]{1,0:T(8,128)S(1)}, u32[]{:S(2)}, u32[]{:S(2)}) collective-permute-start(f32[480,128]{1,0:T(8,128)S(1)} %get-tuple-element.30), channel_id=1, source_target_pairs={{8,16},{16,8},{9,17},{17,9},{10,18},{18,10},{11,19},{19,11},{12,20... | collective-permute-start | bytes 737288 | tf_op jit(solution)/shard_map/ppermute | solution.py:420
  14.6 8.5 %collective-permute-start.6 = (f32[2,2,16,512]{3,2,1,0:T(8,128)S(1)}, f32[2,2,16,512]{3,2,1,0:T(8,128)S(1)}, u32[]{:S(2)}, u32[]{:S(2)}) collective-permute-start(f32[2,2,16,512]{3,2,1,0:T(8,128)S(1)} %get-tuple-element.34), channel_id=1, source_target_pairs={{0,4},{1,5},{2,6},{3,7},{4,0},{5,1},{6,2},{7,3},{8,12},{9,13},{10,... | collective-permute-start | bytes 393224 | tf_op jit(solution)/shard_map/ppermute | solution.py:422
  17.2 7.6 %collective-permute-start.7 = (f32[2,2,16,512]{3,2,1,0:T(8,128)S(1)}, f32[2,2,16,512]{3,2,1,0:T(8,128)S(1)}, u32[]{:S(2)}, u32[]{:S(2)}) collective-permute-start(f32[2,2,16,512]{3,2,1,0:T(8,128)S(1)} %get-tuple-element.35.later), channel_id=1, source_target_pairs={{0,2},{1,3},{2,0},{3,1},{4,6},{5,7},{6,4},{7,5},{8,10},{9,11},{10,... | collective-permute-start | bytes 393224 | tf_op jit(solution)/shard_map/ppermute | solution.py:422
  18.3 6.6 %copy-start.4 = (f32[4,9]{1,0:T(4,128)S(1)}, f32[4,9]{1,0:T(4,128)}, u32[]{:S(2)}) copy-start(f32[4,9]{1,0:T(4,128)} %row_taps.7) | copy-start | bytes 436
  18.3 6.5 %copy-start.5 = (f32[4,9]{1,0:T(4,128)S(1)}, f32[4,9]{1,0:T(4,128)}, u32[]{:S(2)}) copy-start(f32[4,9]{1,0:T(4,128)} %column_taps.7) | copy-start | bytes 436
  18.3 6.5 %copy-start.8 = (f32[4,41]{1,0:T(4,128)S(1)}, f32[4,41]{1,0:T(4,128)}, u32[]{:S(2)}) copy-start(f32[4,41]{1,0:T(4,128)} %depth_taps.1) | copy-start | bytes 1972
  18.3 9.4 %collective-permute-start.8 = (f32[32,8,128]{2,1,0:T(8,128)S(1)}, f32[32,8,128]{2,1,0:T(8,128)S(1)}, u32[]{:S(2)}, u32[]{:S(2)}) collective-permute-start(f32[32,8,128]{2,1,0:T(8,128)S(1)} %get-tuple-element.40), channel_id=1, source_target_pairs={{0,7},{1,6},{2,5},{3,4},{4,3},{5,2},{6,1},{7,0},{8,15},{9,14},{10,... | collective-permute-start | bytes 393224 | tf_op jit(solution)/shard_map/ppermute | solution.py:418
  27.8 10.1 %collective-permute-start.9 = (f32[296,128]{1,0:T(8,128)S(1)}, f32[296,128]{1,0:T(8,128)S(1)}, u32[]{:S(2)}, u32[]{:S(2)}) collective-permute-start(f32[296,128]{1,0:T(8,128)S(1)} %shard_map.80), channel_id=1, source_target_pairs={{0,7},{1,6},{2,5},{3,4},{4,3},{5,2},{6,1},{7,0},{8,15},{9,14},{10,... | collective-permute-start | bytes 454664 | tf_op jit(solution)/shard_map/ppermute | solution.py:451
  32.3 6.7 %collective-permute-start.10 = (f32[4,72,128]{2,1,0:T(8,128)S(1)}, f32[4,72,128]{2,1,0:T(8,128)S(1)}, u32[]{:S(2)}, u32[]{:S(2)}) collective-permute-start(f32[4,72,128]{2,1,0:T(8,128)S(1)} %get-tuple-element.44), channel_id=1, source_target_pairs={{0,1},{1,0},{2,3},{3,2},{4,5},{5,4},{6,7},{7,6},{8,9},{9,8},{10,11... | collective-permute-start | bytes 442376 | tf_op jit(solution)/shard_map/ppermute | solution.py:457
  32.3 6.7 %collective-permute-start.11 = (f32[4,72,128]{2,1,0:T(8,128)S(1)}, f32[4,72,128]{2,1,0:T(8,128)S(1)}, u32[]{:S(2)}, u32[]{:S(2)}) collective-permute-start(f32[4,72,128]{2,1,0:T(8,128)S(1)} %get-tuple-element.45), channel_id=1, source_target_pairs={{1,2},{2,1},{3,4},{4,3},{5,6},{6,5},{9,10},{10,9},{11,12},{12,11},... | collective-permute-start | bytes 442376 | tf_op jit(solution)/shard_map/ppermute | solution.py:457
  39.1 6.4 %collective-permute-start.12 = (f32[320,128]{1,0:T(8,128)S(1)}, f32[320,128]{1,0:T(8,128)S(1)}, u32[]{:S(2)}, u32[]{:S(2)}) collective-permute-start(f32[320,128]{1,0:T(8,128)S(1)} %get-tuple-element.47), channel_id=1, source_target_pairs={{0,8},{8,0},{16,24},{24,16},{1,9},{9,1},{17,25},{25,17},{2,10},{10... | collective-permute-start | bytes 491528 | tf_op jit(solution)/shard_map/ppermute | solution.py:475
  41.1 8.7 %collective-permute-start.13 = (f32[320,128]{1,0:T(8,128)S(1)}, f32[320,128]{1,0:T(8,128)S(1)}, u32[]{:S(2)}, u32[]{:S(2)}) collective-permute-start(f32[320,128]{1,0:T(8,128)S(1)} %get-tuple-element.48), channel_id=1, source_target_pairs={{8,16},{16,8},{9,17},{17,9},{10,18},{18,10},{11,19},{19,11},{12,20... | collective-permute-start | bytes 491528 | tf_op jit(solution)/shard_map/ppermute | solution.py:475

commit v6 on v5

--- a/solution.py
+++ b/solution.py
@@ -49,7 +49,7 @@
     return lax.rem(lax.axis_index(axis), 2) == 1
 
 
-def pick(turns, recorded, later, outer, inner):
+def pick(turns, recorded, later, later_too, outer, inner):
     rows = recorded.shape[2]
     half = outer.shape[1] // 2
     outer[:, :half] = recorded[0, :, :half]
@@ -124,16 +124,14 @@
     return [source[view, width - 1 - s if flipped else s] for s in range(width)]
 
 
-def predict(turns, offsets, depth_taps, row_taps, column_taps, own, even_x, odd_x, even_y, odd_y, later,
-            predicted, lane_back, depth_back, half_back, extended, blurred):
-    depth, rows, lanes = own.shape
-    side = even_x.shape[0]
-    reach = even_y.shape[0] // (rows + 2 * side)
-    width = 2 * side + 1
+def matrices(turns, offsets, depth_taps, row_taps, column_taps, depth_forth, lane_forth, depth_back, lane_back, half_back):
+    padded = depth_back.shape[1]
+    depth = half_back.shape[1] // 3
+    lanes = lane_back.shape[2]
+    reach = (depth_taps.shape[1] - 1) // 2
+    width = row_taps.shape[1]
     deep = depth + 2 * reach
-    padded = extended.shape[1]
     views = [view_of(turns, turn) for turn in range(VIEWS)]
-
     column = lax.broadcasted_iota(jnp.int32, (depth, LANES), 1)
     row = lax.broadcasted_iota(jnp.int32, (depth, LANES), 0)
     layer = jnp.where(column < depth, column, jnp.where(column < depth + reach, column - depth - reach, column - reach))
@@ -151,7 +149,36 @@
     half = slice(2 * depth, 3 * depth)
     half_back[...] = jnp.concatenate([back_high[:, half], back_low[:, half], back_high[:, half]], axis=1)
     high, low = split(matrix)
-    depth_high, depth_low = high[:, :padded], low[:, :padded]
+    depth_forth[...] = jnp.concatenate([high[:, :padded], low[:, :padded], high[:, :padded]], axis=1)
+    inward = lax.broadcasted_iota(jnp.int32, (lanes, lanes), 0)
+    outward = lax.broadcasted_iota(jnp.int32, (lanes, lanes), 1)
+    for turn, view in enumerate(views):
+        place = outward
+        if turn % 2 == 0:
+            place = outward - offsets[view]
+            place = jnp.where(place < 0, place + lanes, place)
+        tap = (lanes - 1 - place - inward if turn >= 2 else inward - place) + width // 2
+        source = row_taps if turn % 2 else column_taps
+        matrix = jnp.zeros((lanes, lanes), F32)
+        for r in range(width):
+            matrix = jnp.where(tap == r, source[view, r], matrix)
+        high, low = split(matrix)
+        lane_forth[turn, 0] = high
+        lane_forth[turn, 1] = low
+        back_high, back_low = split(matrix.T)
+        lane_back[turn, 0] = back_high
+        lane_back[turn, 1] = back_low
+
+
+def predict(turns, row_taps, column_taps, depth_forth, lane_forth, own, even_x, odd_x, even_y, odd_y, later,
+            predicted, extended, blurred):
+    depth, rows, lanes = own.shape
+    side = even_x.shape[0]
+    reach = even_y.shape[0] // (rows + 2 * side)
+    width = 2 * side + 1
+    deep = depth + 2 * reach
+    padded = extended.shape[1]
+    forth = depth_forth[...]
 
     flip_x, flip_y = is_odd("gx"), is_odd("gy")
     for e in range(rows + 2 * side):
@@ -167,35 +194,28 @@
         if padded > deep:
             extended[e, deep:padded] = jnp.zeros((padded - deep, lanes), F32)
 
-    for i in range(rows + 2 * side):
-        e_high, e_low = split(extended[i])
-        blurred[i] = dot(depth_high, e_high) + dot(depth_high, e_low) + dot(depth_low, e_high)
-
-    inward = lax.broadcasted_iota(jnp.int32, (lanes, lanes), 0)
-    outward = lax.broadcasted_iota(jnp.int32, (lanes, lanes), 1)
-    for turn, view in enumerate(views):
-        place = outward
-        if turn % 2 == 0:
-            place = outward - offsets[view]
-            place = jnp.where(place < 0, place + lanes, place)
-        tap = (lanes - 1 - place - inward if turn >= 2 else inward - place) + side
-        source = row_taps if turn % 2 else column_taps
-        matrix = jnp.zeros((lanes, lanes), F32)
-        for r in range(width):
-            matrix = jnp.where(tap == r, source[view, r], matrix)
-        high, low = split(matrix)
-        back_high, back_low = split(matrix.T)
-        lane_back[turn, 0] = back_high
-        lane_back[turn, 1] = back_low
+    for i in range(0, rows + 2 * side, 2):
+        e_high, e_low = split(jnp.concatenate([extended[i], extended[i + 1]], axis=1))
+        result = dot(forth, jnp.concatenate([e_high, e_high, e_low], axis=0))
+        blurred[i] = result[:, :lanes]
+        blurred[i + 1] = result[:, lanes:]
+
+    for turn in range(VIEWS):
+        view = view_of(turns, turn)
+        high, low = lane_forth[turn, 0], lane_forth[turn, 1]
         both = jnp.concatenate([high, high], axis=0)
         factor = row_taps_of(turn, view, row_taps, column_taps, width)
-        for i in range(rows):
-            layers = pl.ds(turn * depth, depth)
-            total = factor[0] * blurred[i, layers]
-            for s in range(1, width):
-                total = total + factor[s] * blurred[i + s, layers]
-            t_high, t_low = split(total)
-            predicted[turn, i] = dot(jnp.concatenate([t_high, t_low], axis=1), both) + dot(t_high, low)
+        layers = pl.ds(turn * depth, depth)
+        for block in range(0, rows, 8):
+            totals = []
+            for i in range(block, block + 8):
+                total = factor[0] * blurred[i, layers]
+                for s in range(1, width):
+                    total = total + factor[s] * blurred[i + s, layers]
+                totals.append(total)
+            t_high, t_low = split(jnp.concatenate(totals, axis=0))
+            result = dot(jnp.concatenate([t_high, t_low], axis=1), both) + dot(t_high, low)
+            predicted[turn, block : block + 8] = result.reshape(8, depth, lanes)
 
 
 def gate(*rest):
@@ -240,9 +260,11 @@
 
 def lane_blur(recorded, predicted, back):
     high, low = back[0], back[1]
-    r_high, r_low = split(recorded / predicted)
+    ratio = jnp.concatenate([r / p for r, p in zip(recorded, predicted)], axis=0)
+    r_high, r_low = split(ratio)
     both = jnp.concatenate([high, high], axis=0)
-    return dot(jnp.concatenate([r_high, r_low], axis=1), both) + dot(r_high, low)
+    result = dot(jnp.concatenate([r_high, r_low], axis=1), both) + dot(r_high, low)
+    return result.reshape(len(recorded), -1, result.shape[1])
 
 
 def depth_blur(back, parts):
@@ -266,14 +288,13 @@
     side, deep, _ = even_pair.shape
     row_list = [*range(side), *range(rows - side, rows)]
     for turn in range(VIEWS):
-        for j, i in enumerate(row_list):
-            if turn == 0:
-                recorded = kept[:, i]
-            elif turn == 2:
-                recorded = outer[:, 2 * side - 1 - j]
-            else:
-                recorded = data[turn // 2, rows - 1 - i if turn == 1 else i]
-            backed[turn, j] = lane_blur(recorded, predicted[turn, i], lane_back.at[turn])
+        if turn == 0:
+            recorded = [kept[:, i] for i in row_list]
+        elif turn == 2:
+            recorded = [outer[:, 2 * side - 1 - j] for j in range(2 * side)]
+        else:
+            recorded = [data[turn // 2, rows - 1 - i if turn == 1 else i] for i in row_list]
+        backed[turn] = lane_blur(recorded, [predicted[turn, i] for i in row_list], lane_back.at[turn])
     factors = [
         row_taps_of(turn, view_of(turns, turn), row_taps, column_taps, 2 * side + 1) for turn in range(VIEWS)
     ]
@@ -297,14 +318,14 @@
     for turn in range(VIEWS):
         for j, i in enumerate(row_list):
             backed[turn, i] = outer_backed[turn, j]
-        for i in range(side, rows - side):
-            if turn == 0:
-                recorded = kept[:, i]
-            elif turn == 2:
-                continue
-            else:
-                recorded = data[turn // 2, rows - 1 - i if turn == 1 else i]
-            backed[turn, i] = lane_blur(recorded, predicted[turn, i], lane_back.at[turn])
+        if turn == 2:
+            continue
+        inner = range(side, rows - side)
+        if turn == 0:
+            recorded = [kept[:, i] for i in inner]
+        else:
+            recorded = [data[turn // 2, rows - 1 - i if turn == 1 else i] for i in inner]
+        backed[turn, side : rows - side] = lane_blur(recorded, [predicted[turn, i] for i in inner], lane_back.at[turn])
     factors = [
         row_taps_of(turn, view_of(turns, turn), row_taps, column_taps, 2 * side + 1) for turn in range(VIEWS)
     ]
@@ -322,8 +343,8 @@
     side = (rows - inner.shape[1]) // 2
     inner[...] = flat[: depth * inner.shape[1]].reshape(inner.shape)
     row_list = range(side, rows - side)
-    for i in row_list:
-        backed[i] = lane_blur(inner[:, rows - side - 1 - i], predicted[2, i], lane_back.at[2])
+    recorded = [inner[:, rows - side - 1 - i] for i in row_list]
+    backed[side : rows - side] = lane_blur(recorded, [predicted[2, i] for i in row_list], lane_back.at[2])
     factor = row_taps_of(2, view_of(turns, 2), row_taps, column_taps, 2 * side + 1)
     back = half_back[...]
     for e in range(rows):
@@ -397,6 +418,17 @@
     mirror = [(i, parts - 1 - i) for i in range(parts)]
     swapped = lax.ppermute(theirs, "gx", [(i, i ^ 1) for i in range(parts)])
     messages = call(merge, (struct(2, 2, rows, wide),) * (chips - 1), [VMEM] * 2)(mine, swapped)
+    depth_forth, lane_forth, depth_back, lane_back, half_back = call(
+        matrices,
+        (
+            struct(VIEWS * depth, 3 * padded, dtype=BF16),
+            struct(VIEWS, 2, lanes, lanes, dtype=BF16),
+            struct(2, padded, VIEWS * depth, dtype=BF16),
+            struct(VIEWS, 2, lanes, lanes, dtype=BF16),
+            struct(padded, 3 * depth, dtype=BF16),
+        ),
+        [SMEM] * 5,
+    )(quarter_turns, offsets, depth_taps, row_taps, column_taps)
     outer, inner = pl.pallas_call(
         pick,
         out_shape=(struct(depth, 2 * side, lanes), struct(depth, rows - 2 * side, lanes)),
@@ -406,6 +438,7 @@
             in_specs=[
                 pl.BlockSpec((1, depth, rows, lanes), lambda i, turns: (view_of(turns, 2), 0, 0, 0)),
                 ORDER,
+                ORDER,
             ],
             out_specs=[
                 pl.BlockSpec((depth, 2 * side, lanes), lambda i, turns: (0, 0, 0)),
@@ -414,7 +447,7 @@
         ),
         compiler_params=PARAMS,
         cost_estimate=COST,
-    )(quarter_turns, recorded, messages[0])
+    )(quarter_turns, recorded, messages[0], half_back)
     outer = lax.ppermute(outer, "gx", mirror)
     third, fourth = call(layers_out, (struct((rows + 2 * side) * reach, lanes),) * 2, [VMEM] * 3)(estimate, first, second)
     third, fourth = lax.ppermute(third, "gy", even_y), lax.ppermute(fourth, "gy", odd_y)
@@ -432,20 +465,15 @@
         [pltpu.VMEM((parts, 2, rows, wide), F32)],
     )(mine, swapped, *[moved[k] for k in range(1, chips)])
 
-    predicted, lane_back, depth_back, half_back = call(
+    predicted = call(
         predict,
-        (
-            struct(VIEWS, rows, depth, lanes),
-            struct(VIEWS, 2, lanes, lanes, dtype=BF16),
-            struct(2, padded, VIEWS * depth, dtype=BF16),
-            struct(padded, 3 * depth, dtype=BF16),
-        ),
-        [SMEM] * 5 + [VMEM] * 5 + [ORDER],
+        struct(VIEWS, rows, depth, lanes),
+        [SMEM] * 3 + [VMEM] * 7 + [ORDER],
         [
             pltpu.VMEM((rows + 2 * side, padded, lanes), F32),
             pltpu.VMEM((rows + 2 * side, VIEWS * depth, lanes), F32),
         ],
-    )(quarter_turns, offsets, depth_taps, row_taps, column_taps, estimate, first, second, third, fourth, passed)
+    )(quarter_turns, row_taps, column_taps, depth_forth, lane_forth, estimate, first, second, third, fourth, passed)
 
     inner = call(hold, struct(side * deep + 8, lanes), [VMEM] + [ORDER] * 2)(inner, predicted, outer)
     inner = lax.ppermute(inner, "gx", mirror)

time: 51.3 us -> 51 us (level)
  waiting for transfers between devices: 15 us -> 16.6 us
  starting transfers between devices: 21.6 us -> 20.1 us
    ppermute x1, waiting for transfers between devices: 0.01 us -> 1.39 us  [shards(): outer = lax.ppermute(outer, 'gx', mirror)]
    ppermute x3, waiting for transfers between devices: 6.43 us -> 5.28 us  [shards(): lax.ppermute(messages[k - 1], 'gx', [(i, i ^ 2 * k) for i in range(parts)])]
    ppermute x2, starting transfers between devices: 6.18 us -> 5.36 us  [shards(): lax.ppermute(second, 'gx', odd_x)]
    ppermute x2, waiting for transfers between devices: 1.52 us -> 2.21 us  [shards(): lax.ppermute(third, 'gy', even_y)]
    pallas_call x1 -> x2, Pallas kernels: 2.88 us -> 3.12 us  [the longest x1 1.96 us: shards(): call(predict, struct(VIEWS, rows, depth, lanes), [SMEM] * 3 + [VMEM] * 7...]
  transfers between devices with their start and end apart: 14 -> 14, of which waited for: 6 -> 9; matrix products, arithmetic and copies ran while one was open for 0% -> 0% of each run, Pallas kernels for 19% -> 19%
where the time goes in v6:
time: 51 us; the launch traced here: 50.7 us
  starting transfers between devices  20.1 us (39%)
  waiting for transfers between devices  16.6 us (33%)
  Pallas kernels  11.7 us (23%)
  local copies, waits for them, and re-layouts  2.21 us (4%)
    ppermute x2, starting transfers between devices, shards(): lax.ppermute(second, 'gx', odd_x)  5.36 us
    ppermute x2, starting transfers between devices, shards(): lax.ppermute(fourth, 'gy', odd_y)  5.35 us
    ppermute x3, waiting for transfers between devices, shards(): lax.ppermute(messages[k - 1], 'gx', [(i, i ^ 2 * k) for i in range(parts)])  5.28 us
    ppermute x3, starting transfers between devices, shards(): lax.ppermute(messages[k - 1], 'gx', [(i, i ^ 2 * k) for i in range(parts)])  4.74 us
    ppermute x2, waiting for transfers between devices, shards(): lax.ppermute(fourth, 'gy', odd_y)  4.22 us
    ppermute x2, starting transfers between devices, shards(): lax.ppermute(third, 'gy', even_y)  3.15 us
    ppermute x2, waiting for transfers between devices, shards(): lax.ppermute(third, 'gy', even_y)  2.21 us
    unnamed x18, local copies, waits for them, and re-layouts  2.21 us
  transfers between devices with their start and end apart: 14, of which 9 were waited for; matrix products, arithmetic and copies ran while one was open for 0% of the time, Pallas kernels for 19%

profile of v6, /device:TPU:12, one launch (start us, length us, event | category | flops | bytes accessed | tf_op | source)
XLA Modules:
  0.0 50.7 jit_solution(2008870930669558966)
XLA Ops:
  0.0 0.0 copy-start
  0.0 0.9 %copy-done = f32[32,16,128]{2,1,0:T(8,128)S(1)} copy-done((f32[32,16,128]{2,1,0:T(8,128)S(1)}, f32[32,16,128]{2,1,0:T(8,128)}, u32[]{:S(2)}) %copy-start) | copy-done | bytes 262168
  1.0 0.1 shard_map.74
  1.1 0.0 copy-start.6
  1.1 0.0 copy-start.7
  1.1 0.1 collective-permute-start
  1.2 1.2 %collective-permute-done.from_even.later.even_x = f32[4,32,128]{2,1,0:T(8,128)S(1)} collective-permute-done((f32[4,32,128]{2,1,0:T(8,128)S(1)}, f32[4,32,128]{2,1,0:T(8,128)S(1)}, u32[]{:S(2)}, u32[]{:S(2)}) %collective-permute-start) | collective-permute-done | bytes 65568 | tf_op jit(solution)/shard_map/ppermute | solution.py:411
  2.4 0.0 copy-done.6
  2.4 0.0 copy-done.7
  2.4 0.0 copy-start.2
  2.4 1.2 %copy-done.2 = f32[4,32,16,128]{3,2,1,0:T(8,128)S(1)} copy-done((f32[4,32,16,128]{3,2,1,0:T(8,128)S(1)}, f32[4,32,16,128]{3,2,1,0:T(8,128)}, u32[]{:S(2)}) %copy-start.2) | copy-done | bytes 1048600
  3.6 0.0 copy-start.3
  3.6 0.9 %shard_map.76 = (f32[32,16,128]{2,1,0:T(8,128)S(1)}, f32[4,2,16,512]{3,2,1,0:T(8,128)S(1)}, f32[4,2,16,512]{3,2,1,0:T(8,128)S(1)}) custom-call(s32[4]{0:T(128)S(1)} %copy-done.6, s32[4]{0:T(128)S(1)} %copy-done.7, f32[4,32,16,128]{3,2,1,0:T(8,128)S(1)} %copy-done.2, f32[4,32,128]{2,1,0:T(8,128)S(1)} %collective-permute-done.from_even.later.even_x), custom_call_target="tpu_custom_call" | custom-call | flops 1 | bytes 1 | tf_op jit(solution)/shard_map/pallas_call | solution.py:412
  4.6 0.2 collective-permute-start.4
  4.8 2.3 %collective-permute-start.1 = (f32[4,32,128]{2,1,0:T(8,128)S(1)}, f32[4,32,128]{2,1,0:T(8,128)S(1)}, u32[]{:S(2)}, u32[]{:S(2)}) collective-permute-start(f32[4,32,128]{2,1,0:T(8,128)S(1)} %get-tuple-element.31), channel_id=1, source_target_pairs={{1,2},{2,1},{3,4},{4,3},{5,6},{6,5},{9,10},{10,9},{11,12},{12,11},... | collective-permute-start | bytes 196616 | tf_op jit(solution)/shard_map/ppermute | solution.py:411
  7.1 0.0 collective-permute-done.4.swapped
  7.1 0.0 copy-start.1
  7.2 1.6 %collective-permute-start.5 = (f32[2,2,16,512]{3,2,1,0:T(8,128)S(1)}, f32[2,2,16,512]{3,2,1,0:T(8,128)S(1)}, u32[]{:S(2)}, u32[]{:S(2)}) collective-permute-start(f32[2,2,16,512]{3,2,1,0:T(8,128)S(1)} %get-tuple-element.36), channel_id=1, source_target_pairs={{0,6},{1,7},{2,4},{3,5},{4,2},{5,3},{6,0},{7,1},{8,14},{9,15},{10,... | collective-permute-start | bytes 393224 | tf_op jit(solution)/shard_map/ppermute | solution.py:455
  8.8 1.6 %collective-permute-done.1.from_odd.odd_x = f32[4,32,128]{2,1,0:T(8,128)S(1)} collective-permute-done((f32[4,32,128]{2,1,0:T(8,128)S(1)}, f32[4,32,128]{2,1,0:T(8,128)S(1)}, u32[]{:S(2)}, u32[]{:S(2)}) %collective-permute-start.1) | collective-permute-done | bytes 65568 | tf_op jit(solution)/shard_map/ppermute | solution.py:411
  10.4 0.0 copy-done.1
  10.4 0.3 shard_map.75
  10.7 0.0 copy-start.8
  10.7 1.6 %collective-permute-start.2 = (f32[480,128]{1,0:T(8,128)S(1)}, f32[480,128]{1,0:T(8,128)S(1)}, u32[]{:S(2)}, u32[]{:S(2)}) collective-permute-start(f32[480,128]{1,0:T(8,128)S(1)} %get-tuple-element.32), channel_id=1, source_target_pairs={{0,8},{8,0},{16,24},{24,16},{1,9},{9,1},{17,25},{25,17},{2,10},{10... | collective-permute-start | bytes 737288 | tf_op jit(solution)/shard_map/ppermute | solution.py:453
  12.2 0.0 copy-start.5
  12.2 0.0 copy-start.4
  12.2 2.5 %collective-permute-start.3 = (f32[480,128]{1,0:T(8,128)S(1)}, f32[480,128]{1,0:T(8,128)S(1)}, u32[]{:S(2)}, u32[]{:S(2)}) collective-permute-start(f32[480,128]{1,0:T(8,128)S(1)} %get-tuple-element.33), channel_id=1, source_target_pairs={{8,16},{16,8},{9,17},{17,9},{10,18},{18,10},{11,19},{19,11},{12,20... | collective-permute-start | bytes 737288 | tf_op jit(solution)/shard_map/ppermute | solution.py:453
  14.7 2.7 %collective-permute-start.6 = (f32[2,2,16,512]{3,2,1,0:T(8,128)S(1)}, f32[2,2,16,512]{3,2,1,0:T(8,128)S(1)}, u32[]{:S(2)}, u32[]{:S(2)}) collective-permute-start(f32[2,2,16,512]{3,2,1,0:T(8,128)S(1)} %get-tuple-element.37), channel_id=1, source_target_pairs={{0,4},{1,5},{2,6},{3,7},{4,0},{5,1},{6,2},{7,3},{8,12},{9,13},{10,... | collective-permute-start | bytes 393224 | tf_op jit(solution)/shard_map/ppermute | solution.py:455
  17.4 0.4 collective-permute-start.7
  17.8 0.0 copy-done.8
  17.8 0.0 copy-done.5
  17.8 0.0 copy-done.4
  17.9 1.2 %shard_map.73 = (bf16[128,240]{1,0:T(8,128)(2,1)S(1)}, bf16[4,2,128,128]{3,2,1,0:T(8,128)(2,1)S(1)}, bf16[2,80,128]{2,1,0:T(8,128)(2,1)S(1)}, bf16[4,2,128,128]{3,2,1,0:T(8,128)(2,1)S(1)}, bf16[80,96]{1,0:T(8,128)(2,1)S(1)}) custom-call(s32[4]{0:T(128)S(1)} %copy-done.6, s32[4]{0:T(128)S(1)} %copy-done.7, f32[4,41]{1,0:T(4,128)S(1)} %copy-done.8, ...), custom_call_target="tpu_custom_call" | custom-call | flops 1 | bytes 1 | tf_op jit(solution)/shard_map/pallas_call | solution.py:421
  19.0 0.0 copy-done.3
  19.0 0.6 %shard_map.80 = (f32[32,8,128]{2,1,0:T(8,128)S(1)}, f32[32,8,128]{2,1,0:T(8,128)S(1)}) custom-call(s32[4]{0:T(128)S(1)} %copy-done.6, f32[4,32,16,128]{3,2,1,0:T(8,128)S(1)} %copy-done.3, f32[2,2,16,512]{3,2,1,0:T(8,128)S(1)} %get-tuple-element.38.later, bf16[80,96]{1,0:T(8,128)(2,1)S(1)} %get-tuple-element.40.later_too.half_back), custom_call_target="tpu_custom_call" | custom-call | flops 1 | bytes 1 | tf_op jit(solution)/shard_map/pallas_call | solution.py:432
  19.6 0.0 collective-permute-done.5.rest_0_.rest_2_
  19.6 0.1 collective-permute-start.8
  19.7 2.9 %collective-permute-done.6.rest_1_ = f32[2,2,16,512]{3,2,1,0:T(8,128)S(1)} collective-permute-done((f32[2,2,16,512]{3,2,1,0:T(8,128)S(1)}, f32[2,2,16,512]{3,2,1,0:T(8,128)S(1)}, u32[]{:S(2)}, u32[]{:S(2)}) %collective-permute-start.6) | collective-permute-done | bytes 131104 | tf_op jit(solution)/shard_map/ppermute | solution.py:455
  22.6 2.4 %collective-permute-done.7.rest_2_.rest_0_ = f32[2,2,16,512]{3,2,1,0:T(8,128)S(1)} collective-permute-done((f32[2,2,16,512]{3,2,1,0:T(8,128)S(1)}, f32[2,2,16,512]{3,2,1,0:T(8,128)S(1)}, u32[]{:S(2)}, u32[]{:S(2)}) %collective-permute-start.7) | collective-permute-done | bytes 131104 | tf_op jit(solution)/shard_map/ppermute | solution.py:455
  25.0 0.0 collective-permute-done.2.even_y
  25.0 0.0 collective-permute-done.3.odd_y
  25.0 2.0 %shard_map.79.rest_0_.predicted = f32[4,16,32,128]{3,2,1,0:T(8,128)S(1)} custom-call(s32[4]{0:T(128)S(1)} %copy-done.6, f32[4,9]{1,0:T(4,128)S(1)} %copy-done.4, f32[4,9]{1,0:T(4,128)S(1)} %copy-done.5, bf16[128,240]{1,0:T(8,128)(2,1)S(1)} %get-tuple-element.28.depth_forth, bf16[4,2,128,128]{3,2,1,0:T(8,128)(2,1)S(1)} %get-tuple-element.29.lane_forth, ...), custom_call_target="tpu_custom_call" | custom-call | flops 1 | bytes 1 | tf_op jit(solution)/shard_map/pallas_call | solution.py:468
  26.9 1.4 %collective-permute-done.8.rest_1_.outer = f32[32,8,128]{2,1,0:T(8,128)S(1)} collective-permute-done((f32[32,8,128]{2,1,0:T(8,128)S(1)}, f32[32,8,128]{2,1,0:T(8,128)S(1)}, u32[]{:S(2)}, u32[]{:S(2)}) %collective-permute-start.8) | collective-permute-done | bytes 131104 | tf_op jit(solution)/shard_map/ppermute | solution.py:451
  28.4 1.0 %collective-permute-start.9 = (f32[296,128]{1,0:T(8,128)S(1)}, f32[296,128]{1,0:T(8,128)S(1)}, u32[]{:S(2)}, u32[]{:S(2)}) collective-permute-start(f32[296,128]{1,0:T(8,128)S(1)} %shard_map.81), channel_id=1, source_target_pairs={{0,7},{1,6},{2,5},{3,4},{4,3},{5,2},{6,1},{7,0},{8,15},{9,14},{10,... | collective-permute-start | bytes 454664 | tf_op jit(solution)/shard_map/ppermute | solution.py:479
  29.4 1.5 %shard_map.82.data = f32[2,16,32,128]{3,2,1,0:T(8,128)S(1)} custom-call(f32[4,2,16,512]{3,2,1,0:T(8,128)S(1)} %get-tuple-element.34.mine, f32[4,2,16,512]{3,2,1,0:T(8,128)S(1)} %collective-permute-done.4.swapped, f32[2,2,16,512]{3,2,1,0:T(8,128)S(1)} %collective-permute-done.7.rest_2_.rest_0_, f32[2,2,16,512]{3,2,1,0:T(8,128)S(1)} %collective-permute-done.6.rest_1_, ...), custom_call_target="tpu_custom_call" | custom-call | flops 1 | bytes 1 | tf_op jit(solution)/shard_map/pallas_call | solution.py:461
  30.8 1.3 %shard_map.83 = (f32[4,72,128]{2,1,0:T(8,128)S(1)}, f32[4,72,128]{2,1,0:T(8,128)S(1)}, f32[4,8,32,128]{3,2,1,0:T(8,128)S(1)}) custom-call(s32[4]{0:T(128)S(1)} %copy-done.6, f32[4,9]{1,0:T(4,128)S(1)} %copy-done.4, f32[4,9]{1,0:T(4,128)S(1)} %copy-done.5, f32[4,16,32,128]{3,2,1,0:T(8,128)S(1)} %shard_map.79.rest_0_.predicted, ...), custom_call_target="tpu_custom_call" | custom-call | flops 1 | bytes 1 | tf_op jit(solution)/shard_map/pallas_call | solution.py:480
  32.2 0.1 collective-permute-start.10
  32.3 3.1 %collective-permute-start.11 = (f32[4,72,128]{2,1,0:T(8,128)S(1)}, f32[4,72,128]{2,1,0:T(8,128)S(1)}, u32[]{:S(2)}, u32[]{:S(2)}) collective-permute-start(f32[4,72,128]{2,1,0:T(8,128)S(1)} %get-tuple-element.47), channel_id=1, source_target_pairs={{1,2},{2,1},{3,4},{4,3},{5,6},{6,5},{9,10},{10,9},{11,12},{12,11},... | collective-permute-start | bytes 442376 | tf_op jit(solution)/shard_map/ppermute | solution.py:485
  35.3 1.6 %shard_map.84.partial = f32[16,72,128]{2,1,0:T(8,128)S(1)} custom-call(s32[4]{0:T(128)S(1)} %copy-done.6, f32[4,9]{1,0:T(4,128)S(1)} %copy-done.4, f32[4,9]{1,0:T(4,128)S(1)} %copy-done.5, f32[4,16,32,128]{3,2,1,0:T(8,128)S(1)} %shard_map.79.rest_0_.predicted, bf16[4,2,128,128]{3,2,1,0:T(8,128)(2,1)S(1)} %get-tuple-element.39.lane_back, ...), custom_call_target="tpu_custom_call" | custom-call | flops 1 | bytes 1 | tf_op jit(solution)/shard_map/pallas_call | solution.py:486
  37.0 0.4 collective-permute-done.9.flat
  37.3 1.1 %shard_map.85.middle = f32[16,72,128]{2,1,0:T(8,128)S(1)} custom-call(s32[4]{0:T(128)S(1)} %copy-done.6, f32[4,9]{1,0:T(4,128)S(1)} %copy-done.4, f32[4,9]{1,0:T(4,128)S(1)} %copy-done.5, f32[4,16,32,128]{3,2,1,0:T(8,128)S(1)} %shard_map.79.rest_0_.predicted, bf16[4,2,128,128]{3,2,1,0:T(8,128)(2,1)S(1)} %get-tuple-element.39.lane_back, ...), custom_call_target="tpu_custom_call" | custom-call | flops 1 | bytes 1 | tf_op jit(solution)/shard_map/pallas_call | solution.py:492
  38.4 0.0 collective-permute-done.10.even_x
  38.4 0.3 collective-permute-done.11.odd_x
  38.7 0.1 shard_map.86
  38.8 1.6 %collective-permute-start.12 = (f32[320,128]{1,0:T(8,128)S(1)}, f32[320,128]{1,0:T(8,128)S(1)}, u32[]{:S(2)}, u32[]{:S(2)}) collective-permute-start(f32[320,128]{1,0:T(8,128)S(1)} %get-tuple-element.49), channel_id=1, source_target_pairs={{0,8},{8,0},{16,24},{24,16},{1,9},{9,1},{17,25},{25,17},{2,10},{10... | collective-permute-start | bytes 491528 | tf_op jit(solution)/shard_map/ppermute | solution.py:503
  40.4 2.8 %collective-permute-start.13 = (f32[320,128]{1,0:T(8,128)S(1)}, f32[320,128]{1,0:T(8,128)S(1)}, u32[]{:S(2)}, u32[]{:S(2)}) collective-permute-start(f32[320,128]{1,0:T(8,128)S(1)} %get-tuple-element.50), channel_id=1, source_target_pairs={{8,16},{16,8},{9,17},{17,9},{10,18},{18,10},{11,19},{19,11},{12,20... | collective-permute-start | bytes 491528 | tf_op jit(solution)/shard_map/ppermute | solution.py:503
  43.3 2.2 %collective-permute-done.12.even_y = f32[320,128]{1,0:T(8,128)S(1)} collective-permute-done((f32[320,128]{1,0:T(8,128)S(1)}, f32[320,128]{1,0:T(8,128)S(1)}, u32[]{:S(2)}, u32[]{:S(2)}) %collective-permute-start.12) | collective-permute-done | bytes 163872 | tf_op jit(solution)/shard_map/ppermute | solution.py:503
  45.5 4.2 %collective-permute-done.13.odd_y = f32[320,128]{1,0:T(8,128)S(1)} collective-permute-done((f32[320,128]{1,0:T(8,128)S(1)}, f32[320,128]{1,0:T(8,128)S(1)}, u32[]{:S(2)}, u32[]{:S(2)}) %collective-permute-start.13) | collective-permute-done | bytes 163872 | tf_op jit(solution)/shard_map/ppermute | solution.py:503
  49.7 1.0 %shard_map.87 = f32[32,16,128]{2,1,0:T(8,128)} custom-call(f32[32,16,128]{2,1,0:T(8,128)S(1)} %copy-done.1, f32[16,32,128]{2,1,0:T(8,128)S(1)} %get-tuple-element.48.own, f32[320,128]{1,0:T(8,128)S(1)} %collective-permute-done.12.even_y, f32[320,128]{1,0:T(8,128)S(1)} %collective-permute-done.13.odd_y), custom_call_target="tpu_custom_call" | custom-call | flops 1 | bytes 1 | tf_op jit(solution)/shard_map/pallas_call | solution.py:504
  (3 shorter events, 0.0 us)
Async XLA Ops:
  0.0 0.9 %copy-start = (f32[32,16,128]{2,1,0:T(8,128)S(1)}, f32[32,16,128]{2,1,0:T(8,128)}, u32[]{:S(2)}) copy-start(f32[32,16,128]{2,1,0:T(8,128)} %estimate.1) | copy-start | bytes 786436
  1.1 1.3 %copy-start.6 = (s32[4]{0:T(128)S(1)}, s32[4]{0:T(128)}, u32[]{:S(2)}) copy-start(s32[4]{0:T(128)} %turns.13) | copy-start | bytes 52
  1.1 1.3 %copy-start.7 = (s32[4]{0:T(128)S(1)}, s32[4]{0:T(128)}, u32[]{:S(2)}) copy-start(s32[4]{0:T(128)} %offsets.3) | copy-start | bytes 52
  1.1 1.3 %collective-permute-start = (f32[4,32,128]{2,1,0:T(8,128)S(1)}, f32[4,32,128]{2,1,0:T(8,128)S(1)}, u32[]{:S(2)}, u32[]{:S(2)}) collective-permute-start(f32[4,32,128]{2,1,0:T(8,128)S(1)} %get-tuple-element.30), channel_id=1, source_target_pairs={{0,1},{1,0},{2,3},{3,2},{4,5},{5,4},{6,7},{7,6},{8,9},{9,8},{10,11... | collective-permute-start | bytes 196616 | tf_op jit(solution)/shard_map/ppermute | solution.py:411
  2.4 1.2 %copy-start.2 = (f32[4,32,16,128]{3,2,1,0:T(8,128)S(1)}, f32[4,32,16,128]{3,2,1,0:T(8,128)}, u32[]{:S(2)}) copy-start(f32[4,32,16,128]{3,2,1,0:T(8,128)} %recorded.3) | copy-start | bytes 3145732
  3.6 15.4 %copy-start.3 = (f32[4,32,16,128]{3,2,1,0:T(8,128)S(1)}, f32[4,32,16,128]{3,2,1,0:T(8,128)}, u32[]{:S(2)}) copy-start(f32[4,32,16,128]{3,2,1,0:T(8,128)} %recorded.3) | copy-start | bytes 3145732
  4.6 2.5 %collective-permute-start.4 = (f32[4,2,16,512]{3,2,1,0:T(8,128)S(1)}, f32[4,2,16,512]{3,2,1,0:T(8,128)S(1)}, u32[]{:S(2)}, u32[]{:S(2)}) collective-permute-start(f32[4,2,16,512]{3,2,1,0:T(8,128)S(1)} %get-tuple-element.35), channel_id=1, source_target_pairs={{0,1},{1,0},{2,3},{3,2},{4,5},{5,4},{6,7},{7,6},{8,9},{9,8},{10,11... | collective-permute-start | bytes 786440 | tf_op jit(solution)/shard_map/ppermute | solution.py:419
  4.8 5.6 %collective-permute-start.1 = (f32[4,32,128]{2,1,0:T(8,128)S(1)}, f32[4,32,128]{2,1,0:T(8,128)S(1)}, u32[]{:S(2)}, u32[]{:S(2)}) collective-permute-start(f32[4,32,128]{2,1,0:T(8,128)S(1)} %get-tuple-element.31), channel_id=1, source_target_pairs={{1,2},{2,1},{3,4},{4,3},{5,6},{6,5},{9,10},{10,9},{11,12},{12,11},... | collective-permute-start | bytes 196616 | tf_op jit(solution)/shard_map/ppermute | solution.py:411
  7.1 3.3 %copy-start.1 = (f32[32,16,128]{2,1,0:T(8,128)S(1)}, f32[32,16,128]{2,1,0:T(8,128)}, u32[]{:S(2)}) copy-start(f32[32,16,128]{2,1,0:T(8,128)} %estimate.1) | copy-start | bytes 786436
  7.2 12.4 %collective-permute-start.5 = (f32[2,2,16,512]{3,2,1,0:T(8,128)S(1)}, f32[2,2,16,512]{3,2,1,0:T(8,128)S(1)}, u32[]{:S(2)}, u32[]{:S(2)}) collective-permute-start(f32[2,2,16,512]{3,2,1,0:T(8,128)S(1)} %get-tuple-element.36), channel_id=1, source_target_pairs={{0,6},{1,7},{2,4},{3,5},{4,2},{5,3},{6,0},{7,1},{8,14},{9,15},{10,... | collective-permute-start | bytes 393224 | tf_op jit(solution)/shard_map/ppermute | solution.py:455
  10.7 7.2 %copy-start.8 = (f32[4,41]{1,0:T(4,128)S(1)}, f32[4,41]{1,0:T(4,128)}, u32[]{:S(2)}) copy-start(f32[4,41]{1,0:T(4,128)} %depth_taps.1) | copy-start | bytes 1972
  10.7 14.3 %collective-permute-start.2 = (f32[480,128]{1,0:T(8,128)S(1)}, f32[480,128]{1,0:T(8,128)S(1)}, u32[]{:S(2)}, u32[]{:S(2)}) collective-permute-start(f32[480,128]{1,0:T(8,128)S(1)} %get-tuple-element.32), channel_id=1, source_target_pairs={{0,8},{8,0},{16,24},{24,16},{1,9},{9,1},{17,25},{25,17},{2,10},{10... | collective-permute-start | bytes 737288 | tf_op jit(solution)/shard_map/ppermute | solution.py:453
  12.2 5.6 %copy-start.5 = (f32[4,9]{1,0:T(4,128)S(1)}, f32[4,9]{1,0:T(4,128)}, u32[]{:S(2)}) copy-start(f32[4,9]{1,0:T(4,128)} %column_taps.9) | copy-start | bytes 436
  12.2 5.6 %copy-start.4 = (f32[4,9]{1,0:T(4,128)S(1)}, f32[4,9]{1,0:T(4,128)}, u32[]{:S(2)}) copy-start(f32[4,9]{1,0:T(4,128)} %row_taps.9) | copy-start | bytes 436
  12.2 12.8 %collective-permute-start.3 = (f32[480,128]{1,0:T(8,128)S(1)}, f32[480,128]{1,0:T(8,128)S(1)}, u32[]{:S(2)}, u32[]{:S(2)}) collective-permute-start(f32[480,128]{1,0:T(8,128)S(1)} %get-tuple-element.33), channel_id=1, source_target_pairs={{8,16},{16,8},{9,17},{17,9},{10,18},{18,10},{11,19},{19,11},{12,20... | collective-permute-start | bytes 737288 | tf_op jit(solution)/shard_map/ppermute | solution.py:453
  14.7 7.9 %collective-permute-start.6 = (f32[2,2,16,512]{3,2,1,0:T(8,128)S(1)}, f32[2,2,16,512]{3,2,1,0:T(8,128)S(1)}, u32[]{:S(2)}, u32[]{:S(2)}) collective-permute-start(f32[2,2,16,512]{3,2,1,0:T(8,128)S(1)} %get-tuple-element.37), channel_id=1, source_target_pairs={{0,4},{1,5},{2,6},{3,7},{4,0},{5,1},{6,2},{7,3},{8,12},{9,13},{10,... | collective-permute-start | bytes 393224 | tf_op jit(solution)/shard_map/ppermute | solution.py:455
  17.4 7.6 %collective-permute-start.7 = (f32[2,2,16,512]{3,2,1,0:T(8,128)S(1)}, f32[2,2,16,512]{3,2,1,0:T(8,128)S(1)}, u32[]{:S(2)}, u32[]{:S(2)}) collective-permute-start(f32[2,2,16,512]{3,2,1,0:T(8,128)S(1)} %get-tuple-element.38.later), channel_id=1, source_target_pairs={{0,2},{1,3},{2,0},{3,1},{4,6},{5,7},{6,4},{7,5},{8,10},{9,11},{10,... | collective-permute-start | bytes 393224 | tf_op jit(solution)/shard_map/ppermute | solution.py:455
  19.6 8.7 %collective-permute-start.8 = (f32[32,8,128]{2,1,0:T(8,128)S(1)}, f32[32,8,128]{2,1,0:T(8,128)S(1)}, u32[]{:S(2)}, u32[]{:S(2)}) collective-permute-start(f32[32,8,128]{2,1,0:T(8,128)S(1)} %get-tuple-element.42), channel_id=1, source_target_pairs={{0,7},{1,6},{2,5},{3,4},{4,3},{5,2},{6,1},{7,0},{8,15},{9,14},{10,... | collective-permute-start | bytes 393224 | tf_op jit(solution)/shard_map/ppermute | solution.py:451
  28.4 9.0 %collective-permute-start.9 = (f32[296,128]{1,0:T(8,128)S(1)}, f32[296,128]{1,0:T(8,128)S(1)}, u32[]{:S(2)}, u32[]{:S(2)}) collective-permute-start(f32[296,128]{1,0:T(8,128)S(1)} %shard_map.81), channel_id=1, source_target_pairs={{0,7},{1,6},{2,5},{3,4},{4,3},{5,2},{6,1},{7,0},{8,15},{9,14},{10,... | collective-permute-start | bytes 454664 | tf_op jit(solution)/shard_map/ppermute | solution.py:479
  32.2 6.2 %collective-permute-start.10 = (f32[4,72,128]{2,1,0:T(8,128)S(1)}, f32[4,72,128]{2,1,0:T(8,128)S(1)}, u32[]{:S(2)}, u32[]{:S(2)}) collective-permute-start(f32[4,72,128]{2,1,0:T(8,128)S(1)} %get-tuple-element.46), channel_id=1, source_target_pairs={{0,1},{1,0},{2,3},{3,2},{4,5},{5,4},{6,7},{7,6},{8,9},{9,8},{10,11... | collective-permute-start | bytes 442376 | tf_op jit(solution)/shard_map/ppermute | solution.py:485
  32.3 6.5 %collective-permute-start.11 = (f32[4,72,128]{2,1,0:T(8,128)S(1)}, f32[4,72,128]{2,1,0:T(8,128)S(1)}, u32[]{:S(2)}, u32[]{:S(2)}) collective-permute-start(f32[4,72,128]{2,1,0:T(8,128)S(1)} %get-tuple-element.47), channel_id=1, source_target_pairs={{1,2},{2,1},{3,4},{4,3},{5,6},{6,5},{9,10},{10,9},{11,12},{12,11},... | collective-permute-start | bytes 442376 | tf_op jit(solution)/shard_map/ppermute | solution.py:485
  38.8 6.7 %collective-permute-start.12 = (f32[320,128]{1,0:T(8,128)S(1)}, f32[320,128]{1,0:T(8,128)S(1)}, u32[]{:S(2)}, u32[]{:S(2)}) collective-permute-start(f32[320,128]{1,0:T(8,128)S(1)} %get-tuple-element.49), channel_id=1, source_target_pairs={{0,8},{8,0},{16,24},{24,16},{1,9},{9,1},{17,25},{25,17},{2,10},{10... | collective-permute-start | bytes 491528 | tf_op jit(solution)/shard_map/ppermute | solution.py:503
  40.4 9.3 %collective-permute-start.13 = (f32[320,128]{1,0:T(8,128)S(1)}, f32[320,128]{1,0:T(8,128)S(1)}, u32[]{:S(2)}, u32[]{:S(2)}) collective-permute-start(f32[320,128]{1,0:T(8,128)S(1)} %get-tuple-element.50), channel_id=1, source_target_pairs={{8,16},{16,8},{9,17},{17,9},{10,18},{18,10},{11,19},{19,11},{12,20... | collective-permute-start | bytes 491528 | tf_op jit(solution)/shard_map/ppermute | solution.py:503

commit v7 on v6

--- a/solution.py
+++ b/solution.py
@@ -414,7 +414,7 @@
         (struct(depth, rows, lanes),) + (struct(chips, 2, rows, wide),) * 2,
         [SMEM, SMEM, VMEM, ORDER],
         [pltpu.VMEM((lanes, wide), F32)],
-    )(quarter_turns, offsets, recorded, first)
+    )(quarter_turns, offsets, recorded, edge)
     mirror = [(i, parts - 1 - i) for i in range(parts)]
     swapped = lax.ppermute(theirs, "gx", [(i, i ^ 1) for i in range(parts)])
     messages = call(merge, (struct(2, 2, rows, wide),) * (chips - 1), [VMEM] * 2)(mine, swapped)

time: 51 us -> 50.5 us (level)
  waiting for transfers between devices: 16.6 us -> 14 us
  starting transfers between devices: 20.1 us -> 21.1 us
  local copies, waits for them, and re-layouts: 2.21 us -> 2.85 us
    ppermute x2, waiting for transfers between devices: 1.86 us -> 0.23 us  [shards(): lax.ppermute(second, 'gx', odd_x)]
    ppermute x1, waiting for transfers between devices: 1.24 us -> 0.01 us  [shards(): lax.ppermute(edge, 'gx', even_x)]
    ppermute x1, starting transfers between devices: 0.07 us -> 1.22 us  [shards(): lax.ppermute(edge, 'gx', even_x)]
    unnamed x18, local copies, waits for them, and re-layouts: 2.21 us -> 2.85 us
    ppermute x2, starting transfers between devices: 5.35 us -> 4.81 us  [shards(): lax.ppermute(fourth, 'gy', odd_y)]
    ppermute x2, starting transfers between devices: 3.15 us -> 3.68 us  [shards(): lax.ppermute(third, 'gy', even_y)]
  transfers between devices with their start and end apart: 14 -> 14, of which waited for: 9 -> 7; matrix products, arithmetic and copies ran while one was open for 0% -> 0% of each run, Pallas kernels for 19% -> 19%
where the time goes in v7:
time: 50.5 us; the launch traced here: 49.8 us
  starting transfers between devices  21.1 us (42%)
  waiting for transfers between devices  14 us (28%)
  Pallas kernels  11.7 us (23%)
  local copies, waits for them, and re-layouts  2.85 us (6%)
    ppermute x2, starting transfers between devices, shards(): lax.ppermute(second, 'gx', odd_x)  5.51 us
    ppermute x3, waiting for transfers between devices, shards(): lax.ppermute(messages[k - 1], 'gx', [(i, i ^ 2 * k) for i in range(parts)])  5.3 us
    ppermute x2, starting transfers between devices, shards(): lax.ppermute(fourth, 'gy', odd_y)  4.81 us
    ppermute x3, starting transfers between devices, shards(): lax.ppermute(messages[k - 1], 'gx', [(i, i ^ 2 * k) for i in range(parts)])  4.75 us
    ppermute x2, waiting for transfers between devices, shards(): lax.ppermute(fourth, 'gy', odd_y)  4.21 us
    ppermute x2, starting transfers between devices, shards(): lax.ppermute(third, 'gy', even_y)  3.68 us
    unnamed x18, local copies, waits for them, and re-layouts  2.85 us
    ppermute x2, waiting for transfers between devices, shards(): lax.ppermute(third, 'gy', even_y)  2.16 us
  transfers between devices with their start and end apart: 14, of which 7 were waited for; matrix products, arithmetic and copies ran while one was open for 0% of the time, Pallas kernels for 19%

profile of v7, /device:TPU:12, one launch (start us, length us, event | category | flops | bytes accessed | tf_op | source)
XLA Modules:
  0.0 49.8 jit_solution(13277334895459886267)
XLA Ops:
  0.0 0.0 copy-start
  0.0 0.9 %copy-done = f32[32,16,128]{2,1,0:T(8,128)S(1)} copy-done((f32[32,16,128]{2,1,0:T(8,128)S(1)}, f32[32,16,128]{2,1,0:T(8,128)}, u32[]{:S(2)}) %copy-start) | copy-done | bytes 262168
  1.0 0.1 shard_map.74
  1.1 0.0 copy-start.6
  1.1 0.0 copy-start.7
  1.1 0.6 %copy-done.6 = s32[4]{0:T(128)S(1)} copy-done((s32[4]{0:T(128)S(1)}, s32[4]{0:T(128)}, u32[]{:S(2)}) %copy-start.6) | copy-done | bytes 40
  1.7 0.0 copy-done.7
  1.7 0.0 copy-start.2
  1.7 1.2 %copy-done.2 = f32[4,32,16,128]{3,2,1,0:T(8,128)S(1)} copy-done((f32[4,32,16,128]{3,2,1,0:T(8,128)S(1)}, f32[4,32,16,128]{3,2,1,0:T(8,128)}, u32[]{:S(2)}) %copy-start.2) | copy-done | bytes 1048600
  3.0 0.0 copy-start.3
  3.0 0.9 %shard_map.76 = (f32[32,16,128]{2,1,0:T(8,128)S(1)}, f32[4,2,16,512]{3,2,1,0:T(8,128)S(1)}, f32[4,2,16,512]{3,2,1,0:T(8,128)S(1)}) custom-call(s32[4]{0:T(128)S(1)} %copy-done.6, s32[4]{0:T(128)S(1)} %copy-done.7, f32[4,32,16,128]{3,2,1,0:T(8,128)S(1)} %copy-done.2, f32[4,32,128]{2,1,0:T(8,128)S(1)} %get-tuple-element.30.later), custom_call_target="tpu_custom_call" | custom-call | flops 1 | bytes 1 | tf_op jit(solution)/shard_map/pallas_call | solution.py:412
  3.9 0.1 collective-permute-start.4
  4.0 2.4 %collective-permute-start.1 = (f32[4,32,128]{2,1,0:T(8,128)S(1)}, f32[4,32,128]{2,1,0:T(8,128)S(1)}, u32[]{:S(2)}, u32[]{:S(2)}) collective-permute-start(f32[4,32,128]{2,1,0:T(8,128)S(1)} %get-tuple-element.31), channel_id=1, source_target_pairs={{1,2},{2,1},{3,4},{4,3},{5,6},{6,5},{9,10},{10,9},{11,12},{12,11},... | collective-permute-start | bytes 196616 | tf_op jit(solution)/shard_map/ppermute | solution.py:411
  6.4 1.2 %collective-permute-start = (f32[4,32,128]{2,1,0:T(8,128)S(1)}, f32[4,32,128]{2,1,0:T(8,128)S(1)}, u32[]{:S(2)}, u32[]{:S(2)}) collective-permute-start(f32[4,32,128]{2,1,0:T(8,128)S(1)} %get-tuple-element.30.later), channel_id=1, source_target_pairs={{0,1},{1,0},{2,3},{3,2},{4,5},{5,4},{6,7},{7,6},{8,9},{9,8},{10,11... | collective-permute-start | bytes 196616 | tf_op jit(solution)/shard_map/ppermute | solution.py:411
  7.7 0.0 collective-permute-done.4.swapped
  7.7 0.0 copy-start.1
  7.7 1.6 %collective-permute-start.5 = (f32[2,2,16,512]{3,2,1,0:T(8,128)S(1)}, f32[2,2,16,512]{3,2,1,0:T(8,128)S(1)}, u32[]{:S(2)}, u32[]{:S(2)}) collective-permute-start(f32[2,2,16,512]{3,2,1,0:T(8,128)S(1)} %get-tuple-element.36), channel_id=1, source_target_pairs={{0,6},{1,7},{2,4},{3,5},{4,2},{5,3},{6,0},{7,1},{8,14},{9,15},{10,... | collective-permute-start | bytes 393224 | tf_op jit(solution)/shard_map/ppermute | solution.py:455
  9.3 0.2 collective-permute-done.1.from_odd.odd_x
  9.6 0.0 collective-permute-done.from_even.even_x
  9.6 0.0 copy-done.1
  9.6 0.3 shard_map.75
  9.8 0.0 copy-start.8
  9.9 1.6 %collective-permute-start.2 = (f32[480,128]{1,0:T(8,128)S(1)}, f32[480,128]{1,0:T(8,128)S(1)}, u32[]{:S(2)}, u32[]{:S(2)}) collective-permute-start(f32[480,128]{1,0:T(8,128)S(1)} %get-tuple-element.32), channel_id=1, source_target_pairs={{0,8},{8,0},{16,24},{24,16},{1,9},{9,1},{17,25},{25,17},{2,10},{10... | collective-permute-start | bytes 737288 | tf_op jit(solution)/shard_map/ppermute | solution.py:453
  11.4 0.0 copy-start.5
  11.4 0.0 copy-start.4
  11.4 2.5 %collective-permute-start.3 = (f32[480,128]{1,0:T(8,128)S(1)}, f32[480,128]{1,0:T(8,128)S(1)}, u32[]{:S(2)}, u32[]{:S(2)}) collective-permute-start(f32[480,128]{1,0:T(8,128)S(1)} %get-tuple-element.33), channel_id=1, source_target_pairs={{8,16},{16,8},{9,17},{17,9},{10,18},{18,10},{11,19},{19,11},{12,20... | collective-permute-start | bytes 737288 | tf_op jit(solution)/shard_map/ppermute | solution.py:453
  13.9 2.7 %collective-permute-start.6 = (f32[2,2,16,512]{3,2,1,0:T(8,128)S(1)}, f32[2,2,16,512]{3,2,1,0:T(8,128)S(1)}, u32[]{:S(2)}, u32[]{:S(2)}) collective-permute-start(f32[2,2,16,512]{3,2,1,0:T(8,128)S(1)} %get-tuple-element.37), channel_id=1, source_target_pairs={{0,4},{1,5},{2,6},{3,7},{4,0},{5,1},{6,2},{7,3},{8,12},{9,13},{10,... | collective-permute-start | bytes 393224 | tf_op jit(solution)/shard_map/ppermute | solution.py:455
  16.6 0.4 collective-permute-start.7
  17.0 0.0 copy-done.8
  17.0 0.0 copy-done.5
  17.0 0.0 copy-done.4
  17.0 1.2 %shard_map.73 = (bf16[128,240]{1,0:T(8,128)(2,1)S(1)}, bf16[4,2,128,128]{3,2,1,0:T(8,128)(2,1)S(1)}, bf16[2,80,128]{2,1,0:T(8,128)(2,1)S(1)}, bf16[4,2,128,128]{3,2,1,0:T(8,128)(2,1)S(1)}, bf16[80,96]{1,0:T(8,128)(2,1)S(1)}) custom-call(s32[4]{0:T(128)S(1)} %copy-done.6, s32[4]{0:T(128)S(1)} %copy-done.7, f32[4,41]{1,0:T(4,128)S(1)} %copy-done.8, ...), custom_call_target="tpu_custom_call" | custom-call | flops 1 | bytes 1 | tf_op jit(solution)/shard_map/pallas_call | solution.py:421
  18.2 0.0 copy-done.3
  18.2 0.6 %shard_map.80 = (f32[32,8,128]{2,1,0:T(8,128)S(1)}, f32[32,8,128]{2,1,0:T(8,128)S(1)}) custom-call(s32[4]{0:T(128)S(1)} %copy-done.6, f32[4,32,16,128]{3,2,1,0:T(8,128)S(1)} %copy-done.3, f32[2,2,16,512]{3,2,1,0:T(8,128)S(1)} %get-tuple-element.38.later, bf16[80,96]{1,0:T(8,128)(2,1)S(1)} %get-tuple-element.40.later_too.half_back), custom_call_target="tpu_custom_call" | custom-call | flops 1 | bytes 1 | tf_op jit(solution)/shard_map/pallas_call | solution.py:432
  18.8 0.0 collective-permute-done.5.rest_0_.rest_2_
  18.8 0.1 collective-permute-start.8
  18.9 2.7 %collective-permute-done.6.rest_1_ = f32[2,2,16,512]{3,2,1,0:T(8,128)S(1)} collective-permute-done((f32[2,2,16,512]{3,2,1,0:T(8,128)S(1)}, f32[2,2,16,512]{3,2,1,0:T(8,128)S(1)}, u32[]{:S(2)}, u32[]{:S(2)}) %collective-permute-start.6) | collective-permute-done | bytes 131104 | tf_op jit(solution)/shard_map/ppermute | solution.py:455
  21.6 2.6 %collective-permute-done.7.rest_2_.rest_0_ = f32[2,2,16,512]{3,2,1,0:T(8,128)S(1)} collective-permute-done((f32[2,2,16,512]{3,2,1,0:T(8,128)S(1)}, f32[2,2,16,512]{3,2,1,0:T(8,128)S(1)}, u32[]{:S(2)}, u32[]{:S(2)}) %collective-permute-start.7) | collective-permute-done | bytes 131104 | tf_op jit(solution)/shard_map/ppermute | solution.py:455
  24.2 0.0 collective-permute-done.2.even_y
  24.2 0.0 collective-permute-done.3.odd_y
  24.2 2.0 %shard_map.79.rest_0_.predicted = f32[4,16,32,128]{3,2,1,0:T(8,128)S(1)} custom-call(s32[4]{0:T(128)S(1)} %copy-done.6, f32[4,9]{1,0:T(4,128)S(1)} %copy-done.4, f32[4,9]{1,0:T(4,128)S(1)} %copy-done.5, bf16[128,240]{1,0:T(8,128)(2,1)S(1)} %get-tuple-element.28.depth_forth, bf16[4,2,128,128]{3,2,1,0:T(8,128)(2,1)S(1)} %get-tuple-element.29.lane_forth, ...), custom_call_target="tpu_custom_call" | custom-call | flops 1 | bytes 1 | tf_op jit(solution)/shard_map/pallas_call | solution.py:468
  26.2 1.4 %collective-permute-done.8.rest_1_.outer = f32[32,8,128]{2,1,0:T(8,128)S(1)} collective-permute-done((f32[32,8,128]{2,1,0:T(8,128)S(1)}, f32[32,8,128]{2,1,0:T(8,128)S(1)}, u32[]{:S(2)}, u32[]{:S(2)}) %collective-permute-start.8) | collective-permute-done | bytes 131104 | tf_op jit(solution)/shard_map/ppermute | solution.py:451
  27.6 0.9 %collective-permute-start.9 = (f32[296,128]{1,0:T(8,128)S(1)}, f32[296,128]{1,0:T(8,128)S(1)}, u32[]{:S(2)}, u32[]{:S(2)}) collective-permute-start(f32[296,128]{1,0:T(8,128)S(1)} %shard_map.81), channel_id=1, source_target_pairs={{0,7},{1,6},{2,5},{3,4},{4,3},{5,2},{6,1},{7,0},{8,15},{9,14},{10,... | collective-permute-start | bytes 454664 | tf_op jit(solution)/shard_map/ppermute | solution.py:479
  28.5 1.5 %shard_map.82.data = f32[2,16,32,128]{3,2,1,0:T(8,128)S(1)} custom-call(f32[4,2,16,512]{3,2,1,0:T(8,128)S(1)} %get-tuple-element.34.mine, f32[4,2,16,512]{3,2,1,0:T(8,128)S(1)} %collective-permute-done.4.swapped, f32[2,2,16,512]{3,2,1,0:T(8,128)S(1)} %collective-permute-done.7.rest_2_.rest_0_, f32[2,2,16,512]{3,2,1,0:T(8,128)S(1)} %collective-permute-done.6.rest_1_, ...), custom_call_target="tpu_custom_call" | custom-call | flops 1 | bytes 1 | tf_op jit(solution)/shard_map/pallas_call | solution.py:461
  29.9 1.3 %shard_map.83 = (f32[4,72,128]{2,1,0:T(8,128)S(1)}, f32[4,72,128]{2,1,0:T(8,128)S(1)}, f32[4,8,32,128]{3,2,1,0:T(8,128)S(1)}) custom-call(s32[4]{0:T(128)S(1)} %copy-done.6, f32[4,9]{1,0:T(4,128)S(1)} %copy-done.4, f32[4,9]{1,0:T(4,128)S(1)} %copy-done.5, f32[4,16,32,128]{3,2,1,0:T(8,128)S(1)} %shard_map.79.rest_0_.predicted, ...), custom_call_target="tpu_custom_call" | custom-call | flops 1 | bytes 1 | tf_op jit(solution)/shard_map/pallas_call | solution.py:480
  31.3 0.1 collective-permute-start.10
  31.4 3.1 %collective-permute-start.11 = (f32[4,72,128]{2,1,0:T(8,128)S(1)}, f32[4,72,128]{2,1,0:T(8,128)S(1)}, u32[]{:S(2)}, u32[]{:S(2)}) collective-permute-start(f32[4,72,128]{2,1,0:T(8,128)S(1)} %get-tuple-element.47), channel_id=1, source_target_pairs={{1,2},{2,1},{3,4},{4,3},{5,6},{6,5},{9,10},{10,9},{11,12},{12,11},... | collective-permute-start | bytes 442376 | tf_op jit(solution)/shard_map/ppermute | solution.py:485
  34.4 1.6 %shard_map.84.partial = f32[16,72,128]{2,1,0:T(8,128)S(1)} custom-call(s32[4]{0:T(128)S(1)} %copy-done.6, f32[4,9]{1,0:T(4,128)S(1)} %copy-done.4, f32[4,9]{1,0:T(4,128)S(1)} %copy-done.5, f32[4,16,32,128]{3,2,1,0:T(8,128)S(1)} %shard_map.79.rest_0_.predicted, bf16[4,2,128,128]{3,2,1,0:T(8,128)(2,1)S(1)} %get-tuple-element.39.lane_back, ...), custom_call_target="tpu_custom_call" | custom-call | flops 1 | bytes 1 | tf_op jit(solution)/shard_map/pallas_call | solution.py:486
  36.0 0.7 %collective-permute-done.9.flat = f32[296,128]{1,0:T(8,128)S(1)} collective-permute-done((f32[296,128]{1,0:T(8,128)S(1)}, f32[296,128]{1,0:T(8,128)S(1)}, u32[]{:S(2)}, u32[]{:S(2)}) %collective-permute-start.9) | collective-permute-done | bytes 151584 | tf_op jit(solution)/shard_map/ppermute | solution.py:479
  36.8 1.1 %shard_map.85.middle = f32[16,72,128]{2,1,0:T(8,128)S(1)} custom-call(s32[4]{0:T(128)S(1)} %copy-done.6, f32[4,9]{1,0:T(4,128)S(1)} %copy-done.4, f32[4,9]{1,0:T(4,128)S(1)} %copy-done.5, f32[4,16,32,128]{3,2,1,0:T(8,128)S(1)} %shard_map.79.rest_0_.predicted, bf16[4,2,128,128]{3,2,1,0:T(8,128)(2,1)S(1)} %get-tuple-element.39.lane_back, ...), custom_call_target="tpu_custom_call" | custom-call | flops 1 | bytes 1 | tf_op jit(solution)/shard_map/pallas_call | solution.py:492
  37.9 0.0 collective-permute-done.10.even_x
  37.9 0.0 collective-permute-done.11.odd_x
  37.9 0.1 shard_map.86
  38.0 2.1 %collective-permute-start.12 = (f32[320,128]{1,0:T(8,128)S(1)}, f32[320,128]{1,0:T(8,128)S(1)}, u32[]{:S(2)}, u32[]{:S(2)}) collective-permute-start(f32[320,128]{1,0:T(8,128)S(1)} %get-tuple-element.49), channel_id=1, source_target_pairs={{0,8},{8,0},{16,24},{24,16},{1,9},{9,1},{17,25},{25,17},{2,10},{10... | collective-permute-start | bytes 491528 | tf_op jit(solution)/shard_map/ppermute | solution.py:503
  40.1 2.3 %collective-permute-start.13 = (f32[320,128]{1,0:T(8,128)S(1)}, f32[320,128]{1,0:T(8,128)S(1)}, u32[]{:S(2)}, u32[]{:S(2)}) collective-permute-start(f32[320,128]{1,0:T(8,128)S(1)} %get-tuple-element.50), channel_id=1, source_target_pairs={{8,16},{16,8},{9,17},{17,9},{10,18},{18,10},{11,19},{19,11},{12,20... | collective-permute-start | bytes 491528 | tf_op jit(solution)/shard_map/ppermute | solution.py:503
  42.4 2.2 %collective-permute-done.12.even_y = f32[320,128]{1,0:T(8,128)S(1)} collective-permute-done((f32[320,128]{1,0:T(8,128)S(1)}, f32[320,128]{1,0:T(8,128)S(1)}, u32[]{:S(2)}, u32[]{:S(2)}) %collective-permute-start.12) | collective-permute-done | bytes 163872 | tf_op jit(solution)/shard_map/ppermute | solution.py:503
  44.6 4.2 %collective-permute-done.13.odd_y = f32[320,128]{1,0:T(8,128)S(1)} collective-permute-done((f32[320,128]{1,0:T(8,128)S(1)}, f32[320,128]{1,0:T(8,128)S(1)}, u32[]{:S(2)}, u32[]{:S(2)}) %collective-permute-start.13) | collective-permute-done | bytes 163872 | tf_op jit(solution)/shard_map/ppermute | solution.py:503
  48.8 1.0 %shard_map.87 = f32[32,16,128]{2,1,0:T(8,128)} custom-call(f32[32,16,128]{2,1,0:T(8,128)S(1)} %copy-done.1, f32[16,32,128]{2,1,0:T(8,128)S(1)} %get-tuple-element.48.own, f32[320,128]{1,0:T(8,128)S(1)} %collective-permute-done.12.even_y, f32[320,128]{1,0:T(8,128)S(1)} %collective-permute-done.13.odd_y), custom_call_target="tpu_custom_call" | custom-call | flops 1 | bytes 1 | tf_op jit(solution)/shard_map/pallas_call | solution.py:504
  (3 shorter events, 0.0 us)
Async XLA Ops:
  0.0 0.9 %copy-start = (f32[32,16,128]{2,1,0:T(8,128)S(1)}, f32[32,16,128]{2,1,0:T(8,128)}, u32[]{:S(2)}) copy-start(f32[32,16,128]{2,1,0:T(8,128)} %estimate.1) | copy-start | bytes 786436
  1.1 0.7 %copy-start.6 = (s32[4]{0:T(128)S(1)}, s32[4]{0:T(128)}, u32[]{:S(2)}) copy-start(s32[4]{0:T(128)} %turns.13) | copy-start | bytes 52
  1.1 0.7 %copy-start.7 = (s32[4]{0:T(128)S(1)}, s32[4]{0:T(128)}, u32[]{:S(2)}) copy-start(s32[4]{0:T(128)} %offsets.3) | copy-start | bytes 52
  1.7 1.2 %copy-start.2 = (f32[4,32,16,128]{3,2,1,0:T(8,128)S(1)}, f32[4,32,16,128]{3,2,1,0:T(8,128)}, u32[]{:S(2)}) copy-start(f32[4,32,16,128]{3,2,1,0:T(8,128)} %recorded.3) | copy-start | bytes 3145732
  3.0 15.2 %copy-start.3 = (f32[4,32,16,128]{3,2,1,0:T(8,128)S(1)}, f32[4,32,16,128]{3,2,1,0:T(8,128)}, u32[]{:S(2)}) copy-start(f32[4,32,16,128]{3,2,1,0:T(8,128)} %recorded.3) | copy-start | bytes 3145732
  3.9 3.8 %collective-permute-start.4 = (f32[4,2,16,512]{3,2,1,0:T(8,128)S(1)}, f32[4,2,16,512]{3,2,1,0:T(8,128)S(1)}, u32[]{:S(2)}, u32[]{:S(2)}) collective-permute-start(f32[4,2,16,512]{3,2,1,0:T(8,128)S(1)} %get-tuple-element.35), channel_id=1, source_target_pairs={{0,1},{1,0},{2,3},{3,2},{4,5},{5,4},{6,7},{7,6},{8,9},{9,8},{10,11... | collective-permute-start | bytes 786440 | tf_op jit(solution)/shard_map/ppermute | solution.py:419
  4.0 5.6 %collective-permute-start.1 = (f32[4,32,128]{2,1,0:T(8,128)S(1)}, f32[4,32,128]{2,1,0:T(8,128)S(1)}, u32[]{:S(2)}, u32[]{:S(2)}) collective-permute-start(f32[4,32,128]{2,1,0:T(8,128)S(1)} %get-tuple-element.31), channel_id=1, source_target_pairs={{1,2},{2,1},{3,4},{4,3},{5,6},{6,5},{9,10},{10,9},{11,12},{12,11},... | collective-permute-start | bytes 196616 | tf_op jit(solution)/shard_map/ppermute | solution.py:411
  6.4 3.1 %collective-permute-start = (f32[4,32,128]{2,1,0:T(8,128)S(1)}, f32[4,32,128]{2,1,0:T(8,128)S(1)}, u32[]{:S(2)}, u32[]{:S(2)}) collective-permute-start(f32[4,32,128]{2,1,0:T(8,128)S(1)} %get-tuple-element.30.later), channel_id=1, source_target_pairs={{0,1},{1,0},{2,3},{3,2},{4,5},{5,4},{6,7},{7,6},{8,9},{9,8},{10,11... | collective-permute-start | bytes 196616 | tf_op jit(solution)/shard_map/ppermute | solution.py:411
  7.7 1.9 %copy-start.1 = (f32[32,16,128]{2,1,0:T(8,128)S(1)}, f32[32,16,128]{2,1,0:T(8,128)}, u32[]{:S(2)}) copy-start(f32[32,16,128]{2,1,0:T(8,128)} %estimate.1) | copy-start | bytes 786436
  7.7 11.1 %collective-permute-start.5 = (f32[2,2,16,512]{3,2,1,0:T(8,128)S(1)}, f32[2,2,16,512]{3,2,1,0:T(8,128)S(1)}, u32[]{:S(2)}, u32[]{:S(2)}) collective-permute-start(f32[2,2,16,512]{3,2,1,0:T(8,128)S(1)} %get-tuple-element.36), channel_id=1, source_target_pairs={{0,6},{1,7},{2,4},{3,5},{4,2},{5,3},{6,0},{7,1},{8,14},{9,15},{10,... | collective-permute-start | bytes 393224 | tf_op jit(solution)/shard_map/ppermute | solution.py:455
  9.8 7.2 %copy-start.8 = (f32[4,41]{1,0:T(4,128)S(1)}, f32[4,41]{1,0:T(4,128)}, u32[]{:S(2)}) copy-start(f32[4,41]{1,0:T(4,128)} %depth_taps.1) | copy-start | bytes 1972
  9.9 14.3 %collective-permute-start.2 = (f32[480,128]{1,0:T(8,128)S(1)}, f32[480,128]{1,0:T(8,128)S(1)}, u32[]{:S(2)}, u32[]{:S(2)}) collective-permute-start(f32[480,128]{1,0:T(8,128)S(1)} %get-tuple-element.32), channel_id=1, source_target_pairs={{0,8},{8,0},{16,24},{24,16},{1,9},{9,1},{17,25},{25,17},{2,10},{10... | collective-permute-start | bytes 737288 | tf_op jit(solution)/shard_map/ppermute | solution.py:453
  11.4 5.6 %copy-start.5 = (f32[4,9]{1,0:T(4,128)S(1)}, f32[4,9]{1,0:T(4,128)}, u32[]{:S(2)}) copy-start(f32[4,9]{1,0:T(4,128)} %column_taps.9) | copy-start | bytes 436
  11.4 5.6 %copy-start.4 = (f32[4,9]{1,0:T(4,128)S(1)}, f32[4,9]{1,0:T(4,128)}, u32[]{:S(2)}) copy-start(f32[4,9]{1,0:T(4,128)} %row_taps.9) | copy-start | bytes 436
  11.4 12.8 %collective-permute-start.3 = (f32[480,128]{1,0:T(8,128)S(1)}, f32[480,128]{1,0:T(8,128)S(1)}, u32[]{:S(2)}, u32[]{:S(2)}) collective-permute-start(f32[480,128]{1,0:T(8,128)S(1)} %get-tuple-element.33), channel_id=1, source_target_pairs={{8,16},{16,8},{9,17},{17,9},{10,18},{18,10},{11,19},{19,11},{12,20... | collective-permute-start | bytes 737288 | tf_op jit(solution)/shard_map/ppermute | solution.py:453
  13.9 7.6 %collective-permute-start.6 = (f32[2,2,16,512]{3,2,1,0:T(8,128)S(1)}, f32[2,2,16,512]{3,2,1,0:T(8,128)S(1)}, u32[]{:S(2)}, u32[]{:S(2)}) collective-permute-start(f32[2,2,16,512]{3,2,1,0:T(8,128)S(1)} %get-tuple-element.37), channel_id=1, source_target_pairs={{0,4},{1,5},{2,6},{3,7},{4,0},{5,1},{6,2},{7,3},{8,12},{9,13},{10,... | collective-permute-start | bytes 393224 | tf_op jit(solution)/shard_map/ppermute | solution.py:455
  16.6 7.6 %collective-permute-start.7 = (f32[2,2,16,512]{3,2,1,0:T(8,128)S(1)}, f32[2,2,16,512]{3,2,1,0:T(8,128)S(1)}, u32[]{:S(2)}, u32[]{:S(2)}) collective-permute-start(f32[2,2,16,512]{3,2,1,0:T(8,128)S(1)} %get-tuple-element.38.later), channel_id=1, source_target_pairs={{0,2},{1,3},{2,0},{3,1},{4,6},{5,7},{6,4},{7,5},{8,10},{9,11},{10,... | collective-permute-start | bytes 393224 | tf_op jit(solution)/shard_map/ppermute | solution.py:455
  18.8 8.7 %collective-permute-start.8 = (f32[32,8,128]{2,1,0:T(8,128)S(1)}, f32[32,8,128]{2,1,0:T(8,128)S(1)}, u32[]{:S(2)}, u32[]{:S(2)}) collective-permute-start(f32[32,8,128]{2,1,0:T(8,128)S(1)} %get-tuple-element.42), channel_id=1, source_target_pairs={{0,7},{1,6},{2,5},{3,4},{4,3},{5,2},{6,1},{7,0},{8,15},{9,14},{10,... | collective-permute-start | bytes 393224 | tf_op jit(solution)/shard_map/ppermute | solution.py:451
  27.6 9.2 %collective-permute-start.9 = (f32[296,128]{1,0:T(8,128)S(1)}, f32[296,128]{1,0:T(8,128)S(1)}, u32[]{:S(2)}, u32[]{:S(2)}) collective-permute-start(f32[296,128]{1,0:T(8,128)S(1)} %shard_map.81), channel_id=1, source_target_pairs={{0,7},{1,6},{2,5},{3,4},{4,3},{5,2},{6,1},{7,0},{8,15},{9,14},{10,... | collective-permute-start | bytes 454664 | tf_op jit(solution)/shard_map/ppermute | solution.py:479
  31.3 6.6 %collective-permute-start.10 = (f32[4,72,128]{2,1,0:T(8,128)S(1)}, f32[4,72,128]{2,1,0:T(8,128)S(1)}, u32[]{:S(2)}, u32[]{:S(2)}) collective-permute-start(f32[4,72,128]{2,1,0:T(8,128)S(1)} %get-tuple-element.46), channel_id=1, source_target_pairs={{0,1},{1,0},{2,3},{3,2},{4,5},{5,4},{6,7},{7,6},{8,9},{9,8},{10,11... | collective-permute-start | bytes 442376 | tf_op jit(solution)/shard_map/ppermute | solution.py:485
  31.4 6.5 %collective-permute-start.11 = (f32[4,72,128]{2,1,0:T(8,128)S(1)}, f32[4,72,128]{2,1,0:T(8,128)S(1)}, u32[]{:S(2)}, u32[]{:S(2)}) collective-permute-start(f32[4,72,128]{2,1,0:T(8,128)S(1)} %get-tuple-element.47), channel_id=1, source_target_pairs={{1,2},{2,1},{3,4},{4,3},{5,6},{6,5},{9,10},{10,9},{11,12},{12,11},... | collective-permute-start | bytes 442376 | tf_op jit(solution)/shard_map/ppermute | solution.py:485
  38.0 6.6 %collective-permute-start.12 = (f32[320,128]{1,0:T(8,128)S(1)}, f32[320,128]{1,0:T(8,128)S(1)}, u32[]{:S(2)}, u32[]{:S(2)}) collective-permute-start(f32[320,128]{1,0:T(8,128)S(1)} %get-tuple-element.49), channel_id=1, source_target_pairs={{0,8},{8,0},{16,24},{24,16},{1,9},{9,1},{17,25},{25,17},{2,10},{10... | collective-permute-start | bytes 491528 | tf_op jit(solution)/shard_map/ppermute | solution.py:503
  40.1 8.7 %collective-permute-start.13 = (f32[320,128]{1,0:T(8,128)S(1)}, f32[320,128]{1,0:T(8,128)S(1)}, u32[]{:S(2)}, u32[]{:S(2)}) collective-permute-start(f32[320,128]{1,0:T(8,128)S(1)} %get-tuple-element.50), channel_id=1, source_target_pairs={{8,16},{16,8},{9,17},{17,9},{10,18},{18,10},{11,19},{19,11},{12,20... | collective-permute-start | bytes 491528 | tf_op jit(solution)/shard_map/ppermute | solution.py:503

commit v8 on v7

--- a/solution.py
+++ b/solution.py
@@ -49,7 +49,7 @@
     return lax.rem(lax.axis_index(axis), 2) == 1
 
 
-def pick(turns, recorded, later, later_too, outer, inner):
+def pick(turns, recorded, later, outer, inner):
     rows = recorded.shape[2]
     half = outer.shape[1] // 2
     outer[:, :half] = recorded[0, :, :half]
@@ -438,7 +438,6 @@
             in_specs=[
                 pl.BlockSpec((1, depth, rows, lanes), lambda i, turns: (view_of(turns, 2), 0, 0, 0)),
                 ORDER,
-                ORDER,
             ],
             out_specs=[
                 pl.BlockSpec((depth, 2 * side, lanes), lambda i, turns: (0, 0, 0)),
@@ -447,7 +446,7 @@
         ),
         compiler_params=PARAMS,
         cost_estimate=COST,
-    )(quarter_turns, recorded, messages[0], half_back)
+    )(quarter_turns, recorded, messages[0])
     outer = lax.ppermute(outer, "gx", mirror)
     third, fourth = call(layers_out, (struct((rows + 2 * side) * reach, lanes),) * 2, [VMEM] * 3)(estimate, first, second)
     third, fourth = lax.ppermute(third, "gy", even_y), lax.ppermute(fourth, "gy", odd_y)
@@ -456,7 +455,7 @@
         for k in range(chips - 1, 0, -1)
     }
 
-    arrivals = list(moved.values())
+    arrivals = [half_back, *moved.values()]
     passed = call(gate, struct(8, LANES), [ORDER] * len(arrivals))(*arrivals)
     data = call(
         turned,

time: 50.5 us -> 50.5 us (level)
  transfers between devices with their start and end apart: 14 -> 14, of which waited for: 7 -> 8; matrix products, arithmetic and copies ran while one was open for 0% -> 0% of each run, Pallas kernels for 19% -> 19%
where the time goes in v8:
time: 50.5 us; the launch traced here: 49.8 us
  starting transfers between devices  21.4 us (42%)
  waiting for transfers between devices  13.7 us (27%)
  Pallas kernels  11.7 us (23%)
  local copies, waits for them, and re-layouts  2.88 us (6%)
    ppermute x2, starting transfers between devices, shards(): lax.ppermute(second, 'gx', odd_x)  5.48 us
    ppermute x3, waiting for transfers between devices, shards(): lax.ppermute(messages[k - 1], 'gx', [(i, i ^ 2 * k) for i in range(parts)])  5.27 us
    ppermute x3, starting transfers between devices, shards(): lax.ppermute(messages[k - 1], 'gx', [(i, i ^ 2 * k) for i in range(parts)])  4.75 us
    ppermute x2, starting transfers between devices, shards(): lax.ppermute(fourth, 'gy', odd_y)  4.5 us
    ppermute x2, waiting for transfers between devices, shards(): lax.ppermute(fourth, 'gy', odd_y)  4.08 us
    ppermute x2, starting transfers between devices, shards(): lax.ppermute(third, 'gy', even_y)  4.02 us
    unnamed x18, local copies, waits for them, and re-layouts  2.88 us
    ppermute x2, waiting for transfers between devices, shards(): lax.ppermute(third, 'gy', even_y)  2.26 us
  transfers between devices with their start and end apart: 14, of which 8 were waited for; matrix products, arithmetic and copies ran while one was open for 0% of the time, Pallas kernels for 19%

profile of v8, /device:TPU:12, one launch (start us, length us, event | category | flops | bytes accessed | tf_op | source)
XLA Modules:
  0.0 49.8 jit_solution(17393898438912228367)
XLA Ops:
  0.0 0.0 copy-start
  0.0 0.9 %copy-done = f32[32,16,128]{2,1,0:T(8,128)S(1)} copy-done((f32[32,16,128]{2,1,0:T(8,128)S(1)}, f32[32,16,128]{2,1,0:T(8,128)}, u32[]{:S(2)}) %copy-start) | copy-done | bytes 262168
  1.0 0.1 shard_map.74
  1.1 0.0 copy-start.6
  1.1 0.0 copy-start.7
  1.1 0.6 %copy-done.6 = s32[4]{0:T(128)S(1)} copy-done((s32[4]{0:T(128)S(1)}, s32[4]{0:T(128)}, u32[]{:S(2)}) %copy-start.6) | copy-done | bytes 40
  1.7 0.0 copy-done.7
  1.7 0.0 copy-start.2
  1.7 1.2 %copy-done.2 = f32[4,32,16,128]{3,2,1,0:T(8,128)S(1)} copy-done((f32[4,32,16,128]{3,2,1,0:T(8,128)S(1)}, f32[4,32,16,128]{3,2,1,0:T(8,128)}, u32[]{:S(2)}) %copy-start.2) | copy-done | bytes 1048600
  3.0 0.0 copy-start.3
  3.0 0.9 %shard_map.76 = (f32[32,16,128]{2,1,0:T(8,128)S(1)}, f32[4,2,16,512]{3,2,1,0:T(8,128)S(1)}, f32[4,2,16,512]{3,2,1,0:T(8,128)S(1)}) custom-call(s32[4]{0:T(128)S(1)} %copy-done.6, s32[4]{0:T(128)S(1)} %copy-done.7, f32[4,32,16,128]{3,2,1,0:T(8,128)S(1)} %copy-done.2, f32[4,32,128]{2,1,0:T(8,128)S(1)} %get-tuple-element.30.later), custom_call_target="tpu_custom_call" | custom-call | flops 1 | bytes 1 | tf_op jit(solution)/shard_map/pallas_call | solution.py:412
  3.9 0.1 collective-permute-start.4
  4.0 2.4 %collective-permute-start.1 = (f32[4,32,128]{2,1,0:T(8,128)S(1)}, f32[4,32,128]{2,1,0:T(8,128)S(1)}, u32[]{:S(2)}, u32[]{:S(2)}) collective-permute-start(f32[4,32,128]{2,1,0:T(8,128)S(1)} %get-tuple-element.31), channel_id=1, source_target_pairs={{1,2},{2,1},{3,4},{4,3},{5,6},{6,5},{9,10},{10,9},{11,12},{12,11},... | collective-permute-start | bytes 196616 | tf_op jit(solution)/shard_map/ppermute | solution.py:411
  6.4 1.2 %collective-permute-start = (f32[4,32,128]{2,1,0:T(8,128)S(1)}, f32[4,32,128]{2,1,0:T(8,128)S(1)}, u32[]{:S(2)}, u32[]{:S(2)}) collective-permute-start(f32[4,32,128]{2,1,0:T(8,128)S(1)} %get-tuple-element.30.later), channel_id=1, source_target_pairs={{0,1},{1,0},{2,3},{3,2},{4,5},{5,4},{6,7},{7,6},{8,9},{9,8},{10,11... | collective-permute-start | bytes 196616 | tf_op jit(solution)/shard_map/ppermute | solution.py:411
  7.7 0.0 collective-permute-done.4.swapped
  7.7 0.0 copy-start.1
  7.7 1.6 %collective-permute-start.5 = (f32[2,2,16,512]{3,2,1,0:T(8,128)S(1)}, f32[2,2,16,512]{3,2,1,0:T(8,128)S(1)}, u32[]{:S(2)}, u32[]{:S(2)}) collective-permute-start(f32[2,2,16,512]{3,2,1,0:T(8,128)S(1)} %get-tuple-element.37), channel_id=1, source_target_pairs={{0,6},{1,7},{2,4},{3,5},{4,2},{5,3},{6,0},{7,1},{8,14},{9,15},{10,... | collective-permute-start | bytes 393224 | tf_op jit(solution)/shard_map/ppermute | solution.py:454
  9.3 0.2 collective-permute-done.1.from_odd.odd_x
  9.6 0.0 collective-permute-done.from_even.even_x
  9.6 0.0 copy-done.1
  9.6 0.3 shard_map.75
  9.8 1.6 %collective-permute-start.2 = (f32[480,128]{1,0:T(8,128)S(1)}, f32[480,128]{1,0:T(8,128)S(1)}, u32[]{:S(2)}, u32[]{:S(2)}) collective-permute-start(f32[480,128]{1,0:T(8,128)S(1)} %get-tuple-element.32), channel_id=1, source_target_pairs={{0,8},{8,0},{16,24},{24,16},{1,9},{9,1},{17,25},{25,17},{2,10},{10... | collective-permute-start | bytes 737288 | tf_op jit(solution)/shard_map/ppermute | solution.py:452
  11.4 2.4 %collective-permute-start.3 = (f32[480,128]{1,0:T(8,128)S(1)}, f32[480,128]{1,0:T(8,128)S(1)}, u32[]{:S(2)}, u32[]{:S(2)}) collective-permute-start(f32[480,128]{1,0:T(8,128)S(1)} %get-tuple-element.33), channel_id=1, source_target_pairs={{8,16},{16,8},{9,17},{17,9},{10,18},{18,10},{11,19},{19,11},{12,20... | collective-permute-start | bytes 737288 | tf_op jit(solution)/shard_map/ppermute | solution.py:452
  13.8 2.7 %collective-permute-start.6 = (f32[2,2,16,512]{3,2,1,0:T(8,128)S(1)}, f32[2,2,16,512]{3,2,1,0:T(8,128)S(1)}, u32[]{:S(2)}, u32[]{:S(2)}) collective-permute-start(f32[2,2,16,512]{3,2,1,0:T(8,128)S(1)} %get-tuple-element.38), channel_id=1, source_target_pairs={{0,4},{1,5},{2,6},{3,7},{4,0},{5,1},{6,2},{7,3},{8,12},{9,13},{10,... | collective-permute-start | bytes 393224 | tf_op jit(solution)/shard_map/ppermute | solution.py:454
  16.4 0.4 collective-permute-start.7
  16.9 0.0 copy-done.3
  16.9 0.0 copy-start.4
  16.9 0.0 copy-start.5
  16.9 0.0 copy-start.8
  16.9 0.6 %shard_map.80 = (f32[32,8,128]{2,1,0:T(8,128)S(1)}, f32[32,8,128]{2,1,0:T(8,128)S(1)}) custom-call(s32[4]{0:T(128)S(1)} %copy-done.6, f32[4,32,16,128]{3,2,1,0:T(8,128)S(1)} %copy-done.3, f32[2,2,16,512]{3,2,1,0:T(8,128)S(1)} %get-tuple-element.39.later), custom_call_target="tpu_custom_call" | custom-call | flops 1 | bytes 1 | tf_op jit(solution)/shard_map/pallas_call | solution.py:432
  17.5 0.0 collective-permute-done.5.rest_1_.rest_2_
  17.5 0.1 collective-permute-start.8
  17.6 0.0 copy-done.4
  17.6 0.0 copy-done.5
  17.6 0.0 copy-done.8
  17.6 1.2 %shard_map.73 = (bf16[128,240]{1,0:T(8,128)(2,1)S(1)}, bf16[4,2,128,128]{3,2,1,0:T(8,128)(2,1)S(1)}, bf16[2,80,128]{2,1,0:T(8,128)(2,1)S(1)}, bf16[4,2,128,128]{3,2,1,0:T(8,128)(2,1)S(1)}, bf16[80,96]{1,0:T(8,128)(2,1)S(1)}) custom-call(s32[4]{0:T(128)S(1)} %copy-done.6, s32[4]{0:T(128)S(1)} %copy-done.7, f32[4,41]{1,0:T(4,128)S(1)} %copy-done.8, ...), custom_call_target="tpu_custom_call" | custom-call | flops 1 | bytes 1 | tf_op jit(solution)/shard_map/pallas_call | solution.py:421
  18.8 3.5 %collective-permute-done.6.rest_2_.rest_1_ = f32[2,2,16,512]{3,2,1,0:T(8,128)S(1)} collective-permute-done((f32[2,2,16,512]{3,2,1,0:T(8,128)S(1)}, f32[2,2,16,512]{3,2,1,0:T(8,128)S(1)}, u32[]{:S(2)}, u32[]{:S(2)}) %collective-permute-start.6) | collective-permute-done | bytes 131104 | tf_op jit(solution)/shard_map/ppermute | solution.py:454
  22.2 1.8 %collective-permute-done.7.rest_3_.rest_0_ = f32[2,2,16,512]{3,2,1,0:T(8,128)S(1)} collective-permute-done((f32[2,2,16,512]{3,2,1,0:T(8,128)S(1)}, f32[2,2,16,512]{3,2,1,0:T(8,128)S(1)}, u32[]{:S(2)}, u32[]{:S(2)}) %collective-permute-start.7) | collective-permute-done | bytes 131104 | tf_op jit(solution)/shard_map/ppermute | solution.py:454
  24.0 0.0 collective-permute-done.2.even_y
  24.0 0.0 collective-permute-done.3.odd_y
  24.0 2.0 %shard_map.79.rest_0_.predicted = f32[4,16,32,128]{3,2,1,0:T(8,128)S(1)} custom-call(s32[4]{0:T(128)S(1)} %copy-done.6, f32[4,9]{1,0:T(4,128)S(1)} %copy-done.4, f32[4,9]{1,0:T(4,128)S(1)} %copy-done.5, bf16[128,240]{1,0:T(8,128)(2,1)S(1)} %get-tuple-element.28.depth_forth, bf16[4,2,128,128]{3,2,1,0:T(8,128)(2,1)S(1)} %get-tuple-element.29.lane_forth, ...), custom_call_target="tpu_custom_call" | custom-call | flops 1 | bytes 1 | tf_op jit(solution)/shard_map/pallas_call | solution.py:467
  26.0 1.1 %collective-permute-done.8.rest_1_.outer = f32[32,8,128]{2,1,0:T(8,128)S(1)} collective-permute-done((f32[32,8,128]{2,1,0:T(8,128)S(1)}, f32[32,8,128]{2,1,0:T(8,128)S(1)}, u32[]{:S(2)}, u32[]{:S(2)}) %collective-permute-start.8) | collective-permute-done | bytes 131104 | tf_op jit(solution)/shard_map/ppermute | solution.py:450
  27.1 1.2 %collective-permute-start.9 = (f32[296,128]{1,0:T(8,128)S(1)}, f32[296,128]{1,0:T(8,128)S(1)}, u32[]{:S(2)}, u32[]{:S(2)}) collective-permute-start(f32[296,128]{1,0:T(8,128)S(1)} %shard_map.81), channel_id=1, source_target_pairs={{0,7},{1,6},{2,5},{3,4},{4,3},{5,2},{6,1},{7,0},{8,15},{9,14},{10,... | collective-permute-start | bytes 454664 | tf_op jit(solution)/shard_map/ppermute | solution.py:478
  28.3 1.5 %shard_map.82.data = f32[2,16,32,128]{3,2,1,0:T(8,128)S(1)} custom-call(f32[4,2,16,512]{3,2,1,0:T(8,128)S(1)} %get-tuple-element.35.mine, f32[4,2,16,512]{3,2,1,0:T(8,128)S(1)} %collective-permute-done.4.swapped, f32[2,2,16,512]{3,2,1,0:T(8,128)S(1)} %collective-permute-done.7.rest_3_.rest_0_, f32[2,2,16,512]{3,2,1,0:T(8,128)S(1)} %collective-permute-done.6.rest_2_.rest_1_, ...), custom_call_target="tpu_custom_call" | custom-call | flops 1 | bytes 1 | tf_op jit(solution)/shard_map/pallas_call | solution.py:460
  29.8 1.3 %shard_map.83 = (f32[4,72,128]{2,1,0:T(8,128)S(1)}, f32[4,72,128]{2,1,0:T(8,128)S(1)}, f32[4,8,32,128]{3,2,1,0:T(8,128)S(1)}) custom-call(s32[4]{0:T(128)S(1)} %copy-done.6, f32[4,9]{1,0:T(4,128)S(1)} %copy-done.4, f32[4,9]{1,0:T(4,128)S(1)} %copy-done.5, f32[4,16,32,128]{3,2,1,0:T(8,128)S(1)} %shard_map.79.rest_0_.predicted, ...), custom_call_target="tpu_custom_call" | custom-call | flops 1 | bytes 1 | tf_op jit(solution)/shard_map/pallas_call | solution.py:479
  31.2 0.1 collective-permute-start.10
  31.2 3.0 %collective-permute-start.11 = (f32[4,72,128]{2,1,0:T(8,128)S(1)}, f32[4,72,128]{2,1,0:T(8,128)S(1)}, u32[]{:S(2)}, u32[]{:S(2)}) collective-permute-start(f32[4,72,128]{2,1,0:T(8,128)S(1)} %get-tuple-element.47), channel_id=1, source_target_pairs={{1,2},{2,1},{3,4},{4,3},{5,6},{6,5},{9,10},{10,9},{11,12},{12,11},... | collective-permute-start | bytes 442376 | tf_op jit(solution)/shard_map/ppermute | solution.py:484
  34.3 1.6 %shard_map.84.partial = f32[16,72,128]{2,1,0:T(8,128)S(1)} custom-call(s32[4]{0:T(128)S(1)} %copy-done.6, f32[4,9]{1,0:T(4,128)S(1)} %copy-done.4, f32[4,9]{1,0:T(4,128)S(1)} %copy-done.5, f32[4,16,32,128]{3,2,1,0:T(8,128)S(1)} %shard_map.79.rest_0_.predicted, bf16[4,2,128,128]{3,2,1,0:T(8,128)(2,1)S(1)} %get-tuple-element.40.lane_back, ...), custom_call_target="tpu_custom_call" | custom-call | flops 1 | bytes 1 | tf_op jit(solution)/shard_map/pallas_call | solution.py:485
  35.9 0.6 %collective-permute-done.9.flat = f32[296,128]{1,0:T(8,128)S(1)} collective-permute-done((f32[296,128]{1,0:T(8,128)S(1)}, f32[296,128]{1,0:T(8,128)S(1)}, u32[]{:S(2)}, u32[]{:S(2)}) %collective-permute-start.9) | collective-permute-done | bytes 151584 | tf_op jit(solution)/shard_map/ppermute | solution.py:478
  36.5 1.1 %shard_map.85.middle = f32[16,72,128]{2,1,0:T(8,128)S(1)} custom-call(s32[4]{0:T(128)S(1)} %copy-done.6, f32[4,9]{1,0:T(4,128)S(1)} %copy-done.4, f32[4,9]{1,0:T(4,128)S(1)} %copy-done.5, f32[4,16,32,128]{3,2,1,0:T(8,128)S(1)} %shard_map.79.rest_0_.predicted, bf16[4,2,128,128]{3,2,1,0:T(8,128)(2,1)S(1)} %get-tuple-element.40.lane_back, ...), custom_call_target="tpu_custom_call" | custom-call | flops 1 | bytes 1 | tf_op jit(solution)/shard_map/pallas_call | solution.py:491
  37.6 0.0 collective-permute-done.10.even_x
  37.6 0.1 collective-permute-done.11.odd_x
  37.7 0.1 shard_map.86
  37.8 2.5 %collective-permute-start.12 = (f32[320,128]{1,0:T(8,128)S(1)}, f32[320,128]{1,0:T(8,128)S(1)}, u32[]{:S(2)}, u32[]{:S(2)}) collective-permute-start(f32[320,128]{1,0:T(8,128)S(1)} %get-tuple-element.49), channel_id=1, source_target_pairs={{0,8},{8,0},{16,24},{24,16},{1,9},{9,1},{17,25},{25,17},{2,10},{10... | collective-permute-start | bytes 491528 | tf_op jit(solution)/shard_map/ppermute | solution.py:502
  40.3 2.1 %collective-permute-start.13 = (f32[320,128]{1,0:T(8,128)S(1)}, f32[320,128]{1,0:T(8,128)S(1)}, u32[]{:S(2)}, u32[]{:S(2)}) collective-permute-start(f32[320,128]{1,0:T(8,128)S(1)} %get-tuple-element.50), channel_id=1, source_target_pairs={{8,16},{16,8},{9,17},{17,9},{10,18},{18,10},{11,19},{19,11},{12,20... | collective-permute-start | bytes 491528 | tf_op jit(solution)/shard_map/ppermute | solution.py:502
  42.4 2.3 %collective-permute-done.12.even_y = f32[320,128]{1,0:T(8,128)S(1)} collective-permute-done((f32[320,128]{1,0:T(8,128)S(1)}, f32[320,128]{1,0:T(8,128)S(1)}, u32[]{:S(2)}, u32[]{:S(2)}) %collective-permute-start.12) | collective-permute-done | bytes 163872 | tf_op jit(solution)/shard_map/ppermute | solution.py:502
  44.6 4.1 %collective-permute-done.13.odd_y = f32[320,128]{1,0:T(8,128)S(1)} collective-permute-done((f32[320,128]{1,0:T(8,128)S(1)}, f32[320,128]{1,0:T(8,128)S(1)}, u32[]{:S(2)}, u32[]{:S(2)}) %collective-permute-start.13) | collective-permute-done | bytes 163872 | tf_op jit(solution)/shard_map/ppermute | solution.py:502
  48.7 1.0 %shard_map.87 = f32[32,16,128]{2,1,0:T(8,128)} custom-call(f32[32,16,128]{2,1,0:T(8,128)S(1)} %copy-done.1, f32[16,32,128]{2,1,0:T(8,128)S(1)} %get-tuple-element.48.own, f32[320,128]{1,0:T(8,128)S(1)} %collective-permute-done.12.even_y, f32[320,128]{1,0:T(8,128)S(1)} %collective-permute-done.13.odd_y), custom_call_target="tpu_custom_call" | custom-call | flops 1 | bytes 1 | tf_op jit(solution)/shard_map/pallas_call | solution.py:503
  (3 shorter events, 0.0 us)
Async XLA Ops:
  0.0 0.9 %copy-start = (f32[32,16,128]{2,1,0:T(8,128)S(1)}, f32[32,16,128]{2,1,0:T(8,128)}, u32[]{:S(2)}) copy-start(f32[32,16,128]{2,1,0:T(8,128)} %estimate.1) | copy-start | bytes 786436
  1.1 0.7 %copy-start.6 = (s32[4]{0:T(128)S(1)}, s32[4]{0:T(128)}, u32[]{:S(2)}) copy-start(s32[4]{0:T(128)} %turns.13) | copy-start | bytes 52
  1.1 0.7 %copy-start.7 = (s32[4]{0:T(128)S(1)}, s32[4]{0:T(128)}, u32[]{:S(2)}) copy-start(s32[4]{0:T(128)} %offsets.3) | copy-start | bytes 52
  1.7 1.2 %copy-start.2 = (f32[4,32,16,128]{3,2,1,0:T(8,128)S(1)}, f32[4,32,16,128]{3,2,1,0:T(8,128)}, u32[]{:S(2)}) copy-start(f32[4,32,16,128]{3,2,1,0:T(8,128)} %recorded.3) | copy-start | bytes 3145732
  3.0 13.9 %copy-start.3 = (f32[4,32,16,128]{3,2,1,0:T(8,128)S(1)}, f32[4,32,16,128]{3,2,1,0:T(8,128)}, u32[]{:S(2)}) copy-start(f32[4,32,16,128]{3,2,1,0:T(8,128)} %recorded.3) | copy-start | bytes 3145732
  3.9 3.8 %collective-permute-start.4 = (f32[4,2,16,512]{3,2,1,0:T(8,128)S(1)}, f32[4,2,16,512]{3,2,1,0:T(8,128)S(1)}, u32[]{:S(2)}, u32[]{:S(2)}) collective-permute-start(f32[4,2,16,512]{3,2,1,0:T(8,128)S(1)} %get-tuple-element.36), channel_id=1, source_target_pairs={{0,1},{1,0},{2,3},{3,2},{4,5},{5,4},{6,7},{7,6},{8,9},{9,8},{10,11... | collective-permute-start | bytes 786440 | tf_op jit(solution)/shard_map/ppermute | solution.py:419
  4.0 5.6 %collective-permute-start.1 = (f32[4,32,128]{2,1,0:T(8,128)S(1)}, f32[4,32,128]{2,1,0:T(8,128)S(1)}, u32[]{:S(2)}, u32[]{:S(2)}) collective-permute-start(f32[4,32,128]{2,1,0:T(8,128)S(1)} %get-tuple-element.31), channel_id=1, source_target_pairs={{1,2},{2,1},{3,4},{4,3},{5,6},{6,5},{9,10},{10,9},{11,12},{12,11},... | collective-permute-start | bytes 196616 | tf_op jit(solution)/shard_map/ppermute | solution.py:411
  6.4 3.1 %collective-permute-start = (f32[4,32,128]{2,1,0:T(8,128)S(1)}, f32[4,32,128]{2,1,0:T(8,128)S(1)}, u32[]{:S(2)}, u32[]{:S(2)}) collective-permute-start(f32[4,32,128]{2,1,0:T(8,128)S(1)} %get-tuple-element.30.later), channel_id=1, source_target_pairs={{0,1},{1,0},{2,3},{3,2},{4,5},{5,4},{6,7},{7,6},{8,9},{9,8},{10,11... | collective-permute-start | bytes 196616 | tf_op jit(solution)/shard_map/ppermute | solution.py:411
  7.7 1.9 %copy-start.1 = (f32[32,16,128]{2,1,0:T(8,128)S(1)}, f32[32,16,128]{2,1,0:T(8,128)}, u32[]{:S(2)}) copy-start(f32[32,16,128]{2,1,0:T(8,128)} %estimate.1) | copy-start | bytes 786436
  7.7 9.8 %collective-permute-start.5 = (f32[2,2,16,512]{3,2,1,0:T(8,128)S(1)}, f32[2,2,16,512]{3,2,1,0:T(8,128)S(1)}, u32[]{:S(2)}, u32[]{:S(2)}) collective-permute-start(f32[2,2,16,512]{3,2,1,0:T(8,128)S(1)} %get-tuple-element.37), channel_id=1, source_target_pairs={{0,6},{1,7},{2,4},{3,5},{4,2},{5,3},{6,0},{7,1},{8,14},{9,15},{10,... | collective-permute-start | bytes 393224 | tf_op jit(solution)/shard_map/ppermute | solution.py:454
  9.8 14.2 %collective-permute-start.2 = (f32[480,128]{1,0:T(8,128)S(1)}, f32[480,128]{1,0:T(8,128)S(1)}, u32[]{:S(2)}, u32[]{:S(2)}) collective-permute-start(f32[480,128]{1,0:T(8,128)S(1)} %get-tuple-element.32), channel_id=1, source_target_pairs={{0,8},{8,0},{16,24},{24,16},{1,9},{9,1},{17,25},{25,17},{2,10},{10... | collective-permute-start | bytes 737288 | tf_op jit(solution)/shard_map/ppermute | solution.py:452
  11.4 12.6 %collective-permute-start.3 = (f32[480,128]{1,0:T(8,128)S(1)}, f32[480,128]{1,0:T(8,128)S(1)}, u32[]{:S(2)}, u32[]{:S(2)}) collective-permute-start(f32[480,128]{1,0:T(8,128)S(1)} %get-tuple-element.33), channel_id=1, source_target_pairs={{8,16},{16,8},{9,17},{17,9},{10,18},{18,10},{11,19},{19,11},{12,20... | collective-permute-start | bytes 737288 | tf_op jit(solution)/shard_map/ppermute | solution.py:452
  13.8 8.5 %collective-permute-start.6 = (f32[2,2,16,512]{3,2,1,0:T(8,128)S(1)}, f32[2,2,16,512]{3,2,1,0:T(8,128)S(1)}, u32[]{:S(2)}, u32[]{:S(2)}) collective-permute-start(f32[2,2,16,512]{3,2,1,0:T(8,128)S(1)} %get-tuple-element.38), channel_id=1, source_target_pairs={{0,4},{1,5},{2,6},{3,7},{4,0},{5,1},{6,2},{7,3},{8,12},{9,13},{10,... | collective-permute-start | bytes 393224 | tf_op jit(solution)/shard_map/ppermute | solution.py:454
  16.4 7.6 %collective-permute-start.7 = (f32[2,2,16,512]{3,2,1,0:T(8,128)S(1)}, f32[2,2,16,512]{3,2,1,0:T(8,128)S(1)}, u32[]{:S(2)}, u32[]{:S(2)}) collective-permute-start(f32[2,2,16,512]{3,2,1,0:T(8,128)S(1)} %get-tuple-element.39.later), channel_id=1, source_target_pairs={{0,2},{1,3},{2,0},{3,1},{4,6},{5,7},{6,4},{7,5},{8,10},{9,11},{10,... | collective-permute-start | bytes 393224 | tf_op jit(solution)/shard_map/ppermute | solution.py:454
  16.9 0.7 %copy-start.4 = (f32[4,9]{1,0:T(4,128)S(1)}, f32[4,9]{1,0:T(4,128)}, u32[]{:S(2)}) copy-start(f32[4,9]{1,0:T(4,128)} %row_taps.9) | copy-start | bytes 436
  16.9 0.7 %copy-start.5 = (f32[4,9]{1,0:T(4,128)S(1)}, f32[4,9]{1,0:T(4,128)}, u32[]{:S(2)}) copy-start(f32[4,9]{1,0:T(4,128)} %column_taps.9) | copy-start | bytes 436
  16.9 0.7 %copy-start.8 = (f32[4,41]{1,0:T(4,128)S(1)}, f32[4,41]{1,0:T(4,128)}, u32[]{:S(2)}) copy-start(f32[4,41]{1,0:T(4,128)} %depth_taps.1) | copy-start | bytes 1972
  17.5 9.6 %collective-permute-start.8 = (f32[32,8,128]{2,1,0:T(8,128)S(1)}, f32[32,8,128]{2,1,0:T(8,128)S(1)}, u32[]{:S(2)}, u32[]{:S(2)}) collective-permute-start(f32[32,8,128]{2,1,0:T(8,128)S(1)} %get-tuple-element.42), channel_id=1, source_target_pairs={{0,7},{1,6},{2,5},{3,4},{4,3},{5,2},{6,1},{7,0},{8,15},{9,14},{10,... | collective-permute-start | bytes 393224 | tf_op jit(solution)/shard_map/ppermute | solution.py:450
  27.1 9.3 %collective-permute-start.9 = (f32[296,128]{1,0:T(8,128)S(1)}, f32[296,128]{1,0:T(8,128)S(1)}, u32[]{:S(2)}, u32[]{:S(2)}) collective-permute-start(f32[296,128]{1,0:T(8,128)S(1)} %shard_map.81), channel_id=1, source_target_pairs={{0,7},{1,6},{2,5},{3,4},{4,3},{5,2},{6,1},{7,0},{8,15},{9,14},{10,... | collective-permute-start | bytes 454664 | tf_op jit(solution)/shard_map/ppermute | solution.py:478
  31.2 6.4 %collective-permute-start.10 = (f32[4,72,128]{2,1,0:T(8,128)S(1)}, f32[4,72,128]{2,1,0:T(8,128)S(1)}, u32[]{:S(2)}, u32[]{:S(2)}) collective-permute-start(f32[4,72,128]{2,1,0:T(8,128)S(1)} %get-tuple-element.46), channel_id=1, source_target_pairs={{0,1},{1,0},{2,3},{3,2},{4,5},{5,4},{6,7},{7,6},{8,9},{9,8},{10,11... | collective-permute-start | bytes 442376 | tf_op jit(solution)/shard_map/ppermute | solution.py:484
  31.2 6.5 %collective-permute-start.11 = (f32[4,72,128]{2,1,0:T(8,128)S(1)}, f32[4,72,128]{2,1,0:T(8,128)S(1)}, u32[]{:S(2)}, u32[]{:S(2)}) collective-permute-start(f32[4,72,128]{2,1,0:T(8,128)S(1)} %get-tuple-element.47), channel_id=1, source_target_pairs={{1,2},{2,1},{3,4},{4,3},{5,6},{6,5},{9,10},{10,9},{11,12},{12,11},... | collective-permute-start | bytes 442376 | tf_op jit(solution)/shard_map/ppermute | solution.py:484
  37.8 6.9 %collective-permute-start.12 = (f32[320,128]{1,0:T(8,128)S(1)}, f32[320,128]{1,0:T(8,128)S(1)}, u32[]{:S(2)}, u32[]{:S(2)}) collective-permute-start(f32[320,128]{1,0:T(8,128)S(1)} %get-tuple-element.49), channel_id=1, source_target_pairs={{0,8},{8,0},{16,24},{24,16},{1,9},{9,1},{17,25},{25,17},{2,10},{10... | collective-permute-start | bytes 491528 | tf_op jit(solution)/shard_map/ppermute | solution.py:502
  40.3 8.5 %collective-permute-start.13 = (f32[320,128]{1,0:T(8,128)S(1)}, f32[320,128]{1,0:T(8,128)S(1)}, u32[]{:S(2)}, u32[]{:S(2)}) collective-permute-start(f32[320,128]{1,0:T(8,128)S(1)} %get-tuple-element.50), channel_id=1, source_target_pairs={{8,16},{16,8},{9,17},{17,9},{10,18},{18,10},{11,19},{19,11},{12,20... | collective-permute-start | bytes 491528 | tf_op jit(solution)/shard_map/ppermute | solution.py:502
